TPU v7x, 512 devices: a whole 4x8x8 slice. The times are simulated.
512 devices in a mesh: row: 32 (over y_lo, z, core), col: 16 (over y_hi, x).
Axes of the slice: x: 4, y: 8 (y_hi: 4, y_lo: 2; y = y_hi * 2 + y_lo), z: 8, core: 2. Of those that a mesh axis runs over, the one named last changes fastest.
Arguments:
- a_tiles: bfloat16 [32, 16, 2, 16, 128, 128], P('row', 'col'), may hold values from 0 to 0.25
- a_index: int32 [32, 16, 2, 16], P('row', 'col'), may hold values from 0 to 127, as said below
- a_count: int32 [32, 16, 2], P('row', 'col'), may hold values from 1 to 16
- b_tiles: bfloat16 [32, 16, 16, 128, 128], P('row', 'col'), may hold values from 0 to 0.25
- b_index: int32 [32, 16, 16], P('row', 'col'), may hold values from 0 to 127, as said below
- b_count: int32 [32, 16], P('row', 'col'), may hold values from 1 to 16
- c_partial: float32 [16384, 8192], P('row', 'col'), may hold values from 0.25 to 60, as said below
- prune_mask: int32 [128, 64], P('row', 'col'), may hold values from 0 to 1, as said below
Outputs:
- renormed: float32 [16384, 8192], P('row', 'col')
Inputs may be any that keep to these rules, and one draw needn't show every extreme that they name: `a_index`: within one device and section the slots are distinct. `b_index`: within one device the slots are distinct. `prune_mask`: every block column keeps at least one tile. `c_partial`: positive entries.
All inputs are finite; a program needn't handle non-finite values.
Results may differ from a plain program's by a relative error of at most 0.0003.
Values may be sent and summed in bfloat16 or wider, within the bound.
No kernel may reach another device: no remote copies, remote signals or barrier semaphores. Data moves between devices by JAX's collectives and lax.ppermute only.
A program may use at most 64 MiB of HBM per device.

v0:
```python
import jax
import jax.numpy as jnp
from jax import lax
from jax.sharding import PartitionSpec as P

MB = 4
NB = 4
W = 32
KA = 16
KB = 16
SECTIONS = 2


def spread(array, axis, root):
    mine = lax.axis_index(axis) == root
    return lax.psum(jnp.where(mine, array, jnp.zeros_like(array)), axis)


def place_tiles(tiles, slots, count_slots):
    onehot = (slots[:, None] == jnp.arange(count_slots)[None, :]).astype(jnp.bfloat16)
    dense = jnp.einsum("ap,auv->puv", onehot, tiles, preferred_element_type=jnp.float32)
    return dense.astype(jnp.bfloat16)


def section_product(left_tiles, left_slots, right_tiles, right_slots):
    tile = left_tiles.shape[-1]
    left_dense = place_tiles(left_tiles, left_slots, MB * W)
    left_panel = (
        left_dense.reshape(MB, W, tile, tile).transpose(0, 2, 1, 3).reshape(MB * tile, W * tile)
    )
    right_dense = place_tiles(right_tiles, right_slots, W * NB)
    right_panel = (
        right_dense.reshape(W, NB, tile, tile).transpose(0, 2, 1, 3).reshape(W * tile, NB * tile)
    )
    return jnp.dot(left_panel, right_panel, preferred_element_type=jnp.float32)


def local(a_tiles, a_index, a_count, b_tiles, b_index, b_count, c_partial, prune_mask):
    n_row = lax.axis_size("row")
    n_col = lax.axis_size("col")
    left_all = a_tiles[0, 0]
    left_slots = jnp.where(jnp.arange(KA)[None, :] < a_count[0, 0][:, None], a_index[0, 0], -1)
    right_slots = jnp.where(jnp.arange(KB) < b_count[0, 0], b_index[0, 0], -1)
    expanded = c_partial
    for section in range(SECTIONS):
        section_tiles, section_slots = (
            spread(left_all[section], "col", n_col - 1),
            spread(left_slots[section], "col", n_col - 1),
        )
        got_tiles, got_slots = (
            spread(b_tiles[0, 0], "row", n_row - 2 + section),
            spread(right_slots, "row", n_row - 2 + section),
        )
        expanded = expanded + section_product(section_tiles, section_slots, got_tiles, got_slots)
    tile = a_tiles.shape[-1]
    keep = prune_mask.astype(jnp.float32)[:, None, :, None]
    kept = (expanded * expanded).reshape(MB, tile, NB, tile) * keep
    partial_value = jnp.sum(kept, axis=(0, 1)).reshape(NB * tile)
    colsum = lax.psum(partial_value, "row")
    total_rows = n_row * MB * tile
    return kept.reshape(MB * tile, NB * tile) * (total_rows / colsum)[None, :]


def solution(mesh):
    return jax.shard_map(
        local,
        mesh=mesh,
        in_specs=(
            P("row", "col", None, None, None, None),
            P("row", "col", None, None),
            P("row", "col", None),
            P("row", "col", None, None, None),
            P("row", "col", None),
            P("row", "col"),
            P("row", "col"),
            P("row", "col"),
        ),
        out_specs=P("row", "col"),
        check_vma=False,
    )
```

profile of v0, /device:TPU:1, one launch (start us, length us, event | category | flops | bytes accessed | tf_op | source)
XLA Modules:
  0.0 510.8 jit_solution(7766593265371876647)
XLA Ops:
  6.5 0.0 all-reduce.7.cloned.1.call-start
  6.6 2.4 select_bitcast_fusion.1
  9.0 0.0 all-reduce.7.cloned.1.call-update
  9.0 0.0 all-reduce.9.cloned.1.call-start
  9.0 1.3 fusion.46
  10.3 1.6 fusion.30
  11.9 0.0 all-reduce.9.cloned.1.call-update
  12.6 0.0 copy-done.5
  12.6 0.0 copy-done.8
  12.6 20.5 %all-reduce = (s32[16]{0:T(128)S(1)}, s32[16]{0:T(128)S(1)}) all-reduce(s32[16]{0:T(128)S(1)} %get-tuple-element.20, s32[16]{0:T(128)S(1)} %get-tuple-element.19), channel_id=1, replica_groups=mesh['row'=32,'col'=16] {'row'}, use_global_device_ids=true, to_apply=%region_6.7 | all-reduce | flops 32 | bytes 256 | tf_op jit(solution)/shard_map/psum | solution.py:16
  33.1 0.0 copy-done.7
  33.1 0.0 copy-done.6
  33.2 0.1 compare_select_fusion.1
  33.2 14.8 %all-reduce.1 = (s32[16]{0:T(128)S(1)}, s32[16]{0:T(128)S(1)}) all-reduce(s32[16]{0:T(128)S(1)} %get-tuple-element.18, s32[16]{0:T(128)S(1)} %get-tuple-element.17), channel_id=1, replica_groups=mesh['row'=32,'col'=16] {'col'}, use_global_device_ids=true, to_apply=%region_4.5 | all-reduce | flops 32 | bytes 256 | tf_op jit(solution)/shard_map/psum | solution.py:16
  48.1 198.4 %all-reduce.7.cloned.1.call-done = (bf16[16,128,128]{2,0,1:T(8,128)(2,1)}, bf16[16,128,128]{2,0,1:T(8,128)(2,1)}) async-done(((bf16[16,128,128]{2,0,1:T(8,128)(2,1)}, bf16[16,128,128]{2,0,1:T(8,128)(2,1)}), (bf16[16,128,128]{2,0,1:T(8,128)(2,1)}, bf16[16,128,128]{2,0,1:T(8,128)(2,1)})) %all-reduce.7.cloned.1.call-update) | async-done | bytes 1048592 | tf_op jit(solution)/shard_map/psum | solution.py:16
  246.4 4.4 convolution_convert_fusion
  250.8 8.5 %copy.20 = bf16[32,4,128,128]{2,0,3,1:T(8,128)(2,1)} copy(bf16[32,4,128,128]{3,1,0,2:T(4,128)(2,1)} %bitcast.95) | data formatting | bytes 8388608 | tf_op jit(solution)/shard_map/reshape | solution.py:33
  259.3 152.5 %all-reduce.9.cloned.1.call-done = (bf16[16,128,128]{2,0,1:T(8,128)(2,1)}, bf16[16,128,128]{2,0,1:T(8,128)(2,1)}) async-done(((bf16[16,128,128]{2,0,1:T(8,128)(2,1)}, bf16[16,128,128]{2,0,1:T(8,128)(2,1)}), (bf16[16,128,128]{2,0,1:T(8,128)(2,1)}, bf16[16,128,128]{2,0,1:T(8,128)(2,1)})) %all-reduce.9.cloned.1.call-update) | async-done | bytes 1048592 | tf_op jit(solution)/shard_map/psum | solution.py:16
  411.8 2.4 convolution_convert_fusion.1
  414.2 0.0 copy-start.3
  414.2 2.8 copy.18
  417.0 3.3 convolution_convert_fusion.2
  420.3 8.6 %copy.16 = bf16[32,4,128,128]{2,0,3,1:T(8,128)(2,1)} copy(bf16[32,4,128,128]{3,1,0,2:T(4,128)(2,1)} %bitcast.97) | data formatting | bytes 8388608 | tf_op jit(solution)/shard_map/reshape | solution.py:33
  428.9 1.4 convolution_convert_fusion.3
  430.2 0.8 copy.14
  431.1 1.4 copy-done
  432.4 1.3 copy-done.1
  433.7 2.5 fusion
  436.3 0.2 mul.24
  436.5 2.5 fusion.47
  439.0 63.9 %psum.71 = f32[512]{0:T(512)S(1)} all-reduce(f32[512]{0:T(512)S(1)} %get-tuple-element.21), channel_id=1, replica_groups=mesh['row'=32,'col'=16] {'row'}, use_global_device_ids=true, to_apply=%region_9.10 | all-reduce | flops 512 | bytes 4096 | tf_op jit(solution)/shard_map/psum | solution.py:59
  502.9 1.1 broadcast_multiply_fusion
  (17 shorter events, 0.0 us)
Async XLA Ops:
  6.5 6.0 %copy-start.5 = (s32[4,4]{1,0:T(4,128)S(1)}, s32[4,4]{1,0:T(4,128)}, u32[]{:S(2)}) copy-start(s32[4,4]{1,0:T(4,128)} %param.15) | copy-start | bytes 196
  6.5 6.1 %copy-start.8 = (s32[1,1,16]{2,1,0:T(1,128)S(1)}, s32[1,1,16]{2,1,0:T(1,128)}, u32[]{:S(2)}) copy-start(s32[1,1,16]{2,1,0:T(1,128)} %param.12) | copy-start | bytes 196
  6.5 26.6 %copy-start.7 = (s32[1,1,2]{2,1,0:T(1,128)S(1)}, s32[1,1,2]{2,1,0:T(1,128)}, u32[]{:S(2)}) copy-start(s32[1,1,2]{2,1,0:T(1,128)} %param.10) | copy-start | bytes 28
  6.5 26.6 %copy-start.6 = (s32[1,1,2,16]{3,2,1,0:T(2,128)S(1)}, s32[1,1,2,16]{3,2,1,0:T(2,128)}, u32[]{:S(2)}) copy-start(s32[1,1,2,16]{3,2,1,0:T(2,128)} %param.9) | copy-start | bytes 388
  6.5 239.9 %all-reduce.7.cloned.1.call-start = ((), (), s32[]{:S(2)}) async-start(), calls=%async_computation | async-start | bytes 2097152 | tf_op jit(solution)/shard_map/psum | solution.py:16
  9.0 402.8 %all-reduce.9.cloned.1.call-start = ((), (), s32[]{:S(2)}) async-start(), calls=%async_computation.1 | async-start | bytes 2097152 | tf_op jit(solution)/shard_map/psum | solution.py:16
  414.2 2.8 copy-start.3
  420.3 8.6 %copy-start.4 = (bf16[16,128,128]{2,0,1:T(8,128)(2,1)S(1)}, bf16[16,128,128]{2,0,1:T(8,128)(2,1)}, u32[]{:S(2)}) copy-start(bf16[16,128,128]{2,0,1:T(8,128)(2,1)} %get-tuple-element.12) | copy-start | bytes 1572868
  430.2 2.2 copy-start
  430.2 3.5 copy-start.1
  433.7 2.8 copy-start.2
  433.7 2.8 copy-start.9
Sparse Core Ops, SparseCore 0:
  10.3 236.0 all-reduce.6
  249.7 162.0 all-reduce.8
where the time goes:
time: 511 us
  waiting for transfers between devices  351 us (69%)
  blocking collectives  99.2 us (19%)
  local copies, waits for them, and re-layouts  24.8 us (5%)
  matrix products  16.5 us (3%)
  between operations  14.2 us (3%)
  other arithmetic  5.15 us (1%)
    psum x2, waiting for transfers between devices, spread(): return lax.psum(jnp.where(mine, array, jnp.zeros_like(array)), axis)  351 us
    psum x1, blocking collectives, local(): colsum = lax.psum(partial_value, 'row')  63.9 us
    psum x2, blocking collectives, spread(): return lax.psum(jnp.where(mine, array, jnp.zeros_like(array)), axis)  35.4 us
    reshape x2, local copies, waits for them, and re-layouts, section_product(): right_dense.reshape(W, NB, tile, tile).transpose(0, 2, 1, 3)  17.1 us
    dot_general x4, matrix products, place_tiles(): jnp.einsum('ap,auv->puv', onehot, tiles, preferred_element_type=jnp.float32)  11.4 us
  transfers between devices with their start and end apart: 2, of which 2 were waited for; matrix products, arithmetic and copies ran while one was open for 3% of the time, Pallas kernels for 0%

commit v1 on v0

v1 whole, which is shorter than its diff:
```python
import jax
import jax.numpy as jnp
from jax import lax
from jax.experimental import pallas as pl
from jax.experimental.pallas import tpu as pltpu
from jax.sharding import PartitionSpec as P

MB = 4
NB = 4
W = 32
KA = 16
KB = 16
SECTIONS = 2
TILE = 128
ROWS = 16384
Y_LO, Z, CORE = 2, 8, 2
Y_HI, X = 4, 4
N_ROW, N_COL = Y_LO * Z * CORE, Y_HI * X
LQ = SECTIONS * KA // X
RQ = KB // Z
PAD = 16


def row_of(y_lo, z, core):
    return (y_lo * Z + z) * CORE + core


def col_of(y_hi, x):
    return y_hi * X + x


def flat(row, col):
    return row * N_COL + col


def messages(tiles, slots, parts):
    per = tiles.shape[0] // parts
    body = tiles.reshape(parts, per * TILE, TILE)
    tail = jnp.pad(slots.astype(jnp.bfloat16).reshape(parts, 1, per), ((0, 0), (0, PAD - 1), (0, TILE - per)))
    return jnp.concatenate([body, tail], axis=1)


def slots_of(got, per):
    return got[:, per * TILE, :per].astype(jnp.int32).reshape(-1)


def only(condition, array):
    return jnp.where(condition, array, jnp.zeros_like(array))


X_GROUPS = [[col_of(y, x) for x in range(X)] for y in range(Y_HI)]
Z_GROUPS = [[row_of(y, z, c) for z in range(Z)] for y in range(Y_LO) for c in range(CORE)]
CY_GROUPS = [[row_of(y, z, c) for y in range(Y_LO) for c in range(CORE)] for z in range(Z)]


def gather(array, axis, groups):
    n = len(groups[0])
    return lax.all_to_all(jnp.broadcast_to(array, (n,) + array.shape), axis, 0, 0, axis_index_groups=groups)


def left_everywhere(message, row, col):
    y_lo, y_hi, x = row // (Z * CORE), col // X, col % X
    last = y_hi == Y_HI - 1
    have = only(last & (x == X - 1), message[X - 1])
    for q in (1, 0, 2):
        pairs = [(col_of(Y_HI - 1, X - 1), col_of(Y_HI - 1, q))]
        have = have + lax.ppermute(message[q], "col", pairs)
    both = ("row", "col")
    first, second = [], []
    for x_ in range(X):
        for z in range(Z):
            for c in range(CORE):
                lo, hi = row_of(0, z, c), row_of(1, z, c)
                at = lambda r, y: flat(r, col_of(y, x_))
                first += [(at(lo, 3), at(lo, 0)), (at(hi, 3), at(hi, 2))]
                second += [(at(lo, 3), at(lo, 2)), (at(lo, 0), at(lo, 1)), (at(hi, 3), at(hi, 0)), (at(hi, 2), at(hi, 1))]
    have = have + lax.ppermute(have, both, first)
    have = have + lax.ppermute(have, both, second)
    return gather(have, "col", X_GROUPS)


def right_everywhere(message, row):
    y_lo, z = row // (Z * CORE), (row // CORE) % Z
    have = only((y_lo == Y_LO - 1) & (z == Z - 1), message[Z - 1])
    for q in (3, 2, 4, 1, 5, 0, 6):
        pairs = [(row_of(1, Z - 1, c), row_of(1, q, c)) for c in range(CORE)]
        have = have + lax.ppermute(message[q], "row", pairs)
    have = have + lax.ppermute(have, "row", [(row_of(1, z_, c), row_of(0, z_, c)) for z_ in range(Z) for c in range(CORE)])
    mine = gather(have, "row", Z_GROUPS)
    other = lax.ppermute(mine, "row", [(r, r ^ 1) for r in range(N_ROW)])
    return mine, other


def product_kernel(core_ref, place_ref, block_ref, mask_ref, left_ref, mine_ref, other_ref, c_ref, kept_ref, sum_ref):
    kept_ref[...] = c_ref[...]
    core = core_ref[0]

    def section(base, right_ref):
        def step(t, carry):
            a = base + t
            quarter, inside = a // LQ, a % LQ
            rows = pl.ds(pl.multiple_of(block_ref[a] * TILE, TILE), TILE)
            for n in range(NB):
                p = place_ref[a * NB + n]

                @pl.when(p >= 0)
                def _():
                    left = left_ref[quarter, pl.ds(pl.multiple_of(inside * TILE, TILE), TILE), :]
                    right = right_ref[p // RQ, pl.ds(pl.multiple_of((p % RQ) * TILE, TILE), TILE), :]
                    columns = pl.ds(n * TILE, TILE)
                    kept_ref[rows, columns] += jnp.dot(left, right, preferred_element_type=jnp.float32)

            return carry

        lax.fori_loop(0, KA, step, 0)

    section(core * KA, mine_ref)
    section((1 - core) * KA, other_ref)
    for n in range(NB):
        columns = pl.ds(n * TILE, TILE)
        total = jnp.zeros((1, TILE), jnp.float32)
        for m in range(MB):
            rows = pl.ds(m * TILE, TILE)
            value = kept_ref[rows, columns]
            value = value * value * mask_ref[m * NB + n].astype(jnp.float32)
            kept_ref[rows, columns] = value
            total = total + jnp.sum(value, axis=0, keepdims=True)
        sum_ref[:, columns] = total


def product(core, place, block, mask, left, mine, other, c_partial):
    smem = pl.BlockSpec(memory_space=pltpu.SMEM)
    vmem = pl.BlockSpec(memory_space=pltpu.VMEM)
    return pl.pallas_call(
        product_kernel,
        out_shape=(
            jax.ShapeDtypeStruct((MB * TILE, NB * TILE), jnp.float32),
            jax.ShapeDtypeStruct((1, NB * TILE), jnp.float32),
        ),
        in_specs=[smem] * 4 + [vmem] * 4,
        out_specs=(vmem, vmem),
        compiler_params=pltpu.CompilerParams(vmem_limit_bytes=12 * 1024 * 1024),
    )(core, place, block, mask, left, mine, other, c_partial)


def local(a_tiles, a_index, a_count, b_tiles, b_index, b_count, c_partial, prune_mask):
    row, col = lax.axis_index("row"), lax.axis_index("col")
    core = row % CORE
    left_slots = jnp.where(jnp.arange(KA)[None, :] < a_count[0, 0][:, None], a_index[0, 0], -1)
    right_slots = jnp.where(jnp.arange(KB) < b_count[0, 0], b_index[0, 0], -1)
    left = left_everywhere(messages(a_tiles.reshape(SECTIONS * KA, TILE, TILE), left_slots, X), row, col)
    mine, other = right_everywhere(messages(b_tiles.reshape(KB, TILE, TILE), right_slots, Z), row)
    slot = slots_of(left, LQ)
    slot_mine, slot_other = slots_of(mine, RQ), slots_of(other, RQ)
    section = jnp.arange(SECTIONS * KA) // KA
    facing = jnp.where((section == core)[:, None], slot_mine[None, :], slot_other[None, :])
    wanted = (slot % W)[:, None] * NB + jnp.arange(NB)[None, :]
    hit = (facing[:, None, :] == wanted[:, :, None]) & (slot >= 0)[:, None, None]
    place = jnp.max(jnp.where(hit, jnp.arange(KB)[None, None, :], -1), axis=2).reshape(-1)
    block = jnp.maximum(slot, 0) // W
    kept, partial = product(core.reshape(1), place, block, prune_mask.reshape(-1), left, mine, other, c_partial)
    total = jnp.sum(gather(partial[0], "row", CY_GROUPS), axis=0)
    total = jnp.sum(gather(total, "row", Z_GROUPS), axis=0)
    return kept * (ROWS / total)[None, :]


def solution(mesh):
    return jax.shard_map(
        local,
        mesh=mesh,
        in_specs=(
            P("row", "col", None, None, None, None),
            P("row", "col", None, None),
            P("row", "col", None),
            P("row", "col", None, None, None),
            P("row", "col", None),
            P("row", "col"),
            P("row", "col"),
            P("row", "col"),
        ),
        out_specs=P("row", "col"),
        check_vma=False,
    )
```

time: 511 us -> 109 us (0.21)
  the two profiles are of different devices: /device:TPU:1 before, /device:TPU:16 now
where the time goes in v1:
time: 109 us; the launch traced here: 108 us
  waiting for transfers between devices  43.5 us (40%)
  starting transfers between devices  28.9 us (27%)
  blocking collectives  21.5 us (20%)
  local copies, waits for them, and re-layouts  5.34 us (5%)
  other arithmetic  5.2 us (5%)
  Pallas kernels  2.86 us (3%)
    all_to_all x2, blocking collectives, gather(): lax.all_to_all(jnp.broadcast_to(array, (n,) + array.shape), axis, 0, 0, a...  21.5 us
    ppermute x1, waiting for transfers between devices, left_everywhere(): have = have + lax.ppermute(have, both, second)  18.6 us
    all_to_all x2, starting transfers between devices, gather(): lax.all_to_all(jnp.broadcast_to(array, (n,) + array.shape), axis, 0, 0, a...  14.6 us
    ppermute x1, waiting for transfers between devices, right_everywhere(): lax.ppermute(have, 'row', [(row_of(1, z_, c), row_of(0, z_, c)) for z_ in...  12.6 us
    all_to_all x2, waiting for transfers between devices, gather(): lax.all_to_all(jnp.broadcast_to(array, (n,) + array.shape), axis, 0, 0, a...  12.3 us
    ppermute x7, starting transfers between devices, right_everywhere(): have = have + lax.ppermute(message[q], 'row', pairs)  7.14 us
    pallas_call x1, Pallas kernels, product(): pl.pallas_call(product_kernel, out_shape=(jax.ShapeDtypeStruct((MB * TILE...  2.86 us
  transfers between devices with their start and end apart: 16, of which 3 were waited for; matrix products, arithmetic and copies ran while one was open for 3% of the time, Pallas kernels for 0%

profile of v1, /device:TPU:16, one launch (start us, length us, event | category | flops | bytes accessed | tf_op | source)
XLA Modules:
  0.0 108.4 jit_solution(3481127928987359528)
XLA Ops:
  0.0 0.5 broadcast.225
  0.5 1.3 %reduce.17 = s32[16]{0:T(128)S(1)} reduce(s32[1,1,16]{2,1,0:T(1,128)} %param.12, s32[]{:T(128)} %broadcast.225), dimensions={0,1}, to_apply=%param.12.reduce_sub_computation.3 | reduce | bytes 132 | tf_op args[4]
  2.6 1.1 %fusion.3 = bf16[8,272,128]{2,1,0:T(8,128)(2,1)S(1)} fusion(bf16[8,1,2]{2,1,0:T(2,128)(2,1)S(1)} %copy.23, bf16[8,256,128]{2,1,0:T(8,128)(2,1)} %bitcast.54), kind=kLoop, calls=%fused_computation.5 | loop fusion | flops 1671168 | bytes 1081376 | tf_op jit(solution)/shard_map/concatenate | solution.py:40
  3.7 0.7 slice_bitcast_fusion.9
  4.4 0.7 collective-permute-start.6
  5.0 0.7 collective-permute-start.5
  5.7 0.7 collective-permute-start.4
  6.4 1.3 %collective-permute-start.3 = (bf16[272,128]{1,0:T(8,128)(2,1)S(1)}, bf16[272,128]{1,0:T(8,128)(2,1)}, u32[]{:S(2)}, u32[]{:S(2)}) collective-permute-start(bf16[272,128]{1,0:T(8,128)(2,1)S(1)} %get-tuple-element.16), channel_id=1, source_target_pairs={{480,288},{496,304},{481,289},{497,305},{482,290},{498,306},{483,2... | collective-permute-start | bytes 208904 | tf_op jit(solution)/shard_map/ppermute | solution.py:87
  7.7 1.3 %collective-permute-start.2 = (bf16[272,128]{1,0:T(8,128)(2,1)S(1)}, bf16[272,128]{1,0:T(8,128)(2,1)}, u32[]{:S(2)}, u32[]{:S(2)}) collective-permute-start(bf16[272,128]{1,0:T(8,128)(2,1)S(1)} %get-tuple-element.17), channel_id=1, source_target_pairs={{480,384},{496,400},{481,385},{497,401},{482,386},{498,402},{483,3... | collective-permute-start | bytes 208904 | tf_op jit(solution)/shard_map/ppermute | solution.py:87
  9.4 1.3 %collective-permute-start.1 = (bf16[272,128]{1,0:T(8,128)(2,1)}, bf16[272,128]{1,0:T(8,128)(2,1)}, u32[]{:S(2)}, u32[]{:S(2)}) collective-permute-start(bf16[272,128]{1,0:T(8,128)(2,1)} %get-tuple-element.18), channel_id=1, source_target_pairs={{480,320},{496,336},{481,321},{497,337},{482,322},{498,338},{483,3... | collective-permute-start | bytes 208904 | tf_op jit(solution)/shard_map/ppermute | solution.py:87
  10.7 1.3 %collective-permute-start = (bf16[272,128]{1,0:T(8,128)(2,1)}, bf16[272,128]{1,0:T(8,128)(2,1)}, u32[]{:S(2)}, u32[]{:S(2)}) collective-permute-start(bf16[272,128]{1,0:T(8,128)(2,1)} %get-tuple-element.12), channel_id=1, source_target_pairs={{480,352},{496,368},{481,353},{497,369},{482,354},{498,370},{483,3... | collective-permute-start | bytes 208904 | tf_op jit(solution)/shard_map/ppermute | solution.py:87
  12.1 0.7 collective-permute-start.11
  12.8 0.7 collective-permute-start.10
  13.5 0.7 collective-permute-start.9
  14.2 1.0 fusion.15
  15.2 1.3 %collective-permute-start.7 = (bf16[272,128]{1,0:T(8,128)(2,1)S(1)}, bf16[272,128]{1,0:T(8,128)(2,1)S(1)}, u32[]{:S(2)}, u32[]{:S(2)}) collective-permute-start(bf16[272,128]{1,0:T(8,128)(2,1)S(1)} %fusion.15), channel_id=1, source_target_pairs={{256,0},{272,16},{288,32},{304,48},{320,64},{336,80},{352,96},{368... | collective-permute-start | bytes 208904 | tf_op jit(solution)/shard_map/ppermute | solution.py:88
  16.5 12.6 %collective-permute-done.7 = bf16[272,128]{1,0:T(8,128)(2,1)S(1)} collective-permute-done((bf16[272,128]{1,0:T(8,128)(2,1)S(1)}, bf16[272,128]{1,0:T(8,128)(2,1)S(1)}, u32[]{:S(2)}, u32[]{:S(2)}) %collective-permute-start.7) | collective-permute-done | bytes 69664 | tf_op jit(solution)/shard_map/ppermute | solution.py:88
  29.1 0.9 broadcast_in_dim.74
  30.0 10.1 %all-to-all-start = ((bf16[8,272,128]{2,1,0:T(8,128)(2,1)}), bf16[8,272,128]{2,1,0:T(8,128)(2,1)S(1)}, u32[]{:S(2)}, u32[]{:S(2)}) async-start(bf16[8,272,128]{2,1,0:T(8,128)(2,1)} %broadcast_in_dim.74), calls=%async_computation | async-start | bytes 1114112 | tf_op jit(solution)/shard_map/all_to_all | solution.py:58
  40.3 0.7 collective-permute-start.12
  41.0 1.3 %collective-permute-start.13 = (bf16[1040,128]{1,0:T(8,128)(2,1)S(1)}, bf16[1040,128]{1,0:T(8,128)(2,1)S(1)}, u32[]{:S(2)}, u32[]{:S(2)}) collective-permute-start(bf16[1040,128]{1,0:T(8,128)(2,1)S(1)} %add.116), channel_id=1, source_target_pairs={{12,8},{0,4},{268,256},{264,260},{28,24},{16,20},{284,272},{280,27... | collective-permute-start | bytes 798728 | tf_op jit(solution)/shard_map/ppermute | solution.py:78
  42.3 18.6 %collective-permute-done.13 = bf16[1040,128]{1,0:T(8,128)(2,1)S(1)} collective-permute-done((bf16[1040,128]{1,0:T(8,128)(2,1)S(1)}, bf16[1040,128]{1,0:T(8,128)(2,1)S(1)}, u32[]{:S(2)}, u32[]{:S(2)}) %collective-permute-start.13) | collective-permute-done | bytes 266272 | tf_op jit(solution)/shard_map/ppermute | solution.py:78
  61.0 1.1 %broadcast_in_dim.79 = bf16[4,1040,128]{2,1,0:T(8,128)(2,1)} broadcast(bf16[1040,128]{1,0:T(8,128)(2,1)S(1)} %add.117), dimensions={1,2} | broadcast | bytes 1331200 | tf_op jit(solution)/shard_map/broadcast_in_dim | solution.py:58
  62.1 4.4 %all-to-all-start.1 = ((bf16[4,1040,128]{2,1,0:T(8,128)(2,1)}), bf16[4,1040,128]{2,1,0:T(8,128)(2,1)S(1)}, u32[]{:S(2)}, u32[]{:S(2)}) async-start(bf16[4,1040,128]{2,1,0:T(8,128)(2,1)} %broadcast_in_dim.79), calls=%async_computation.1 | async-start | bytes 2129920 | tf_op jit(solution)/shard_map/all_to_all | solution.py:58
  66.7 1.9 %collective-permute-start.8 = (bf16[8,272,128]{2,1,0:T(8,128)(2,1)S(1)}, bf16[8,272,128]{2,1,0:T(8,128)(2,1)S(1)}, u32[]{:S(2)}, u32[]{:S(2)}) collective-permute-start(bf16[8,272,128]{2,1,0:T(8,128)(2,1)S(1)} %all-to-all-done.mine_ref), channel_id=1, source_target_pairs={{0,16},{16,0},{32,48},{48,32},{64,80},{80,64},{96,112},{112,96},{1... | collective-permute-start | bytes 1671176 | tf_op jit(solution)/shard_map/ppermute | solution.py:90
  68.7 12.3 %all-to-all-done.1.left_ref = bf16[4,1040,128]{2,1,0:T(8,128)(2,1)S(1)} async-done(((bf16[4,1040,128]{2,1,0:T(8,128)(2,1)}), bf16[4,1040,128]{2,1,0:T(8,128)(2,1)S(1)}, u32[]{:S(2)}, u32[]{:S(2)}) %all-to-all-start.1) | async-done | bytes 1064992 | tf_op jit(solution)/shard_map/all_to_all | solution.py:58
  81.5 0.1 reshape.227.place_ref
  81.6 1.2 %copy-done = f32[512,512]{1,0:T(8,128)S(1)} copy-done((f32[512,512]{1,0:T(8,128)S(1)}, f32[512,512]{1,0:T(8,128)}, u32[]{:S(2)}) %copy-start) | copy-done | bytes 1048600
  82.8 2.9 %shard_map.82 = (f32[512,512]{1,0:T(8,128)S(1)}, f32[1,512]{1,0:T(1,128)S(1)}) custom-call(s32[1]{0:T(128)} %bitcast.core_ref, s32[128]{0:T(128)S(1)} %reshape.227.place_ref, s32[32]{0:T(128)S(1)} %get-tuple-element.19.block_ref, s32[16]{0:T(128)S(1)} %reshape.228.mask_ref, bf16[4,1040,128]{2,1,0:T(8,128)(2,1)S(1)} %all-to-all-done.1.left_ref, ...), custom_call_target="tpu_custom_call" | custom-call | tf_op jit(solution)/shard_map/pallas_call | solution.py:134
  85.7 6.2 %all_to_all.22 = f32[4,1,512]{2,1,0:T(1,128)S(1)} all-to-all(f32[4,1,512]{2,1,0:T(1,128)S(1)} %broadcast_in_dim.82), channel_id=1, replica_groups={{0,16,256,272},{32,48,288,304},{64,80,320,336},{96,112,352,368},{128,14..., dimensions={0} | all-to-all | bytes 16384 | tf_op jit(solution)/shard_map/all_to_all | solution.py:58
  91.9 15.4 %all_to_all.23 = f32[8,1,512]{2,1,0:T(1,128)S(1)} all-to-all(f32[8,1,512]{2,1,0:T(1,128)S(1)} %broadcast_in_dim.83), channel_id=1, replica_groups={{0,32,64,96,128,160,192,224},{16,48,80,112,144,176,208,240},{256,288,32..., dimensions={0} | all-to-all | bytes 32768 | tf_op jit(solution)/shard_map/all_to_all | solution.py:58
  107.3 1.1 %broadcast_multiply_fusion = f32[512,512]{1,0:T(8,128)} fusion(f32[512,512]{1,0:T(8,128)S(1)} %get-tuple-element.7, f32[512]{0:T(512)S(1)} %broadcast_divide_fusion), kind=kLoop, calls=%fused_computation.6 | loop fusion | flops 262144 | bytes 2099200 | tf_op jit(solution)/shard_map/mul | solution.py:164
  (57 shorter events, 1.5 us)
Async XLA Ops:
  0.0 9.0 %copy-start.3 = (s32[1,1,2,16]{3,2,1,0:T(2,128)S(1)}, s32[1,1,2,16]{3,2,1,0:T(2,128)}, u32[]{:S(2)}) copy-start(s32[1,1,2,16]{3,2,1,0:T(2,128)} %param.9) | copy-start | bytes 388
  0.0 9.1 %copy-start.4 = (s32[1,1,2]{2,1,0:T(1,128)S(1)}, s32[1,1,2]{2,1,0:T(1,128)}, u32[]{:S(2)}) copy-start(s32[1,1,2]{2,1,0:T(1,128)} %param.10) | copy-start | bytes 28
  0.0 9.3 %copy-start.1 = (bf16[1,1,2,16,128,128]{5,4,3,2,1,0:T(8,128)(2,1)S(1)}, bf16[1,1,2,16,128,128]{5,4,3,2,1,0:T(8,128)(2,1)}, u32[]{:S(2)}) copy-start(bf16[1,1,2,16,128,128]{5,4,3,2,1,0:T(8,128)(2,1)} %param.8) | copy-start | bytes 3145732
  4.4 5.0 %collective-permute-start.6 = (bf16[272,128]{1,0:T(8,128)(2,1)S(1)}, bf16[272,128]{1,0:T(8,128)(2,1)S(1)}, u32[]{:S(2)}, u32[]{:S(2)}) collective-permute-start(bf16[272,128]{1,0:T(8,128)(2,1)S(1)} %get-tuple-element.13), channel_id=1, source_target_pairs={{480,448},{496,464},{481,449},{497,465},{482,450},{498,466},{483,4... | collective-permute-start | bytes 208904 | tf_op jit(solution)/shard_map/ppermute | solution.py:87
  5.0 5.6 %collective-permute-start.5 = (bf16[272,128]{1,0:T(8,128)(2,1)S(1)}, bf16[272,128]{1,0:T(8,128)(2,1)S(1)}, u32[]{:S(2)}, u32[]{:S(2)}) collective-permute-start(bf16[272,128]{1,0:T(8,128)(2,1)S(1)} %get-tuple-element.14), channel_id=1, source_target_pairs={{480,256},{496,272},{481,257},{497,273},{482,258},{498,274},{483,2... | collective-permute-start | bytes 208904 | tf_op jit(solution)/shard_map/ppermute | solution.py:87
  5.7 6.4 %collective-permute-start.4 = (bf16[272,128]{1,0:T(8,128)(2,1)S(1)}, bf16[272,128]{1,0:T(8,128)(2,1)S(1)}, u32[]{:S(2)}, u32[]{:S(2)}) collective-permute-start(bf16[272,128]{1,0:T(8,128)(2,1)S(1)} %get-tuple-element.15), channel_id=1, source_target_pairs={{480,416},{496,432},{481,417},{497,433},{482,418},{498,434},{483,4... | collective-permute-start | bytes 208904 | tf_op jit(solution)/shard_map/ppermute | solution.py:87
  6.4 6.4 %collective-permute-start.3 = (bf16[272,128]{1,0:T(8,128)(2,1)S(1)}, bf16[272,128]{1,0:T(8,128)(2,1)}, u32[]{:S(2)}, u32[]{:S(2)}) collective-permute-start(bf16[272,128]{1,0:T(8,128)(2,1)S(1)} %get-tuple-element.16), channel_id=1, source_target_pairs={{480,288},{496,304},{481,289},{497,305},{482,290},{498,306},{483,2... | collective-permute-start | bytes 208904 | tf_op jit(solution)/shard_map/ppermute | solution.py:87
  7.7 5.8 %collective-permute-start.2 = (bf16[272,128]{1,0:T(8,128)(2,1)S(1)}, bf16[272,128]{1,0:T(8,128)(2,1)}, u32[]{:S(2)}, u32[]{:S(2)}) collective-permute-start(bf16[272,128]{1,0:T(8,128)(2,1)S(1)} %get-tuple-element.17), channel_id=1, source_target_pairs={{480,384},{496,400},{481,385},{497,401},{482,386},{498,402},{483,3... | collective-permute-start | bytes 208904 | tf_op jit(solution)/shard_map/ppermute | solution.py:87
  9.4 4.8 %collective-permute-start.1 = (bf16[272,128]{1,0:T(8,128)(2,1)}, bf16[272,128]{1,0:T(8,128)(2,1)}, u32[]{:S(2)}, u32[]{:S(2)}) collective-permute-start(bf16[272,128]{1,0:T(8,128)(2,1)} %get-tuple-element.18), channel_id=1, source_target_pairs={{480,320},{496,336},{481,321},{497,337},{482,322},{498,338},{483,3... | collective-permute-start | bytes 208904 | tf_op jit(solution)/shard_map/ppermute | solution.py:87
  10.7 3.5 %collective-permute-start = (bf16[272,128]{1,0:T(8,128)(2,1)}, bf16[272,128]{1,0:T(8,128)(2,1)}, u32[]{:S(2)}, u32[]{:S(2)}) collective-permute-start(bf16[272,128]{1,0:T(8,128)(2,1)} %get-tuple-element.12), channel_id=1, source_target_pairs={{480,352},{496,368},{481,353},{497,369},{482,354},{498,370},{483,3... | collective-permute-start | bytes 208904 | tf_op jit(solution)/shard_map/ppermute | solution.py:87
  12.1 28.1 %collective-permute-start.11 = (bf16[1040,128]{1,0:T(8,128)(2,1)S(1)}, bf16[1040,128]{1,0:T(8,128)(2,1)S(1)}, u32[]{:S(2)}, u32[]{:S(2)}) collective-permute-start(bf16[1040,128]{1,0:T(8,128)(2,1)S(1)} %get-tuple-element.10), channel_id=1, source_target_pairs={{15,14},{31,30},{47,46},{63,62},{79,78},{95,94},{111,110},{127,126... | collective-permute-start | bytes 798728 | tf_op jit(solution)/shard_map/ppermute | solution.py:67
  12.8 27.4 %collective-permute-start.10 = (bf16[1040,128]{1,0:T(8,128)(2,1)S(1)}, bf16[1040,128]{1,0:T(8,128)(2,1)S(1)}, u32[]{:S(2)}, u32[]{:S(2)}) collective-permute-start(bf16[1040,128]{1,0:T(8,128)(2,1)S(1)} %get-tuple-element.11), channel_id=1, source_target_pairs={{15,12},{31,28},{47,44},{63,60},{79,76},{95,92},{111,108},{127,124... | collective-permute-start | bytes 798728 | tf_op jit(solution)/shard_map/ppermute | solution.py:67
  13.5 26.7 %collective-permute-start.9 = (bf16[1040,128]{1,0:T(8,128)(2,1)S(1)}, bf16[1040,128]{1,0:T(8,128)(2,1)S(1)}, u32[]{:S(2)}, u32[]{:S(2)}) collective-permute-start(bf16[1040,128]{1,0:T(8,128)(2,1)S(1)} %get-tuple-element.9), channel_id=1, source_target_pairs={{15,13},{31,29},{47,45},{63,61},{79,77},{95,93},{111,109},{127,125... | collective-permute-start | bytes 798728 | tf_op jit(solution)/shard_map/ppermute | solution.py:67
  15.2 13.9 %collective-permute-start.7 = (bf16[272,128]{1,0:T(8,128)(2,1)S(1)}, bf16[272,128]{1,0:T(8,128)(2,1)S(1)}, u32[]{:S(2)}, u32[]{:S(2)}) collective-permute-start(bf16[272,128]{1,0:T(8,128)(2,1)S(1)} %fusion.15), channel_id=1, source_target_pairs={{256,0},{272,16},{288,32},{304,48},{320,64},{336,80},{352,96},{368... | collective-permute-start | bytes 208904 | tf_op jit(solution)/shard_map/ppermute | solution.py:88
  30.0 31.0 %all-to-all-start = ((bf16[8,272,128]{2,1,0:T(8,128)(2,1)}), bf16[8,272,128]{2,1,0:T(8,128)(2,1)S(1)}, u32[]{:S(2)}, u32[]{:S(2)}) async-start(bf16[8,272,128]{2,1,0:T(8,128)(2,1)} %broadcast_in_dim.74), calls=%async_computation | async-start | bytes 1114112 | tf_op jit(solution)/shard_map/all_to_all | solution.py:58
  40.3 0.7 collective-permute-start.12
  41.0 19.9 %collective-permute-start.13 = (bf16[1040,128]{1,0:T(8,128)(2,1)S(1)}, bf16[1040,128]{1,0:T(8,128)(2,1)S(1)}, u32[]{:S(2)}, u32[]{:S(2)}) collective-permute-start(bf16[1040,128]{1,0:T(8,128)(2,1)S(1)} %add.116), channel_id=1, source_target_pairs={{12,8},{0,4},{268,256},{264,260},{28,24},{16,20},{284,272},{280,27... | collective-permute-start | bytes 798728 | tf_op jit(solution)/shard_map/ppermute | solution.py:78
  62.1 4.4 %copy-start.2 = (s32[4,4]{1,0:T(4,128)S(1)}, s32[4,4]{1,0:T(4,128)}, u32[]{:S(2)}) copy-start(s32[4,4]{1,0:T(4,128)} %param.15) | copy-start | bytes 196
  62.1 18.9 %all-to-all-start.1 = ((bf16[4,1040,128]{2,1,0:T(8,128)(2,1)}), bf16[4,1040,128]{2,1,0:T(8,128)(2,1)S(1)}, u32[]{:S(2)}, u32[]{:S(2)}) async-start(bf16[4,1040,128]{2,1,0:T(8,128)(2,1)} %broadcast_in_dim.79), calls=%async_computation.1 | async-start | bytes 2129920 | tf_op jit(solution)/shard_map/all_to_all | solution.py:58
  66.7 14.4 %collective-permute-start.8 = (bf16[8,272,128]{2,1,0:T(8,128)(2,1)S(1)}, bf16[8,272,128]{2,1,0:T(8,128)(2,1)S(1)}, u32[]{:S(2)}, u32[]{:S(2)}) collective-permute-start(bf16[8,272,128]{2,1,0:T(8,128)(2,1)S(1)} %all-to-all-done.mine_ref), channel_id=1, source_target_pairs={{0,16},{16,0},{32,48},{48,32},{64,80},{80,64},{96,112},{112,96},{1... | collective-permute-start | bytes 1671176 | tf_op jit(solution)/shard_map/ppermute | solution.py:90
  81.6 1.2 %copy-start = (f32[512,512]{1,0:T(8,128)S(1)}, f32[512,512]{1,0:T(8,128)}, u32[]{:S(2)}) copy-start(f32[512,512]{1,0:T(8,128)} %c_ref.1) | copy-start | bytes 3145732

commit v2 on v1

v2 whole, which is shorter than its diff:
```python
import jax
import jax.numpy as jnp
from jax import lax
from jax.experimental import pallas as pl
from jax.experimental.pallas import tpu as pltpu
from jax.sharding import PartitionSpec as P

MB = 4
NB = 4
W = 32
KA = 16
KB = 16
SECTIONS = 2
TILE = 128
ROWS = 16384
Y_LO, Z, CORE = 2, 8, 2
Y_HI, X = 4, 4
N_ROW, N_COL = Y_LO * Z * CORE, Y_HI * X
LQ = SECTIONS * KA // X
HALVES = 2
RH = KB // HALVES
PAD = 16


def row_of(y_lo, z, core):
    return (y_lo * Z + z) * CORE + core


def col_of(y_hi, x):
    return y_hi * X + x


def flat(row, col):
    return row * N_COL + col


def slots_of(got, per):
    return got[:, per * TILE, :per].astype(jnp.int32).reshape(-1)


Z_GROUPS = [[row_of(y, z, c) for z in range(Z)] for y in range(Y_LO) for c in range(CORE)]
CY_GROUPS = [[row_of(y, z, c) for y in range(Y_LO) for c in range(CORE)] for z in range(Z)]


def gather(array, axis, groups):
    n = len(groups[0])
    return lax.all_to_all(jnp.broadcast_to(array, (n,) + array.shape), axis, 0, 0, axis_index_groups=groups)


def y_pairs():
    first, second = [], []
    for z in range(Z):
        for c in range(CORE):
            for x in range(X):
                lo = lambda y: flat(row_of(0, z, c), col_of(y, x))
                hi = lambda y: flat(row_of(1, z, c), col_of(y, x))
                first += [(lo(3), lo(0)), (hi(3), hi(2))]
                second += [(lo(3), lo(2)), (lo(0), lo(1)), (hi(3), hi(0)), (hi(2), hi(1))]
    return first, second


def after(array, *others):
    return lax.optimization_barrier((array, *others))[0]


def messages_kernel(a_index_ref, a_count_ref, b_index_ref, b_count_ref, a_ref, b_ref, *refs):
    quarter_refs, left_ref, half_refs, sems = refs[: X - 1], refs[X - 1], refs[X : X + HALVES], refs[-1]
    row, col = lax.axis_index("row"), lax.axis_index("col")
    own, root = col == N_COL - 1, row >= N_ROW - CORE
    lane = lax.broadcasted_iota(jnp.int32, (PAD, TILE), 1)
    body, end = pl.ds(0, LQ * TILE), pl.ds(LQ * TILE, PAD)

    def tail(slot_of):
        line = jnp.full((PAD, TILE), -1, jnp.int32)
        for t in range(LQ):
            line = jnp.where(lane == t, slot_of(t), line)
        return line.astype(jnp.float32).astype(jnp.bfloat16)

    @pl.when(own)
    def _():
        outs = (*quarter_refs, left_ref)
        copies = [
            pltpu.make_async_copy(a_ref.at[pl.ds(q * LQ * TILE, LQ * TILE), :], ref.at[body, :], sems.at[q])
            for q, ref in enumerate(outs)
        ]
        for copy in copies:
            copy.start()
        for q, ref in enumerate(outs):

            def slot_of(t, q=q):
                section, place = divmod(q * LQ + t, KA)
                return jnp.where(place < a_count_ref[section], a_index_ref[section * KA + place], -1)

            ref[end, :] = tail(slot_of)
        for copy in copies:
            copy.wait()

    @pl.when(jnp.logical_not(own))
    def _():
        left_ref[...] = jnp.zeros_like(left_ref)

    @pl.when(root)
    def _():
        copies = [
            pltpu.make_async_copy(b_ref.at[pl.ds(h * RH * TILE, RH * TILE), :], ref.at[body, :], sems.at[X + h])
            for h, ref in enumerate(half_refs)
        ]
        for copy in copies:
            copy.start()
        for h, ref in enumerate(half_refs):

            def slot_of(t, h=h):
                return jnp.where(h * RH + t < b_count_ref[0], b_index_ref[h * RH + t], -1)

            ref[end, :] = tail(slot_of)
        for copy in copies:
            copy.wait()

    @pl.when(jnp.logical_not(root))
    def _():
        for ref in half_refs:
            ref[...] = jnp.zeros_like(ref)


def messages(a_tiles, a_index, a_count, b_tiles, b_index, b_count):
    smem = pl.BlockSpec(memory_space=pltpu.SMEM)
    vmem = pl.BlockSpec(memory_space=pltpu.VMEM)
    hbm = pl.BlockSpec(memory_space=pltpu.HBM)
    return pl.pallas_call(
        messages_kernel,
        out_shape=[jax.ShapeDtypeStruct((LQ * TILE + PAD, TILE), jnp.bfloat16)] * (X + HALVES),
        in_specs=[smem] * 4 + [hbm] * 2,
        out_specs=[vmem] * (X + HALVES),
        scratch_shapes=[pltpu.SemaphoreType.DMA((X + HALVES,))],
        compiler_params=pltpu.CompilerParams(vmem_limit_bytes=4 * 1024 * 1024),
    )(a_index, a_count, b_index, b_count, a_tiles, b_tiles)


def right_steps(h):
    def at(place):
        return (Z - 1 + (place if h == 0 else -place)) % Z

    along = ([(0, 3)], [(0, 2), (3, 5)], [(2, 1), (0, 7), (3, 4), (5, 6)])
    return [[((1, Z - 1), (0, Z - 1))]] + [[((y, at(a)), (y, at(b))) for a, b in step for y in range(Y_LO)] for step in along]


def panels_everywhere(a_tiles, a_index, a_count, b_tiles, b_index, b_count, c_partial):
    both = ("row", "col")
    first, second = y_pairs()
    *quarters, left, half0, half1 = messages(
        a_tiles.reshape(SECTIONS * KA * TILE, TILE),
        a_index.reshape(-1),
        a_count.reshape(-1),
        b_tiles.reshape(KB * TILE, TILE),
        b_index.reshape(-1),
        b_count.reshape(-1),
    )
    mine = [half0, half1]
    for q in (1, 0, 2):
        with jax.named_scope("left_scatter"):
            left = left + lax.ppermute(quarters[q], "col", [(col_of(Y_HI - 1, X - 1), col_of(Y_HI - 1, q))])

    def right_step(i):
        for h in range(HALVES):
            with jax.named_scope("right_step"):
                pairs = [(row_of(*a, c), row_of(*b, c)) for a, b in right_steps(h)[i] for c in range(CORE)]
                mine[h] = mine[h] + lax.ppermute(mine[h], "row", pairs)

    def right_after(*arrays):
        for h in range(HALVES):
            mine[h] = after(mine[h], *arrays)

    right_step(0)
    c_partial = after(c_partial, left)
    right_after(left)
    with jax.named_scope("left_y"):
        left = left + lax.ppermute(left, both, first)
    right_step(1)
    held = hold(c_partial)
    right_after(left, held)
    with jax.named_scope("left_y"):
        left = left + lax.ppermute(left, both, second)
    right_step(2)
    right_after(left)
    lefts = [left]
    for d in range(1, X):
        with jax.named_scope("left_x"):
            pairs = [(col_of(y, x_), col_of(y, (x_ + d) % X)) for y in range(Y_HI) for x_ in range(X)]
            lefts.append(lax.ppermute(left, "col", pairs))
    right_step(3)
    with jax.named_scope("right_core"):
        other = lax.ppermute(jnp.stack(mine), "row", [(r, r ^ 1) for r in range(N_ROW)])
    return lefts, [*mine, other], held


def hold_kernel(c_ref, held_ref):
    held_ref[...] = c_ref[...]


def hold(c_partial):
    vmem = pl.BlockSpec(memory_space=pltpu.VMEM)
    return pl.pallas_call(
        hold_kernel,
        out_shape=jax.ShapeDtypeStruct((MB * TILE, NB * TILE), jnp.float32),
        in_specs=[vmem],
        out_specs=vmem,
        compiler_params=pltpu.CompilerParams(vmem_limit_bytes=4 * 1024 * 1024),
    )(c_partial)


def product_kernel(slot_ref, table_ref, mask_ref, *refs):
    lefts, (*mine, other_ref), (held_ref, kept_ref, sum_ref) = refs[:X], refs[X : X + HALVES + 1], refs[X + HALVES + 1 :]
    rights = [*mine, *(other_ref.at[h] for h in range(HALVES))]
    kept_ref[...] = held_ref[...]
    core, x = lax.axis_index("row") % CORE, lax.axis_index("col") % X
    for d, left_ref in enumerate(lefts):
        section = ((x + X - d) % X) // (X // SECTIONS)
        which = jnp.where(section == core, 0, 1)

        def step(t, carry):
            slot = slot_ref[d * LQ + t]

            @pl.when(slot >= 0)
            def _():
                rows = pl.ds(pl.multiple_of((slot // W) * TILE, TILE), TILE)
                tile = pl.ds(pl.multiple_of(t * TILE, TILE), TILE)
                for n in range(NB):
                    p = table_ref[which * W * NB + (slot % W) * NB + n]

                    @pl.when(p >= 0)
                    def _():
                        for r in range(2 * HALVES):

                            @pl.when(which * HALVES + p // RH == r)
                            def _():
                                right = rights[r][pl.ds(pl.multiple_of((p % RH) * TILE, TILE), TILE), :]
                                columns = pl.ds(n * TILE, TILE)
                                kept_ref[rows, columns] += jnp.dot(
                                    left_ref[tile, :], right, preferred_element_type=jnp.float32
                                )

            return carry

        lax.fori_loop(0, LQ, step, 0)

    for n in range(NB):
        columns = pl.ds(n * TILE, TILE)
        total = jnp.zeros((1, TILE), jnp.float32)
        for m in range(MB):
            rows = pl.ds(m * TILE, TILE)
            value = kept_ref[rows, columns]
            value = value * value * mask_ref[m * NB + n].astype(jnp.float32)
            kept_ref[rows, columns] = value
            total = total + jnp.sum(value, axis=0, keepdims=True)
        sum_ref[:, columns] = total


def product(slot, table, mask, lefts, rights, held):
    smem = pl.BlockSpec(memory_space=pltpu.SMEM)
    vmem = pl.BlockSpec(memory_space=pltpu.VMEM)
    return pl.pallas_call(
        product_kernel,
        out_shape=(
            jax.ShapeDtypeStruct((MB * TILE, NB * TILE), jnp.float32),
            jax.ShapeDtypeStruct((1, NB * TILE), jnp.float32),
        ),
        in_specs=[smem] * 3 + [vmem] * (len(lefts) + len(rights) + 1),
        out_specs=(vmem, vmem),
        input_output_aliases={3 + len(lefts) + len(rights): 0},
        compiler_params=pltpu.CompilerParams(vmem_limit_bytes=6 * 1024 * 1024),
    )(slot, table, mask, *lefts, *rights, held)


def local(a_tiles, a_index, a_count, b_tiles, b_index, b_count, c_partial, prune_mask):
    lefts, rights, held = panels_everywhere(a_tiles, a_index, a_count, b_tiles, b_index, b_count, c_partial)
    *mine, other = rights
    facing = jnp.stack([slots_of(right[None], RH) for right in (*mine, *other)]).reshape(2, 1, KB)
    hit = facing == jnp.arange(W * NB)[None, :, None]
    table = jnp.max(jnp.where(hit, jnp.arange(KB)[None, None, :], -1), axis=2).reshape(-1)
    slot = jnp.stack([slots_of(left[None], LQ) for left in lefts]).reshape(-1)
    kept, partial = product(slot, table, prune_mask.reshape(-1), lefts, rights, held)
    total = jnp.sum(gather(partial[0], "row", CY_GROUPS), axis=0)
    total = jnp.sum(gather(total, "row", Z_GROUPS), axis=0)
    return kept * (ROWS / total)[None, :]


def solution(mesh):
    return jax.shard_map(
        local,
        mesh=mesh,
        in_specs=(
            P("row", "col", None, None, None, None),
            P("row", "col", None, None),
            P("row", "col", None),
            P("row", "col", None, None, None),
            P("row", "col", None),
            P("row", "col"),
            P("row", "col"),
            P("row", "col"),
        ),
        out_specs=P("row", "col"),
        check_vma=False,
    )
```

time: 109 us -> 99.5 us (0.913)
  waiting for transfers between devices: 43.5 us -> 34 us
  blocking collectives: 21.5 us -> 28 us
  starting transfers between devices: 28.9 us -> 25.7 us
  other arithmetic: 5.2 us -> 2.94 us
  local copies, waits for them, and re-layouts: 5.34 us -> 3.33 us
    all_to_all x2 -> x0, starting transfers between devices: 14.6 us -> none  [gather(): lax.all_to_all(jnp.broadcast_to(array, (n,) + array.shape), axis, 0, 0, a...]
    all_to_all x2 -> x0, waiting for transfers between devices: 12.3 us -> none  [gather(): lax.all_to_all(jnp.broadcast_to(array, (n,) + array.shape), axis, 0, 0, a...]
    ppermute x14 -> x17, starting transfers between devices: 14.3 us -> 25.7 us  [the longest x3 13 us: panels_everywhere(): lefts.append(lax.ppermute(left, 'col', pairs))]
    all_to_all x2, blocking collectives: 21.5 us -> 28 us  [gather(): lax.all_to_all(jnp.broadcast_to(array, (n,) + array.shape), axis, 0, 0, a...]
    ppermute x14 -> x17, waiting for transfers between devices: 31.2 us -> 34 us  [the longest x1 27 us: panels_everywhere(): left = left + lax.ppermute(left, both, second)]
    broadcast_in_dim x4 -> x2, local copies, waits for them, and re-layouts: 2.01 us -> 0.02 us  [gather(): jnp.broadcast_to(array, (n,) + array.shape)]
    unnamed x1 -> x0, other arithmetic: 1.32 us -> none
    unnamed x13 -> x14, local copies, waits for them, and re-layouts: 1.76 us -> 2.96 us
  transfers between devices with their start and end apart: 16 -> 17, of which waited for: 3 -> 4; matrix products, arithmetic and copies ran while one was open for 3% -> 2% of each run, Pallas kernels for 0% -> 0%
where the time goes in v2:
time: 99.5 us; the launch traced here: 98.9 us
  waiting for transfers between devices  34 us (34%)
  blocking collectives  28 us (28%)
  starting transfers between devices  25.7 us (26%)
  Pallas kernels  3.89 us (4%)
  local copies, waits for them, and re-layouts  3.33 us (3%)
  other arithmetic  2.94 us (3%)
  between operations  1.08 us (1%)
    all_to_all x2, blocking collectives, gather(): lax.all_to_all(jnp.broadcast_to(array, (n,) + array.shape), axis, 0, 0, a...  28 us
    ppermute x1, waiting for transfers between devices, panels_everywhere(): left = left + lax.ppermute(left, both, second)  27 us
    ppermute x3, starting transfers between devices, panels_everywhere(): lefts.append(lax.ppermute(left, 'col', pairs))  13 us
    ppermute x8, starting transfers between devices, right_step(): mine[h] = mine[h] + lax.ppermute(mine[h], 'row', pairs)  6.65 us
    ppermute x3, waiting for transfers between devices, panels_everywhere(): lefts.append(lax.ppermute(left, 'col', pairs))  3.72 us
    ppermute x8, waiting for transfers between devices, right_step(): mine[h] = mine[h] + lax.ppermute(mine[h], 'row', pairs)  3.3 us
    pallas_call x1, Pallas kernels, product(): pl.pallas_call(product_kernel, out_shape=(jax.ShapeDtypeStruct((MB * TILE...  3.09 us
    unnamed x14, local copies, waits for them, and re-layouts  2.96 us
  transfers between devices with their start and end apart: 17, of which 4 were waited for; matrix products, arithmetic and copies ran while one was open for 2% of the time, Pallas kernels for 0%

profile of v2, /device:TPU:16, one launch (start us, length us, event | category | flops | bytes accessed | tf_op | source)
XLA Modules:
  0.0 98.9 jit_solution(13918354540937835542)
XLA Ops:
  0.8 0.7 copy-done.3
  1.4 1.2 %copy-done = bf16[1,1,2,16,128,128]{5,4,3,2,1,0:T(8,128)(2,1)S(1)} copy-done((bf16[1,1,2,16,128,128]{5,4,3,2,1,0:T(8,128)(2,1)S(1)}, bf16[1,1,2,16,128,128]{5,4,3,2,1,0:T(8,128)(2,1)}, u32[]{:S(2)}) %copy-start) | copy-done | bytes 1048600
  2.7 1.0 %copy-done.2 = bf16[1,1,16,128,128]{4,3,2,1,0:T(8,128)(2,1)S(1)} copy-done((bf16[1,1,16,128,128]{4,3,2,1,0:T(8,128)(2,1)S(1)}, bf16[1,1,16,128,128]{4,3,2,1,0:T(8,128)(2,1)}, u32[]{:S(2)}) %copy-start.2) | copy-done | bytes 524312
  3.7 0.7 shard_map.82
  4.4 0.7 collective-permute-start
  5.1 0.7 collective-permute-start.1
  5.8 0.7 collective-permute-start.2
  6.5 0.7 collective-permute-start.8
  7.2 0.7 collective-permute-start.12
  8.0 0.8 collective-permute-start.3
  8.9 0.7 collective-permute-start.9
  9.7 0.7 collective-permute-start.13
  10.5 1.3 %collective-permute-start.4 = (bf16[1040,128]{1,0:T(8,128)(2,1)S(1)}, bf16[1040,128]{1,0:T(8,128)(2,1)S(1)}, u32[]{:S(2)}, u32[]{:S(2)}) collective-permute-start(bf16[1040,128]{1,0:T(8,128)(2,1)S(1)} %add.42), channel_id=1, source_target_pairs={{12,8},{0,4},{268,256},{264,260},{13,9},{1,5},{269,257},{265,261},... | collective-permute-start | bytes 798728 | tf_op jit(solution)/shard_map/left_y/ppermute | solution.py:182
  11.9 0.7 collective-permute-start.10
  12.7 0.7 collective-permute-start.14
  13.4 27.0 %collective-permute-done.4 = bf16[1040,128]{1,0:T(8,128)(2,1)S(1)} collective-permute-done((bf16[1040,128]{1,0:T(8,128)(2,1)S(1)}, bf16[1040,128]{1,0:T(8,128)(2,1)S(1)}, u32[]{:S(2)}, u32[]{:S(2)}) %collective-permute-start.4) | collective-permute-done | bytes 266272 | tf_op jit(solution)/shard_map/left_y/ppermute | solution.py:182
  40.5 1.3 %collective-permute-start.11 = (bf16[1040,128]{1,0:T(8,128)(2,1)S(1)}, bf16[1040,128]{1,0:T(8,128)(2,1)S(1)}, u32[]{:S(2)}, u32[]{:S(2)}) collective-permute-start(bf16[1040,128]{1,0:T(8,128)(2,1)S(1)} %add.46), channel_id=1, source_target_pairs={{32,0},{48,16},{288,256},{304,272},{224,192},{240,208},{480,448},{... | collective-permute-start | bytes 798728 | tf_op jit(solution)/shard_map/right_step/ppermute | solution.py:167
  41.9 1.3 %collective-permute-start.15 = (bf16[1040,128]{1,0:T(8,128)(2,1)S(1)}, bf16[1040,128]{1,0:T(8,128)(2,1)S(1)}, u32[]{:S(2)}, u32[]{:S(2)}) collective-permute-start(bf16[1040,128]{1,0:T(8,128)(2,1)S(1)} %add.50), channel_id=1, source_target_pairs={{160,192},{176,208},{416,448},{432,464},{224,0},{240,16},{480,256}... | collective-permute-start | bytes 798728 | tf_op jit(solution)/shard_map/right_step/ppermute | solution.py:167
  43.3 0.1 reshape.165.mask_ref
  43.3 5.8 %collective-permute-start.7 = (bf16[1040,128]{1,0:T(8,128)(2,1)S(1)}, bf16[1040,128]{1,0:T(8,128)(2,1)S(1)}, u32[]{:S(2)}, u32[]{:S(2)}) collective-permute-start(bf16[1040,128]{1,0:T(8,128)(2,1)S(1)} %add.43.refs_0_), channel_id=1, source_target_pairs={{0,3},{1,0},{2,1},{3,2},{4,7},{5,4},{6,5},{7,6},{8,11},{9,8},{10,9... | collective-permute-start | bytes 798728 | tf_op jit(solution)/shard_map/left_x/ppermute | solution.py:189
  49.2 3.8 %collective-permute-start.6 = (bf16[1040,128]{1,0:T(8,128)(2,1)S(1)}, bf16[1040,128]{1,0:T(8,128)(2,1)S(1)}, u32[]{:S(2)}, u32[]{:S(2)}) collective-permute-start(bf16[1040,128]{1,0:T(8,128)(2,1)S(1)} %add.43.refs_0_), channel_id=1, source_target_pairs={{0,2},{1,3},{2,0},{3,1},{4,6},{5,7},{6,4},{7,5},{8,10},{9,11},{10,... | collective-permute-start | bytes 798728 | tf_op jit(solution)/shard_map/left_x/ppermute | solution.py:189
  53.0 3.3 %collective-permute-start.5 = (bf16[1040,128]{1,0:T(8,128)(2,1)S(1)}, bf16[1040,128]{1,0:T(8,128)(2,1)S(1)}, u32[]{:S(2)}, u32[]{:S(2)}) collective-permute-start(bf16[1040,128]{1,0:T(8,128)(2,1)S(1)} %add.43.refs_0_), channel_id=1, source_target_pairs={{0,1},{1,2},{2,3},{3,0},{4,5},{5,6},{6,7},{7,4},{8,9},{9,10},{10,1... | collective-permute-start | bytes 798728 | tf_op jit(solution)/shard_map/left_x/ppermute | solution.py:189
  56.4 3.3 %collective-permute-done.15 = bf16[1040,128]{1,0:T(8,128)(2,1)S(1)} collective-permute-done((bf16[1040,128]{1,0:T(8,128)(2,1)S(1)}, bf16[1040,128]{1,0:T(8,128)(2,1)S(1)}, u32[]{:S(2)}, u32[]{:S(2)}) %collective-permute-start.15) | collective-permute-done | bytes 266272 | tf_op jit(solution)/shard_map/right_step/ppermute | solution.py:167
  59.8 0.8 pad_maximum_fusion
  60.7 1.9 %collective-permute-start.16 = (bf16[2,1040,128]{2,1,0:T(8,128)(2,1)}, bf16[2,1040,128]{2,1,0:T(8,128)(2,1)S(1)}, u32[]{:S(2)}, u32[]{:S(2)}) collective-permute-start(bf16[2,1040,128]{2,1,0:T(8,128)(2,1)} %pad_maximum_fusion), channel_id=1, source_target_pairs={{0,16},{16,0},{32,48},{48,32},{64,80},{80,64},{96,112},{112,96},{1... | collective-permute-start | bytes 1597448 | tf_op jit(solution)/shard_map/right_core/ppermute | solution.py:192
  62.7 3.6 %collective-permute-done.5.refs_1_ = bf16[1040,128]{1,0:T(8,128)(2,1)S(1)} collective-permute-done((bf16[1040,128]{1,0:T(8,128)(2,1)S(1)}, bf16[1040,128]{1,0:T(8,128)(2,1)S(1)}, u32[]{:S(2)}, u32[]{:S(2)}) %collective-permute-start.5) | collective-permute-done | bytes 266272 | tf_op jit(solution)/shard_map/left_x/ppermute | solution.py:189
  66.3 0.1 reshape.167.slot_ref
  66.5 0.1 select_reduce_fusion
  66.6 3.1 %shard_map.84 = (f32[512,512]{1,0:T(8,128)S(1)}, f32[1,512]{1,0:T(1,128)S(1)}) custom-call(s32[32]{0:T(128)S(1)} %reshape.167.slot_ref, s32[256]{0:T(256)S(1)} %bitcast.40, s32[16]{0:T(128)S(1)} %reshape.165.mask_ref, bf16[1040,128]{1,0:T(8,128)(2,1)S(1)} %add.43.refs_0_, ...), custom_call_target="tpu_custom_call", output_to_operand_aliasing={{0}: (10, {})} | custom-call | tf_op jit(solution)/shard_map/pallas_call | solution.py:261
  69.7 6.2 %all_to_all.12 = f32[4,1,512]{2,1,0:T(1,128)S(1)} all-to-all(f32[4,1,512]{2,1,0:T(1,128)S(1)} %broadcast_in_dim.47), channel_id=1, replica_groups={{0,16,256,272},{32,48,288,304},{64,80,320,336},{96,112,352,368},{128,14..., dimensions={0} | all-to-all | bytes 16384 | tf_op jit(solution)/shard_map/all_to_all | solution.py:47
  75.9 21.8 %all_to_all.13 = f32[8,1,512]{2,1,0:T(1,128)S(1)} all-to-all(f32[8,1,512]{2,1,0:T(1,128)S(1)} %broadcast_in_dim.48), channel_id=1, replica_groups={{0,32,64,96,128,160,192,224},{16,48,80,112,144,176,208,240},{256,288,32..., dimensions={0} | all-to-all | bytes 32768 | tf_op jit(solution)/shard_map/all_to_all | solution.py:47
  97.8 1.1 %broadcast_multiply_fusion = f32[512,512]{1,0:T(8,128)} fusion(f32[512,512]{1,0:T(8,128)S(1)} %get-tuple-element.33, f32[512]{0:T(512)S(1)} %broadcast_divide_fusion), kind=kLoop, calls=%fused_computation.1 | loop fusion | flops 262144 | bytes 2099200 | tf_op jit(solution)/shard_map/mul | solution.py:284
  (52 shorter events, 1.3 us)
Async XLA Ops:
  0.0 0.7 copy-start.6
  0.8 0.7 copy-start.3
  0.8 0.7 copy-start.4
  1.4 1.2 %copy-start = (bf16[1,1,2,16,128,128]{5,4,3,2,1,0:T(8,128)(2,1)S(1)}, bf16[1,1,2,16,128,128]{5,4,3,2,1,0:T(8,128)(2,1)}, u32[]{:S(2)}) copy-start(bf16[1,1,2,16,128,128]{5,4,3,2,1,0:T(8,128)(2,1)} %param.8) | copy-start | bytes 3145732
  2.7 1.0 %copy-start.2 = (bf16[1,1,16,128,128]{4,3,2,1,0:T(8,128)(2,1)S(1)}, bf16[1,1,16,128,128]{4,3,2,1,0:T(8,128)(2,1)}, u32[]{:S(2)}) copy-start(bf16[1,1,16,128,128]{4,3,2,1,0:T(8,128)(2,1)} %param.11) | copy-start | bytes 1572868
  4.4 3.4 %collective-permute-start = (bf16[1040,128]{1,0:T(8,128)(2,1)S(1)}, bf16[1040,128]{1,0:T(8,128)(2,1)S(1)}, u32[]{:S(2)}, u32[]{:S(2)}) collective-permute-start(bf16[1040,128]{1,0:T(8,128)(2,1)S(1)} %get-tuple-element.21), channel_id=1, source_target_pairs={{15,13},{31,29},{47,45},{63,61},{79,77},{95,93},{111,109},{127,125... | collective-permute-start | bytes 798728 | tf_op jit(solution)/shard_map/left_scatter/ppermute | solution.py:161
  5.1 2.8 %collective-permute-start.1 = (bf16[1040,128]{1,0:T(8,128)(2,1)S(1)}, bf16[1040,128]{1,0:T(8,128)(2,1)S(1)}, u32[]{:S(2)}, u32[]{:S(2)}) collective-permute-start(bf16[1040,128]{1,0:T(8,128)(2,1)S(1)} %get-tuple-element.22), channel_id=1, source_target_pairs={{15,12},{31,28},{47,44},{63,60},{79,76},{95,92},{111,108},{127,124... | collective-permute-start | bytes 798728 | tf_op jit(solution)/shard_map/left_scatter/ppermute | solution.py:161
  5.8 2.1 %collective-permute-start.2 = (bf16[1040,128]{1,0:T(8,128)(2,1)S(1)}, bf16[1040,128]{1,0:T(8,128)(2,1)S(1)}, u32[]{:S(2)}, u32[]{:S(2)}) collective-permute-start(bf16[1040,128]{1,0:T(8,128)(2,1)S(1)} %get-tuple-element.23), channel_id=1, source_target_pairs={{15,14},{31,30},{47,46},{63,62},{79,78},{95,94},{111,110},{127,126... | collective-permute-start | bytes 798728 | tf_op jit(solution)/shard_map/left_scatter/ppermute | solution.py:161
  6.5 2.3 %collective-permute-start.8 = (bf16[1040,128]{1,0:T(8,128)(2,1)S(1)}, bf16[1040,128]{1,0:T(8,128)(2,1)S(1)}, u32[]{:S(2)}, u32[]{:S(2)}) collective-permute-start(bf16[1040,128]{1,0:T(8,128)(2,1)S(1)} %get-tuple-element.24), channel_id=1, source_target_pairs={{480,224},{496,240},{481,225},{497,241},{482,226},{498,242},{483,2... | collective-permute-start | bytes 798728 | tf_op jit(solution)/shard_map/right_step/ppermute | solution.py:167
  7.2 2.4 %collective-permute-start.12 = (bf16[1040,128]{1,0:T(8,128)(2,1)S(1)}, bf16[1040,128]{1,0:T(8,128)(2,1)S(1)}, u32[]{:S(2)}, u32[]{:S(2)}) collective-permute-start(bf16[1040,128]{1,0:T(8,128)(2,1)S(1)} %get-tuple-element.29), channel_id=1, source_target_pairs={{480,224},{496,240},{481,225},{497,241},{482,226},{498,242},{483,2... | collective-permute-start | bytes 798728 | tf_op jit(solution)/shard_map/right_step/ppermute | solution.py:167
  8.0 2.4 %copy-start.1 = (f32[512,512]{1,0:T(8,128)S(1)}, f32[512,512]{1,0:T(8,128)}, u32[]{:S(2)}) copy-start(f32[512,512]{1,0:T(8,128)} %c_ref) | copy-start | bytes 3145732
  8.0 2.5 %collective-permute-start.3 = (bf16[1040,128]{1,0:T(8,128)(2,1)S(1)}, bf16[1040,128]{1,0:T(8,128)(2,1)S(1)}, u32[]{:S(2)}, u32[]{:S(2)}) collective-permute-start(bf16[1040,128]{1,0:T(8,128)(2,1)S(1)} %add_add_fusion), channel_id=1, source_target_pairs={{12,0},{268,264},{13,1},{269,265},{14,2},{270,266},{15,3},{271,267... | collective-permute-start | bytes 798728 | tf_op jit(solution)/shard_map/left_y/ppermute | solution.py:177
  8.9 2.9 %collective-permute-start.9 = (bf16[1040,128]{1,0:T(8,128)(2,1)S(1)}, bf16[1040,128]{1,0:T(8,128)(2,1)S(1)}, u32[]{:S(2)}, u32[]{:S(2)}) collective-permute-start(bf16[1040,128]{1,0:T(8,128)(2,1)S(1)} %add.44), channel_id=1, source_target_pairs={{224,64},{240,80},{480,320},{496,336},{225,65},{241,81},{481,321},... | collective-permute-start | bytes 798728 | tf_op jit(solution)/shard_map/right_step/ppermute | solution.py:167
  9.7 2.9 %collective-permute-start.13 = (bf16[1040,128]{1,0:T(8,128)(2,1)S(1)}, bf16[1040,128]{1,0:T(8,128)(2,1)S(1)}, u32[]{:S(2)}, u32[]{:S(2)}) collective-permute-start(bf16[1040,128]{1,0:T(8,128)(2,1)S(1)} %add.48), channel_id=1, source_target_pairs={{224,128},{240,144},{480,384},{496,400},{225,129},{241,145},{481,3... | collective-permute-start | bytes 798728 | tf_op jit(solution)/shard_map/right_step/ppermute | solution.py:167
  10.5 29.8 %collective-permute-start.4 = (bf16[1040,128]{1,0:T(8,128)(2,1)S(1)}, bf16[1040,128]{1,0:T(8,128)(2,1)S(1)}, u32[]{:S(2)}, u32[]{:S(2)}) collective-permute-start(bf16[1040,128]{1,0:T(8,128)(2,1)S(1)} %add.42), channel_id=1, source_target_pairs={{12,8},{0,4},{268,256},{264,260},{13,9},{1,5},{269,257},{265,261},... | collective-permute-start | bytes 798728 | tf_op jit(solution)/shard_map/left_y/ppermute | solution.py:182
  11.9 28.5 %collective-permute-start.10 = (bf16[1040,128]{1,0:T(8,128)(2,1)S(1)}, bf16[1040,128]{1,0:T(8,128)(2,1)S(1)}, u32[]{:S(2)}, u32[]{:S(2)}) collective-permute-start(bf16[1040,128]{1,0:T(8,128)(2,1)S(1)} %add.45), channel_id=1, source_target_pairs={{224,32},{240,48},{480,288},{496,304},{64,128},{80,144},{320,384},... | collective-permute-start | bytes 798728 | tf_op jit(solution)/shard_map/right_step/ppermute | solution.py:167
  12.7 29.1 %collective-permute-start.14 = (bf16[1040,128]{1,0:T(8,128)(2,1)S(1)}, bf16[1040,128]{1,0:T(8,128)(2,1)S(1)}, u32[]{:S(2)}, u32[]{:S(2)}) collective-permute-start(bf16[1040,128]{1,0:T(8,128)(2,1)S(1)} %add.49), channel_id=1, source_target_pairs={{224,160},{240,176},{480,416},{496,432},{128,64},{144,80},{384,320... | collective-permute-start | bytes 798728 | tf_op jit(solution)/shard_map/right_step/ppermute | solution.py:167
  40.5 2.7 %copy-start.5 = (s32[4,4]{1,0:T(4,128)S(1)}, s32[4,4]{1,0:T(4,128)}, u32[]{:S(2)}) copy-start(s32[4,4]{1,0:T(4,128)} %param.15) | copy-start | bytes 196
  40.5 15.8 %collective-permute-start.11 = (bf16[1040,128]{1,0:T(8,128)(2,1)S(1)}, bf16[1040,128]{1,0:T(8,128)(2,1)S(1)}, u32[]{:S(2)}, u32[]{:S(2)}) collective-permute-start(bf16[1040,128]{1,0:T(8,128)(2,1)S(1)} %add.46), channel_id=1, source_target_pairs={{32,0},{48,16},{288,256},{304,272},{224,192},{240,208},{480,448},{... | collective-permute-start | bytes 798728 | tf_op jit(solution)/shard_map/right_step/ppermute | solution.py:167
  41.9 17.8 %collective-permute-start.15 = (bf16[1040,128]{1,0:T(8,128)(2,1)S(1)}, bf16[1040,128]{1,0:T(8,128)(2,1)S(1)}, u32[]{:S(2)}, u32[]{:S(2)}) collective-permute-start(bf16[1040,128]{1,0:T(8,128)(2,1)S(1)} %add.50), channel_id=1, source_target_pairs={{160,192},{176,208},{416,448},{432,464},{224,0},{240,16},{480,256}... | collective-permute-start | bytes 798728 | tf_op jit(solution)/shard_map/right_step/ppermute | solution.py:167
  43.3 17.4 %collective-permute-start.7 = (bf16[1040,128]{1,0:T(8,128)(2,1)S(1)}, bf16[1040,128]{1,0:T(8,128)(2,1)S(1)}, u32[]{:S(2)}, u32[]{:S(2)}) collective-permute-start(bf16[1040,128]{1,0:T(8,128)(2,1)S(1)} %add.43.refs_0_), channel_id=1, source_target_pairs={{0,3},{1,0},{2,1},{3,2},{4,7},{5,4},{6,5},{7,6},{8,11},{9,8},{10,9... | collective-permute-start | bytes 798728 | tf_op jit(solution)/shard_map/left_x/ppermute | solution.py:189
  49.2 13.5 %collective-permute-start.6 = (bf16[1040,128]{1,0:T(8,128)(2,1)S(1)}, bf16[1040,128]{1,0:T(8,128)(2,1)S(1)}, u32[]{:S(2)}, u32[]{:S(2)}) collective-permute-start(bf16[1040,128]{1,0:T(8,128)(2,1)S(1)} %add.43.refs_0_), channel_id=1, source_target_pairs={{0,2},{1,3},{2,0},{3,1},{4,6},{5,7},{6,4},{7,5},{8,10},{9,11},{10,... | collective-permute-start | bytes 798728 | tf_op jit(solution)/shard_map/left_x/ppermute | solution.py:189
  53.0 13.3 %collective-permute-start.5 = (bf16[1040,128]{1,0:T(8,128)(2,1)S(1)}, bf16[1040,128]{1,0:T(8,128)(2,1)S(1)}, u32[]{:S(2)}, u32[]{:S(2)}) collective-permute-start(bf16[1040,128]{1,0:T(8,128)(2,1)S(1)} %add.43.refs_0_), channel_id=1, source_target_pairs={{0,1},{1,2},{2,3},{3,0},{4,5},{5,6},{6,7},{7,4},{8,9},{9,10},{10,1... | collective-permute-start | bytes 798728 | tf_op jit(solution)/shard_map/left_x/ppermute | solution.py:189
  60.7 5.7 %collective-permute-start.16 = (bf16[2,1040,128]{2,1,0:T(8,128)(2,1)}, bf16[2,1040,128]{2,1,0:T(8,128)(2,1)S(1)}, u32[]{:S(2)}, u32[]{:S(2)}) collective-permute-start(bf16[2,1040,128]{2,1,0:T(8,128)(2,1)} %pad_maximum_fusion), channel_id=1, source_target_pairs={{0,16},{16,0},{32,48},{48,32},{64,80},{80,64},{96,112},{112,96},{1... | collective-permute-start | bytes 1597448 | tf_op jit(solution)/shard_map/right_core/ppermute | solution.py:192

commit v3 on v2

--- a/solution.py
+++ b/solution.py
@@ -64,7 +64,8 @@
 
 
 def messages_kernel(a_index_ref, a_count_ref, b_index_ref, b_count_ref, a_ref, b_ref, *refs):
-    quarter_refs, left_ref, half_refs, sems = refs[: X - 1], refs[X - 1], refs[X : X + HALVES], refs[-1]
+    *quarter_refs, left_ref, right_ref, sems = refs
+    half_refs = [right_ref.at[h] for h in range(HALVES)]
     row, col = lax.axis_index("row"), lax.axis_index("col")
     own, root = col == N_COL - 1, row >= N_ROW - CORE
     lane = lax.broadcasted_iota(jnp.int32, (PAD, TILE), 1)
@@ -118,8 +119,7 @@
 
     @pl.when(jnp.logical_not(root))
     def _():
-        for ref in half_refs:
-            ref[...] = jnp.zeros_like(ref)
+        right_ref[...] = jnp.zeros_like(right_ref)
 
 
 def messages(a_tiles, a_index, a_count, b_tiles, b_index, b_count):
@@ -128,26 +128,34 @@
     hbm = pl.BlockSpec(memory_space=pltpu.HBM)
     return pl.pallas_call(
         messages_kernel,
-        out_shape=[jax.ShapeDtypeStruct((LQ * TILE + PAD, TILE), jnp.bfloat16)] * (X + HALVES),
+        out_shape=[jax.ShapeDtypeStruct((LQ * TILE + PAD, TILE), jnp.bfloat16)] * X
+        + [jax.ShapeDtypeStruct((HALVES, RH * TILE + PAD, TILE), jnp.bfloat16)],
         in_specs=[smem] * 4 + [hbm] * 2,
-        out_specs=[vmem] * (X + HALVES),
+        out_specs=[vmem] * (X + 1),
         scratch_shapes=[pltpu.SemaphoreType.DMA((X + HALVES,))],
         compiler_params=pltpu.CompilerParams(vmem_limit_bytes=4 * 1024 * 1024),
     )(a_index, a_count, b_index, b_count, a_tiles, b_tiles)
 
 
 def right_steps(h):
-    def at(place):
-        return (Z - 1 + (place if h == 0 else -place)) % Z
-
-    along = ([(0, 3)], [(0, 2), (3, 5)], [(2, 1), (0, 7), (3, 4), (5, 6)])
-    return [[((1, Z - 1), (0, Z - 1))]] + [[((y, at(a)), (y, at(b))) for a, b in step for y in range(Y_LO)] for step in along]
+    def pairs(*moves):
+        def at(y, place):
+            return y, (Z - 1 + (place if h == 0 else -place)) % Z
+
+        return [(at(y, a), at(to, b)) for y, a, to, b in moves]
+
+    both = [(y, a, y, b) for a, b in ((2, 1), (0, 7), (3, 4), (5, 6)) for y in range(Y_LO)]
+    return [
+        [pairs((1, 0, 1, 3))],
+        [pairs((1, 0, 1, 2), (1, 3, 1, 5), (0, 0, 0, 2)), pairs((1, 3, 0, 3), (0, 0, 0, 5))],
+        [pairs(*both)],
+    ]
 
 
 def panels_everywhere(a_tiles, a_index, a_count, b_tiles, b_index, b_count, c_partial):
     both = ("row", "col")
     first, second = y_pairs()
-    *quarters, left, half0, half1 = messages(
+    *quarters, left, right = messages(
         a_tiles.reshape(SECTIONS * KA * TILE, TILE),
         a_index.reshape(-1),
         a_count.reshape(-1),
@@ -155,39 +163,35 @@
         b_index.reshape(-1),
         b_count.reshape(-1),
     )
-    mine = [half0, half1]
     for q in (1, 0, 2):
         with jax.named_scope("left_scatter"):
             left = left + lax.ppermute(quarters[q], "col", [(col_of(Y_HI - 1, X - 1), col_of(Y_HI - 1, q))])
 
-    def right_step(i):
-        for h in range(HALVES):
-            with jax.named_scope("right_step"):
-                pairs = [(row_of(*a, c), row_of(*b, c)) for a, b in right_steps(h)[i] for c in range(CORE)]
-                mine[h] = mine[h] + lax.ppermute(mine[h], "row", pairs)
-
-    def right_after(*arrays):
-        for h in range(HALVES):
-            mine[h] = after(mine[h], *arrays)
-
-    right_step(0)
+    def right_send(array, pairs):
+        with jax.named_scope("right_step"):
+            return lax.ppermute(array, "row", [(row_of(*a, c), row_of(*b, c)) for a, b in pairs for c in range(CORE)])
+
+    def right_step(array, ops):
+        return sum([right_send(array, pairs) for pairs in ops], array)
+
+    along = [right_send(right[h], right_steps(h)[0][0]) for h in range(HALVES)]
+    right = right_step(right, [[((1, Z - 1), (0, Z - 1))]])
+    mine = [after(right[h] + along[h], left) for h in range(HALVES)]
     c_partial = after(c_partial, left)
-    right_after(left)
     with jax.named_scope("left_y"):
         left = left + lax.ppermute(left, both, first)
-    right_step(1)
+    mine = [right_step(mine[h], right_steps(h)[1]) for h in range(HALVES)]
     held = hold(c_partial)
-    right_after(left, held)
+    mine = [after(half, left, held) for half in mine]
     with jax.named_scope("left_y"):
         left = left + lax.ppermute(left, both, second)
-    right_step(2)
-    right_after(left)
+    mine = [right_step(mine[h], right_steps(h)[2]) for h in range(HALVES)]
+    mine = [after(half, left) for half in mine]
     lefts = [left]
     for d in range(1, X):
         with jax.named_scope("left_x"):
             pairs = [(col_of(y, x_), col_of(y, (x_ + d) % X)) for y in range(Y_HI) for x_ in range(X)]
             lefts.append(lax.ppermute(left, "col", pairs))
-    right_step(3)
     with jax.named_scope("right_core"):
         other = lax.ppermute(jnp.stack(mine), "row", [(r, r ^ 1) for r in range(N_ROW)])
     return lefts, [*mine, other], held

time: 99.5 us -> 98.1 us (0.986)
  waiting for transfers between devices: 34 us -> 30.3 us
  blocking collectives: 28 us -> 30.1 us
    ppermute x1, waiting for transfers between devices: 27 us -> 23.3 us  [panels_everywhere(): left = left + lax.ppermute(left, both, second)]
    ppermute x8 -> x9, waiting for transfers between devices: 3.3 us -> 0.02 us  [right_send(): lax.ppermute(array, 'row', [(row_of(*a, c), row_of(*b, c)) for a, b in pa...]
    ppermute x3, waiting for transfers between devices: 3.72 us -> 6.99 us  [panels_everywhere(): lefts.append(lax.ppermute(left, 'col', pairs))]
    all_to_all x2, blocking collectives: 28 us -> 30.1 us  [gather(): lax.all_to_all(jnp.broadcast_to(array, (n,) + array.shape), axis, 0, 0, a...]
    ppermute x8 -> x9, starting transfers between devices: 6.65 us -> 7.47 us  [right_send(): lax.ppermute(array, 'row', [(row_of(*a, c), row_of(*b, c)) for a, b in pa...]
  transfers between devices with their start and end apart: 17 -> 18, of which waited for: 4 -> 3; matrix products, arithmetic and copies ran while one was open for 2% -> 2% of each run, Pallas kernels for 0% -> 0%
where the time goes in v3:
time: 98.1 us; the launch traced here: 97.5 us
  waiting for transfers between devices  30.3 us (31%)
  blocking collectives  30.1 us (31%)
  starting transfers between devices  26.4 us (27%)
  Pallas kernels  3.41 us (3%)
  local copies, waits for them, and re-layouts  3.37 us (3%)
  other arithmetic  2.85 us (3%)
  between operations  1.07 us (1%)
    all_to_all x2, blocking collectives, gather(): lax.all_to_all(jnp.broadcast_to(array, (n,) + array.shape), axis, 0, 0, a...  30.1 us
    ppermute x1, waiting for transfers between devices, panels_everywhere(): left = left + lax.ppermute(left, both, second)  23.3 us
    ppermute x3, starting transfers between devices, panels_everywhere(): lefts.append(lax.ppermute(left, 'col', pairs))  13 us
    ppermute x9, starting transfers between devices, right_send(): lax.ppermute(array, 'row', [(row_of(*a, c), row_of(*b, c)) for a, b in pa...  7.47 us
    ppermute x3, waiting for transfers between devices, panels_everywhere(): lefts.append(lax.ppermute(left, 'col', pairs))  6.99 us
    unnamed x14, local copies, waits for them, and re-layouts  2.96 us
    pallas_call x1, Pallas kernels, product(): pl.pallas_call(product_kernel, out_shape=(jax.ShapeDtypeStruct((MB * TILE...  2.62 us
    ppermute x3, starting transfers between devices, panels_everywhere(): lax.ppermute(quarters[q], 'col', [(col_of(Y_HI - 1, X - 1), col_of(Y_HI -...  2.03 us
  transfers between devices with their start and end apart: 18, of which 3 were waited for; matrix products, arithmetic and copies ran while one was open for 2% of the time, Pallas kernels for 0%

profile of v3, /device:TPU:16, one launch (start us, length us, event | category | flops | bytes accessed | tf_op | source)
XLA Modules:
  0.0 97.5 jit_solution(9907543116858497720)
XLA Ops:
  0.8 0.7 copy-done.3
  1.4 1.2 %copy-done = bf16[1,1,2,16,128,128]{5,4,3,2,1,0:T(8,128)(2,1)S(1)} copy-done((bf16[1,1,2,16,128,128]{5,4,3,2,1,0:T(8,128)(2,1)S(1)}, bf16[1,1,2,16,128,128]{5,4,3,2,1,0:T(8,128)(2,1)}, u32[]{:S(2)}) %copy-start) | copy-done | bytes 1048600
  2.7 1.0 %copy-done.2 = bf16[1,1,16,128,128]{4,3,2,1,0:T(8,128)(2,1)S(1)} copy-done((bf16[1,1,16,128,128]{4,3,2,1,0:T(8,128)(2,1)S(1)}, bf16[1,1,16,128,128]{4,3,2,1,0:T(8,128)(2,1)}, u32[]{:S(2)}) %copy-start.2) | copy-done | bytes 524312
  3.7 0.7 shard_map.82
  4.4 0.7 collective-permute-start
  5.1 0.7 collective-permute-start.1
  5.8 0.7 collective-permute-start.2
  6.5 0.7 collective-permute-start.8
  7.2 0.7 collective-permute-start.9
  7.9 0.7 collective-permute-start.13
  8.7 0.7 collective-permute-start.3
  9.4 0.1 add.47
  9.6 0.1 fusion.1
  9.7 0.8 collective-permute-start.11
  10.5 0.7 collective-permute-start.10
  11.3 0.7 collective-permute-start.15
  12.0 0.7 collective-permute-start.14
  12.8 1.3 %collective-permute-start.4 = (bf16[1040,128]{1,0:T(8,128)(2,1)S(1)}, bf16[1040,128]{1,0:T(8,128)(2,1)S(1)}, u32[]{:S(2)}, u32[]{:S(2)}) collective-permute-start(bf16[1040,128]{1,0:T(8,128)(2,1)S(1)} %add.45), channel_id=1, source_target_pairs={{12,8},{0,4},{268,256},{264,260},{13,9},{1,5},{269,257},{265,261},... | collective-permute-start | bytes 798728 | tf_op jit(solution)/shard_map/left_y/ppermute | solution.py:187
  14.1 1.3 %collective-permute-start.12 = (bf16[1040,128]{1,0:T(8,128)(2,1)S(1)}, bf16[1040,128]{1,0:T(8,128)(2,1)S(1)}, u32[]{:S(2)}, u32[]{:S(2)}) collective-permute-start(bf16[1040,128]{1,0:T(8,128)(2,1)S(1)} %add_add_fusion.1), channel_id=1, source_target_pairs={{32,0},{48,16},{288,256},{304,272},{224,192},{240,208},{480,448},{... | collective-permute-start | bytes 798728 | tf_op jit(solution)/shard_map/right_step/ppermute | solution.py:172
  15.5 1.3 %collective-permute-start.16 = (bf16[1040,128]{1,0:T(8,128)(2,1)S(1)}, bf16[1040,128]{1,0:T(8,128)(2,1)S(1)}, u32[]{:S(2)}, u32[]{:S(2)}) collective-permute-start(bf16[1040,128]{1,0:T(8,128)(2,1)S(1)} %add_add_fusion), channel_id=1, source_target_pairs={{160,192},{176,208},{416,448},{432,464},{224,0},{240,16},{480,256}... | collective-permute-start | bytes 798728 | tf_op jit(solution)/shard_map/right_step/ppermute | solution.py:172
  16.9 23.3 %collective-permute-done.4 = bf16[1040,128]{1,0:T(8,128)(2,1)S(1)} collective-permute-done((bf16[1040,128]{1,0:T(8,128)(2,1)S(1)}, bf16[1040,128]{1,0:T(8,128)(2,1)S(1)}, u32[]{:S(2)}, u32[]{:S(2)}) %collective-permute-start.4) | collective-permute-done | bytes 266272 | tf_op jit(solution)/shard_map/left_y/ppermute | solution.py:187
  40.3 5.8 %collective-permute-start.7 = (bf16[1040,128]{1,0:T(8,128)(2,1)S(1)}, bf16[1040,128]{1,0:T(8,128)(2,1)S(1)}, u32[]{:S(2)}, u32[]{:S(2)}) collective-permute-start(bf16[1040,128]{1,0:T(8,128)(2,1)S(1)} %add.46.refs_0_), channel_id=1, source_target_pairs={{0,3},{1,0},{2,1},{3,2},{4,7},{5,4},{6,5},{7,6},{8,11},{9,8},{10,9... | collective-permute-start | bytes 798728 | tf_op jit(solution)/shard_map/left_x/ppermute | solution.py:194
  46.1 3.8 %collective-permute-start.6 = (bf16[1040,128]{1,0:T(8,128)(2,1)S(1)}, bf16[1040,128]{1,0:T(8,128)(2,1)S(1)}, u32[]{:S(2)}, u32[]{:S(2)}) collective-permute-start(bf16[1040,128]{1,0:T(8,128)(2,1)S(1)} %add.46.refs_0_), channel_id=1, source_target_pairs={{0,2},{1,3},{2,0},{3,1},{4,6},{5,7},{6,4},{7,5},{8,10},{9,11},{10,... | collective-permute-start | bytes 798728 | tf_op jit(solution)/shard_map/left_x/ppermute | solution.py:194
  50.0 3.3 %collective-permute-start.5 = (bf16[1040,128]{1,0:T(8,128)(2,1)S(1)}, bf16[1040,128]{1,0:T(8,128)(2,1)S(1)}, u32[]{:S(2)}, u32[]{:S(2)}) collective-permute-start(bf16[1040,128]{1,0:T(8,128)(2,1)S(1)} %add.46.refs_0_), channel_id=1, source_target_pairs={{0,1},{1,2},{2,3},{3,0},{4,5},{5,6},{6,7},{7,4},{8,9},{9,10},{10,1... | collective-permute-start | bytes 798728 | tf_op jit(solution)/shard_map/left_x/ppermute | solution.py:194
  53.5 0.8 pad_maximum_fusion
  54.4 3.3 %collective-permute-done.7.refs_3_ = bf16[1040,128]{1,0:T(8,128)(2,1)S(1)} collective-permute-done((bf16[1040,128]{1,0:T(8,128)(2,1)S(1)}, bf16[1040,128]{1,0:T(8,128)(2,1)S(1)}, u32[]{:S(2)}, u32[]{:S(2)}) %collective-permute-start.7) | collective-permute-done | bytes 266272 | tf_op jit(solution)/shard_map/left_x/ppermute | solution.py:194
  57.7 1.9 %collective-permute-start.17 = (bf16[2,1040,128]{2,1,0:T(8,128)(2,1)}, bf16[2,1040,128]{2,1,0:T(8,128)(2,1)S(1)}, u32[]{:S(2)}, u32[]{:S(2)}) collective-permute-start(bf16[2,1040,128]{2,1,0:T(8,128)(2,1)} %pad_maximum_fusion), channel_id=1, source_target_pairs={{0,16},{16,0},{32,48},{48,32},{64,80},{80,64},{96,112},{112,96},{1... | collective-permute-start | bytes 1597448 | tf_op jit(solution)/shard_map/right_core/ppermute | solution.py:196
  59.6 3.6 %collective-permute-done.5.refs_1_ = bf16[1040,128]{1,0:T(8,128)(2,1)S(1)} collective-permute-done((bf16[1040,128]{1,0:T(8,128)(2,1)S(1)}, bf16[1040,128]{1,0:T(8,128)(2,1)S(1)}, u32[]{:S(2)}, u32[]{:S(2)}) %collective-permute-start.5) | collective-permute-done | bytes 266272 | tf_op jit(solution)/shard_map/left_x/ppermute | solution.py:194
  63.6 2.6 %shard_map.84 = (f32[512,512]{1,0:T(8,128)S(1)}, f32[1,512]{1,0:T(1,128)S(1)}) custom-call(s32[32]{0:T(128)S(1)} %reshape.167.slot_ref, s32[256]{0:T(256)S(1)} %bitcast.52, s32[16]{0:T(128)S(1)} %reshape.165.mask_ref, bf16[1040,128]{1,0:T(8,128)(2,1)S(1)} %add.46.refs_0_, ...), custom_call_target="tpu_custom_call", output_to_operand_aliasing={{0}: (10, {})} | custom-call | tf_op jit(solution)/shard_map/pallas_call | solution.py:265
  66.2 6.2 %all_to_all.12 = f32[4,1,512]{2,1,0:T(1,128)S(1)} all-to-all(f32[4,1,512]{2,1,0:T(1,128)S(1)} %broadcast_in_dim.47), channel_id=1, replica_groups={{0,16,256,272},{32,48,288,304},{64,80,320,336},{96,112,352,368},{128,14..., dimensions={0} | all-to-all | bytes 16384 | tf_op jit(solution)/shard_map/all_to_all | solution.py:47
  72.4 23.9 %all_to_all.13 = f32[8,1,512]{2,1,0:T(1,128)S(1)} all-to-all(f32[8,1,512]{2,1,0:T(1,128)S(1)} %broadcast_in_dim.48), channel_id=1, replica_groups={{0,32,64,96,128,160,192,224},{16,48,80,112,144,176,208,240},{256,288,32..., dimensions={0} | all-to-all | bytes 32768 | tf_op jit(solution)/shard_map/all_to_all | solution.py:47
  96.4 1.1 %broadcast_multiply_fusion = f32[512,512]{1,0:T(8,128)} fusion(f32[512,512]{1,0:T(8,128)S(1)} %get-tuple-element.31, f32[512]{0:T(512)S(1)} %broadcast_divide_fusion), kind=kLoop, calls=%fused_computation.1 | loop fusion | flops 262144 | bytes 2099200 | tf_op jit(solution)/shard_map/mul | solution.py:288
  (53 shorter events, 1.2 us)
Async XLA Ops:
  0.0 0.7 copy-start.6
  0.8 0.7 copy-start.3
  0.8 0.7 copy-start.4
  1.4 1.2 %copy-start = (bf16[1,1,2,16,128,128]{5,4,3,2,1,0:T(8,128)(2,1)S(1)}, bf16[1,1,2,16,128,128]{5,4,3,2,1,0:T(8,128)(2,1)}, u32[]{:S(2)}) copy-start(bf16[1,1,2,16,128,128]{5,4,3,2,1,0:T(8,128)(2,1)} %param.8) | copy-start | bytes 3145732
  2.7 1.0 %copy-start.2 = (bf16[1,1,16,128,128]{4,3,2,1,0:T(8,128)(2,1)S(1)}, bf16[1,1,16,128,128]{4,3,2,1,0:T(8,128)(2,1)}, u32[]{:S(2)}) copy-start(bf16[1,1,16,128,128]{4,3,2,1,0:T(8,128)(2,1)} %param.11) | copy-start | bytes 1572868
  4.4 3.5 %collective-permute-start = (bf16[1040,128]{1,0:T(8,128)(2,1)S(1)}, bf16[1040,128]{1,0:T(8,128)(2,1)S(1)}, u32[]{:S(2)}, u32[]{:S(2)}) collective-permute-start(bf16[1040,128]{1,0:T(8,128)(2,1)S(1)} %get-tuple-element.20), channel_id=1, source_target_pairs={{15,13},{31,29},{47,45},{63,61},{79,77},{95,93},{111,109},{127,125... | collective-permute-start | bytes 798728 | tf_op jit(solution)/shard_map/left_scatter/ppermute | solution.py:168
  5.1 3.5 %collective-permute-start.1 = (bf16[1040,128]{1,0:T(8,128)(2,1)S(1)}, bf16[1040,128]{1,0:T(8,128)(2,1)S(1)}, u32[]{:S(2)}, u32[]{:S(2)}) collective-permute-start(bf16[1040,128]{1,0:T(8,128)(2,1)S(1)} %get-tuple-element.21), channel_id=1, source_target_pairs={{15,12},{31,28},{47,44},{63,60},{79,76},{95,92},{111,108},{127,124... | collective-permute-start | bytes 798728 | tf_op jit(solution)/shard_map/left_scatter/ppermute | solution.py:168
  5.8 2.8 %collective-permute-start.2 = (bf16[1040,128]{1,0:T(8,128)(2,1)S(1)}, bf16[1040,128]{1,0:T(8,128)(2,1)S(1)}, u32[]{:S(2)}, u32[]{:S(2)}) collective-permute-start(bf16[1040,128]{1,0:T(8,128)(2,1)S(1)} %get-tuple-element.22), channel_id=1, source_target_pairs={{15,14},{31,30},{47,46},{63,62},{79,78},{95,94},{111,110},{127,126... | collective-permute-start | bytes 798728 | tf_op jit(solution)/shard_map/left_scatter/ppermute | solution.py:168
  6.5 2.9 %collective-permute-start.8 = (bf16[2,1040,128]{2,1,0:T(8,128)(2,1)S(1)}, bf16[2,1040,128]{2,1,0:T(8,128)(2,1)S(1)}, u32[]{:S(2)}, u32[]{:S(2)}) collective-permute-start(bf16[2,1040,128]{2,1,0:T(8,128)(2,1)S(1)} %get-tuple-element.23), channel_id=1, source_target_pairs={{480,224},{496,240},{481,225},{497,241},{482,226},{498,242},{483,2... | collective-permute-start | bytes 1597448 | tf_op jit(solution)/shard_map/right_step/ppermute | solution.py:172
  7.2 2.3 %collective-permute-start.9 = (bf16[1040,128]{1,0:T(8,128)(2,1)S(1)}, bf16[1040,128]{1,0:T(8,128)(2,1)S(1)}, u32[]{:S(2)}, u32[]{:S(2)}) collective-permute-start(bf16[1040,128]{1,0:T(8,128)(2,1)S(1)} %get-tuple-element.37), channel_id=1, source_target_pairs={{480,320},{496,336},{481,321},{497,337},{482,322},{498,338},{483,3... | collective-permute-start | bytes 798728 | tf_op jit(solution)/shard_map/right_step/ppermute | solution.py:172
  7.9 1.7 %collective-permute-start.13 = (bf16[1040,128]{1,0:T(8,128)(2,1)S(1)}, bf16[1040,128]{1,0:T(8,128)(2,1)S(1)}, u32[]{:S(2)}, u32[]{:S(2)}) collective-permute-start(bf16[1040,128]{1,0:T(8,128)(2,1)S(1)} %get-tuple-element.38), channel_id=1, source_target_pairs={{480,384},{496,400},{481,385},{497,401},{482,386},{498,402},{483,3... | collective-permute-start | bytes 798728 | tf_op jit(solution)/shard_map/right_step/ppermute | solution.py:172
  8.7 3.9 %collective-permute-start.3 = (bf16[1040,128]{1,0:T(8,128)(2,1)S(1)}, bf16[1040,128]{1,0:T(8,128)(2,1)S(1)}, u32[]{:S(2)}, u32[]{:S(2)}) collective-permute-start(bf16[1040,128]{1,0:T(8,128)(2,1)S(1)} %add_add_fusion.2), channel_id=1, source_target_pairs={{12,0},{268,264},{13,1},{269,265},{14,2},{270,266},{15,3},{271,267... | collective-permute-start | bytes 798728 | tf_op jit(solution)/shard_map/left_y/ppermute | solution.py:182
  9.6 1.6 %copy-start.1 = (f32[512,512]{1,0:T(8,128)S(1)}, f32[512,512]{1,0:T(8,128)}, u32[]{:S(2)}) copy-start(f32[512,512]{1,0:T(8,128)} %c_ref) | copy-start | bytes 3145732
  9.7 4.4 %collective-permute-start.11 = (bf16[1040,128]{1,0:T(8,128)(2,1)S(1)}, bf16[1040,128]{1,0:T(8,128)(2,1)S(1)}, u32[]{:S(2)}, u32[]{:S(2)}) collective-permute-start(bf16[1040,128]{1,0:T(8,128)(2,1)S(1)} %get-tuple-element.24), channel_id=1, source_target_pairs={{320,64},{336,80},{224,128},{240,144},{321,65},{337,81},{225,129},... | collective-permute-start | bytes 798728 | tf_op jit(solution)/shard_map/right_step/ppermute | solution.py:172
  10.5 3.5 %collective-permute-start.10 = (bf16[1040,128]{1,0:T(8,128)(2,1)S(1)}, bf16[1040,128]{1,0:T(8,128)(2,1)S(1)}, u32[]{:S(2)}, u32[]{:S(2)}) collective-permute-start(bf16[1040,128]{1,0:T(8,128)(2,1)S(1)} %get-tuple-element.24), channel_id=1, source_target_pairs={{480,288},{496,304},{320,384},{336,400},{224,32},{240,48},{481,289... | collective-permute-start | bytes 798728 | tf_op jit(solution)/shard_map/right_step/ppermute | solution.py:172
  11.3 4.2 %collective-permute-start.15 = (bf16[1040,128]{1,0:T(8,128)(2,1)S(1)}, bf16[1040,128]{1,0:T(8,128)(2,1)S(1)}, u32[]{:S(2)}, u32[]{:S(2)}) collective-permute-start(bf16[1040,128]{1,0:T(8,128)(2,1)S(1)} %get-tuple-element.28), channel_id=1, source_target_pairs={{384,128},{400,144},{224,64},{240,80},{385,129},{401,145},{225,65}... | collective-permute-start | bytes 798728 | tf_op jit(solution)/shard_map/right_step/ppermute | solution.py:172
  12.0 3.5 %collective-permute-start.14 = (bf16[1040,128]{1,0:T(8,128)(2,1)S(1)}, bf16[1040,128]{1,0:T(8,128)(2,1)S(1)}, u32[]{:S(2)}, u32[]{:S(2)}) collective-permute-start(bf16[1040,128]{1,0:T(8,128)(2,1)S(1)} %get-tuple-element.28), channel_id=1, source_target_pairs={{480,416},{496,432},{384,320},{400,336},{224,160},{240,176},{481,4... | collective-permute-start | bytes 798728 | tf_op jit(solution)/shard_map/right_step/ppermute | solution.py:172
  12.8 27.5 %collective-permute-start.4 = (bf16[1040,128]{1,0:T(8,128)(2,1)S(1)}, bf16[1040,128]{1,0:T(8,128)(2,1)S(1)}, u32[]{:S(2)}, u32[]{:S(2)}) collective-permute-start(bf16[1040,128]{1,0:T(8,128)(2,1)S(1)} %add.45), channel_id=1, source_target_pairs={{12,8},{0,4},{268,256},{264,260},{13,9},{1,5},{269,257},{265,261},... | collective-permute-start | bytes 798728 | tf_op jit(solution)/shard_map/left_y/ppermute | solution.py:187
  14.1 2.7 %copy-start.5 = (s32[4,4]{1,0:T(4,128)S(1)}, s32[4,4]{1,0:T(4,128)}, u32[]{:S(2)}) copy-start(s32[4,4]{1,0:T(4,128)} %param.15) | copy-start | bytes 196
  14.1 39.2 %collective-permute-start.12 = (bf16[1040,128]{1,0:T(8,128)(2,1)S(1)}, bf16[1040,128]{1,0:T(8,128)(2,1)S(1)}, u32[]{:S(2)}, u32[]{:S(2)}) collective-permute-start(bf16[1040,128]{1,0:T(8,128)(2,1)S(1)} %add_add_fusion.1), channel_id=1, source_target_pairs={{32,0},{48,16},{288,256},{304,272},{224,192},{240,208},{480,448},{... | collective-permute-start | bytes 798728 | tf_op jit(solution)/shard_map/right_step/ppermute | solution.py:172
  15.5 37.9 %collective-permute-start.16 = (bf16[1040,128]{1,0:T(8,128)(2,1)S(1)}, bf16[1040,128]{1,0:T(8,128)(2,1)S(1)}, u32[]{:S(2)}, u32[]{:S(2)}) collective-permute-start(bf16[1040,128]{1,0:T(8,128)(2,1)S(1)} %add_add_fusion), channel_id=1, source_target_pairs={{160,192},{176,208},{416,448},{432,464},{224,0},{240,16},{480,256}... | collective-permute-start | bytes 798728 | tf_op jit(solution)/shard_map/right_step/ppermute | solution.py:172
  40.3 17.4 %collective-permute-start.7 = (bf16[1040,128]{1,0:T(8,128)(2,1)S(1)}, bf16[1040,128]{1,0:T(8,128)(2,1)S(1)}, u32[]{:S(2)}, u32[]{:S(2)}) collective-permute-start(bf16[1040,128]{1,0:T(8,128)(2,1)S(1)} %add.46.refs_0_), channel_id=1, source_target_pairs={{0,3},{1,0},{2,1},{3,2},{4,7},{5,4},{6,5},{7,6},{8,11},{9,8},{10,9... | collective-permute-start | bytes 798728 | tf_op jit(solution)/shard_map/left_x/ppermute | solution.py:194
  46.1 13.5 %collective-permute-start.6 = (bf16[1040,128]{1,0:T(8,128)(2,1)S(1)}, bf16[1040,128]{1,0:T(8,128)(2,1)S(1)}, u32[]{:S(2)}, u32[]{:S(2)}) collective-permute-start(bf16[1040,128]{1,0:T(8,128)(2,1)S(1)} %add.46.refs_0_), channel_id=1, source_target_pairs={{0,2},{1,3},{2,0},{3,1},{4,6},{5,7},{6,4},{7,5},{8,10},{9,11},{10,... | collective-permute-start | bytes 798728 | tf_op jit(solution)/shard_map/left_x/ppermute | solution.py:194
  50.0 13.3 %collective-permute-start.5 = (bf16[1040,128]{1,0:T(8,128)(2,1)S(1)}, bf16[1040,128]{1,0:T(8,128)(2,1)S(1)}, u32[]{:S(2)}, u32[]{:S(2)}) collective-permute-start(bf16[1040,128]{1,0:T(8,128)(2,1)S(1)} %add.46.refs_0_), channel_id=1, source_target_pairs={{0,1},{1,2},{2,3},{3,0},{4,5},{5,6},{6,7},{7,4},{8,9},{9,10},{10,1... | collective-permute-start | bytes 798728 | tf_op jit(solution)/shard_map/left_x/ppermute | solution.py:194
  57.7 5.7 %collective-permute-start.17 = (bf16[2,1040,128]{2,1,0:T(8,128)(2,1)}, bf16[2,1040,128]{2,1,0:T(8,128)(2,1)S(1)}, u32[]{:S(2)}, u32[]{:S(2)}) collective-permute-start(bf16[2,1040,128]{2,1,0:T(8,128)(2,1)} %pad_maximum_fusion), channel_id=1, source_target_pairs={{0,16},{16,0},{32,48},{48,32},{64,80},{80,64},{96,112},{112,96},{1... | collective-permute-start | bytes 1597448 | tf_op jit(solution)/shard_map/right_core/ppermute | solution.py:196

commit v4 on v3

--- a/solution.py
+++ b/solution.py
@@ -63,78 +63,66 @@
     return lax.optimization_barrier((array, *others))[0]
 
 
-def messages_kernel(a_index_ref, a_count_ref, b_index_ref, b_count_ref, a_ref, b_ref, *refs):
-    *quarter_refs, left_ref, right_ref, sems = refs
-    half_refs = [right_ref.at[h] for h in range(HALVES)]
-    row, col = lax.axis_index("row"), lax.axis_index("col")
-    own, root = col == N_COL - 1, row >= N_ROW - CORE
+def fill(tiles_ref, message_refs, slot_of, sems):
+    rows = RH * TILE
     lane = lax.broadcasted_iota(jnp.int32, (PAD, TILE), 1)
-    body, end = pl.ds(0, LQ * TILE), pl.ds(LQ * TILE, PAD)
-
-    def tail(slot_of):
+    copies = [
+        pltpu.make_async_copy(tiles_ref.at[pl.ds(i * rows, rows), :], ref.at[pl.ds(0, rows), :], sems.at[i])
+        for i, ref in enumerate(message_refs)
+    ]
+    for copy in copies:
+        copy.start()
+    for i, ref in enumerate(message_refs):
         line = jnp.full((PAD, TILE), -1, jnp.int32)
-        for t in range(LQ):
-            line = jnp.where(lane == t, slot_of(t), line)
-        return line.astype(jnp.float32).astype(jnp.bfloat16)
+        for t in range(RH):
+            line = jnp.where(lane == t, slot_of(i * RH + t), line)
+        ref[pl.ds(rows, PAD), :] = line.astype(jnp.float32).astype(jnp.bfloat16)
+    for copy in copies:
+        copy.wait()
+
+
+def left_kernel(index_ref, count_ref, tiles_ref, *refs):
+    *quarter_refs, own_ref, sems = refs
+    own = lax.axis_index("col") == N_COL - 1
 
     @pl.when(own)
     def _():
-        outs = (*quarter_refs, left_ref)
-        copies = [
-            pltpu.make_async_copy(a_ref.at[pl.ds(q * LQ * TILE, LQ * TILE), :], ref.at[body, :], sems.at[q])
-            for q, ref in enumerate(outs)
-        ]
-        for copy in copies:
-            copy.start()
-        for q, ref in enumerate(outs):
-
-            def slot_of(t, q=q):
-                section, place = divmod(q * LQ + t, KA)
-                return jnp.where(place < a_count_ref[section], a_index_ref[section * KA + place], -1)
-
-            ref[end, :] = tail(slot_of)
-        for copy in copies:
-            copy.wait()
+        def slot_of(i):
+            section, place = divmod(i, KA)
+            return jnp.where(place < count_ref[section], index_ref[section * KA + place], -1)
+
+        fill(tiles_ref, (*quarter_refs, own_ref), slot_of, sems)
 
     @pl.when(jnp.logical_not(own))
     def _():
-        left_ref[...] = jnp.zeros_like(left_ref)
+        own_ref[...] = jnp.zeros_like(own_ref)
+
+
+def right_kernel(index_ref, count_ref, tiles_ref, right_ref, sems):
+    root = lax.axis_index("row") >= N_ROW - CORE
 
     @pl.when(root)
     def _():
-        copies = [
-            pltpu.make_async_copy(b_ref.at[pl.ds(h * RH * TILE, RH * TILE), :], ref.at[body, :], sems.at[X + h])
-            for h, ref in enumerate(half_refs)
-        ]
-        for copy in copies:
-            copy.start()
-        for h, ref in enumerate(half_refs):
-
-            def slot_of(t, h=h):
-                return jnp.where(h * RH + t < b_count_ref[0], b_index_ref[h * RH + t], -1)
-
-            ref[end, :] = tail(slot_of)
-        for copy in copies:
-            copy.wait()
+        def slot_of(i):
+            return jnp.where(i < count_ref[0], index_ref[i], -1)
+
+        fill(tiles_ref, [right_ref.at[h] for h in range(HALVES)], slot_of, sems)
 
     @pl.when(jnp.logical_not(root))
     def _():
         right_ref[...] = jnp.zeros_like(right_ref)
 
 
-def messages(a_tiles, a_index, a_count, b_tiles, b_index, b_count):
+def messages(kernel, shapes, copies, index, count, tiles):
     smem = pl.BlockSpec(memory_space=pltpu.SMEM)
-    vmem = pl.BlockSpec(memory_space=pltpu.VMEM)
-    hbm = pl.BlockSpec(memory_space=pltpu.HBM)
     return pl.pallas_call(
-        messages_kernel,
-        out_shape=[jax.ShapeDtypeStruct((LQ * TILE + PAD, TILE), jnp.bfloat16)] * X
-        + [jax.ShapeDtypeStruct((HALVES, RH * TILE + PAD, TILE), jnp.bfloat16)],
-        in_specs=[smem] * 4 + [hbm] * 2,
-        out_specs=[vmem] * (X + 1),
-        scratch_shapes=[pltpu.SemaphoreType.DMA((X + HALVES,))],
+        kernel,
+        out_shape=[jax.ShapeDtypeStruct(shape, jnp.bfloat16) for shape in shapes],
+        in_specs=[smem, smem, pl.BlockSpec(memory_space=pl.ANY)],
+        out_specs=[pl.BlockSpec(memory_space=pltpu.VMEM)] * len(shapes),
+        scratch_shapes=[pltpu.SemaphoreType.DMA((copies,))],
         compiler_params=pltpu.CompilerParams(vmem_limit_bytes=4 * 1024 * 1024),
-    )(a_index, a_count, b_index, b_count, a_tiles, b_tiles)
+    )(index.reshape(-1), count.reshape(-1), tiles)
 
 
 def right_steps(h):
@@ -155,14 +143,10 @@
 def panels_everywhere(a_tiles, a_index, a_count, b_tiles, b_index, b_count, c_partial):
     both = ("row", "col")
     first, second = y_pairs()
-    *quarters, left, right = messages(
-        a_tiles.reshape(SECTIONS * KA * TILE, TILE),
-        a_index.reshape(-1),
-        a_count.reshape(-1),
-        b_tiles.reshape(KB * TILE, TILE),
-        b_index.reshape(-1),
-        b_count.reshape(-1),
-    )
+    message = (RH * TILE + PAD, TILE)
+    a_tiles, b_tiles = a_tiles.reshape(SECTIONS * KA * TILE, TILE), b_tiles.reshape(KB * TILE, TILE)
+    *quarters, left = messages(left_kernel, [message] * X, X, a_index, a_count, a_tiles)
+    (right,) = messages(right_kernel, [(HALVES, *message)], HALVES, b_index, b_count, b_tiles)
     for q in (1, 0, 2):
         with jax.named_scope("left_scatter"):
             left = left + lax.ppermute(quarters[q], "col", [(col_of(Y_HI - 1, X - 1), col_of(Y_HI - 1, q))])
@@ -247,6 +231,7 @@
 
         lax.fori_loop(0, LQ, step, 0)
 
+    sum_ref[...] = jnp.zeros_like(sum_ref)
     for n in range(NB):
         columns = pl.ds(n * TILE, TILE)
         total = jnp.zeros((1, TILE), jnp.float32)
@@ -256,7 +241,7 @@
             value = value * value * mask_ref[m * NB + n].astype(jnp.float32)
             kept_ref[rows, columns] = value
             total = total + jnp.sum(value, axis=0, keepdims=True)
-        sum_ref[:, columns] = total
+        sum_ref[n : n + 1, :] = total
 
 
 def product(slot, table, mask, lefts, rights, held):
@@ -266,7 +251,7 @@
         product_kernel,
         out_shape=(
             jax.ShapeDtypeStruct((MB * TILE, NB * TILE), jnp.float32),
-            jax.ShapeDtypeStruct((1, NB * TILE), jnp.float32),
+            jax.ShapeDtypeStruct((8, TILE), jnp.float32),
         ),
         in_specs=[smem] * 3 + [vmem] * (len(lefts) + len(rights) + 1),
         out_specs=(vmem, vmem),
@@ -283,9 +268,9 @@
     table = jnp.max(jnp.where(hit, jnp.arange(KB)[None, None, :], -1), axis=2).reshape(-1)
     slot = jnp.stack([slots_of(left[None], LQ) for left in lefts]).reshape(-1)
     kept, partial = product(slot, table, prune_mask.reshape(-1), lefts, rights, held)
-    total = jnp.sum(gather(partial[0], "row", CY_GROUPS), axis=0)
+    total = jnp.sum(gather(partial, "row", CY_GROUPS), axis=0)
     total = jnp.sum(gather(total, "row", Z_GROUPS), axis=0)
-    return kept * (ROWS / total)[None, :]
+    return kept * (ROWS / total[:NB]).reshape(1, NB * TILE)
 
 
 def solution(mesh):

time: 98.1 us -> 94.3 us (0.961)
  blocking collectives: 30.1 us -> 25.9 us
    all_to_all x2, blocking collectives: 30.1 us -> 25.9 us  [gather(): lax.all_to_all(jnp.broadcast_to(array, (n,) + array.shape), axis, 0, 0, a...]
  transfers between devices with their start and end apart: 18 -> 18, of which waited for: 3 -> 3; matrix products, arithmetic and copies ran while one was open for 2% -> 2% of each run, Pallas kernels for 0% -> 1%
where the time goes in v4:
time: 94.3 us; the launch traced here: 93.7 us
  waiting for transfers between devices  31.1 us (33%)
  starting transfers between devices  26.4 us (28%)
  blocking collectives  25.9 us (27%)
  Pallas kernels  3.63 us (4%)
  other arithmetic  2.8 us (3%)
  local copies, waits for them, and re-layouts  2.76 us (3%)
  between operations  1.17 us (1%)
    all_to_all x2, blocking collectives, gather(): lax.all_to_all(jnp.broadcast_to(array, (n,) + array.shape), axis, 0, 0, a...  25.9 us
    ppermute x1, waiting for transfers between devices, panels_everywhere(): left = left + lax.ppermute(left, both, second)  24 us
    ppermute x3, starting transfers between devices, panels_everywhere(): lefts.append(lax.ppermute(left, 'col', pairs))  13 us
    ppermute x9, starting transfers between devices, right_send(): lax.ppermute(array, 'row', [(row_of(*a, c), row_of(*b, c)) for a, b in pa...  7.48 us
    ppermute x3, waiting for transfers between devices, panels_everywhere(): lefts.append(lax.ppermute(left, 'col', pairs))  6.99 us
    unnamed x14, local copies, waits for them, and re-layouts  2.36 us
    pallas_call x1, Pallas kernels, product(): pl.pallas_call(product_kernel, out_shape=(jax.ShapeDtypeStruct((MB * TILE...  2.29 us
    ppermute x3, starting transfers between devices, panels_everywhere(): lax.ppermute(quarters[q], 'col', [(col_of(Y_HI - 1, X - 1), col_of(Y_HI -...  2.03 us
  transfers between devices with their start and end apart: 18, of which 3 were waited for; matrix products, arithmetic and copies ran while one was open for 2% of the time, Pallas kernels for 1%

profile of v4, /device:TPU:16, one launch (start us, length us, event | category | flops | bytes accessed | tf_op | source)
XLA Modules:
  0.0 93.7 jit_solution(6501890079217293734)
XLA Ops:
  0.8 1.0 %copy-done.2 = bf16[1,1,16,128,128]{4,3,2,1,0:T(8,128)(2,1)S(1)} copy-done((bf16[1,1,16,128,128]{4,3,2,1,0:T(8,128)(2,1)S(1)}, bf16[1,1,16,128,128]{4,3,2,1,0:T(8,128)(2,1)}, u32[]{:S(2)}) %copy-start.2) | copy-done | bytes 524312
  1.8 0.7 copy-done.3
  2.4 0.6 shard_map.83
  3.1 0.7 collective-permute-start.8
  3.9 0.7 copy-done.4
  4.5 0.6 shard_map.82
  5.2 0.7 collective-permute-start
  5.9 0.7 collective-permute-start.1
  6.5 0.7 collective-permute-start.2
  7.3 0.7 collective-permute-start.9
  8.0 0.7 collective-permute-start.13
  8.8 0.7 collective-permute-start.3
  9.5 0.1 add.47
  9.7 0.8 collective-permute-start.11
  10.5 0.7 collective-permute-start.10
  11.3 0.7 collective-permute-start.15
  12.0 0.7 collective-permute-start.14
  12.8 1.3 %collective-permute-start.4 = (bf16[1040,128]{1,0:T(8,128)(2,1)S(1)}, bf16[1040,128]{1,0:T(8,128)(2,1)S(1)}, u32[]{:S(2)}, u32[]{:S(2)}) collective-permute-start(bf16[1040,128]{1,0:T(8,128)(2,1)S(1)} %add.45), channel_id=1, source_target_pairs={{12,8},{0,4},{268,256},{264,260},{13,9},{1,5},{269,257},{265,261},... | collective-permute-start | bytes 798728 | tf_op jit(solution)/shard_map/left_y/ppermute | solution.py:171
  14.2 1.3 %collective-permute-start.12 = (bf16[1040,128]{1,0:T(8,128)(2,1)S(1)}, bf16[1040,128]{1,0:T(8,128)(2,1)S(1)}, u32[]{:S(2)}, u32[]{:S(2)}) collective-permute-start(bf16[1040,128]{1,0:T(8,128)(2,1)S(1)} %add_add_fusion.1), channel_id=1, source_target_pairs={{32,0},{48,16},{288,256},{304,272},{224,192},{240,208},{480,448},{... | collective-permute-start | bytes 798728 | tf_op jit(solution)/shard_map/right_step/ppermute | solution.py:156
  15.5 1.3 %collective-permute-start.16 = (bf16[1040,128]{1,0:T(8,128)(2,1)S(1)}, bf16[1040,128]{1,0:T(8,128)(2,1)S(1)}, u32[]{:S(2)}, u32[]{:S(2)}) collective-permute-start(bf16[1040,128]{1,0:T(8,128)(2,1)S(1)} %add_add_fusion), channel_id=1, source_target_pairs={{160,192},{176,208},{416,448},{432,464},{224,0},{240,16},{480,256}... | collective-permute-start | bytes 798728 | tf_op jit(solution)/shard_map/right_step/ppermute | solution.py:156
  16.9 24.0 %collective-permute-done.4 = bf16[1040,128]{1,0:T(8,128)(2,1)S(1)} collective-permute-done((bf16[1040,128]{1,0:T(8,128)(2,1)S(1)}, bf16[1040,128]{1,0:T(8,128)(2,1)S(1)}, u32[]{:S(2)}, u32[]{:S(2)}) %collective-permute-start.4) | collective-permute-done | bytes 266272 | tf_op jit(solution)/shard_map/left_y/ppermute | solution.py:171
  41.0 5.8 %collective-permute-start.7 = (bf16[1040,128]{1,0:T(8,128)(2,1)S(1)}, bf16[1040,128]{1,0:T(8,128)(2,1)S(1)}, u32[]{:S(2)}, u32[]{:S(2)}) collective-permute-start(bf16[1040,128]{1,0:T(8,128)(2,1)S(1)} %add.46.refs_0_), channel_id=1, source_target_pairs={{0,3},{1,0},{2,1},{3,2},{4,7},{5,4},{6,5},{7,6},{8,11},{9,8},{10,9... | collective-permute-start | bytes 798728 | tf_op jit(solution)/shard_map/left_x/ppermute | solution.py:178
  46.9 3.8 %collective-permute-start.6 = (bf16[1040,128]{1,0:T(8,128)(2,1)S(1)}, bf16[1040,128]{1,0:T(8,128)(2,1)S(1)}, u32[]{:S(2)}, u32[]{:S(2)}) collective-permute-start(bf16[1040,128]{1,0:T(8,128)(2,1)S(1)} %add.46.refs_0_), channel_id=1, source_target_pairs={{0,2},{1,3},{2,0},{3,1},{4,6},{5,7},{6,4},{7,5},{8,10},{9,11},{10,... | collective-permute-start | bytes 798728 | tf_op jit(solution)/shard_map/left_x/ppermute | solution.py:178
  50.7 3.3 %collective-permute-start.5 = (bf16[1040,128]{1,0:T(8,128)(2,1)S(1)}, bf16[1040,128]{1,0:T(8,128)(2,1)S(1)}, u32[]{:S(2)}, u32[]{:S(2)}) collective-permute-start(bf16[1040,128]{1,0:T(8,128)(2,1)S(1)} %add.46.refs_0_), channel_id=1, source_target_pairs={{0,1},{1,2},{2,3},{3,0},{4,5},{5,6},{6,7},{7,4},{8,9},{9,10},{10,1... | collective-permute-start | bytes 798728 | tf_op jit(solution)/shard_map/left_x/ppermute | solution.py:178
  54.3 0.8 pad_maximum_fusion
  55.1 3.3 %collective-permute-done.7.refs_3_ = bf16[1040,128]{1,0:T(8,128)(2,1)S(1)} collective-permute-done((bf16[1040,128]{1,0:T(8,128)(2,1)S(1)}, bf16[1040,128]{1,0:T(8,128)(2,1)S(1)}, u32[]{:S(2)}, u32[]{:S(2)}) %collective-permute-start.7) | collective-permute-done | bytes 266272 | tf_op jit(solution)/shard_map/left_x/ppermute | solution.py:178
  58.4 1.9 %collective-permute-start.17 = (bf16[2,1040,128]{2,1,0:T(8,128)(2,1)}, bf16[2,1040,128]{2,1,0:T(8,128)(2,1)S(1)}, u32[]{:S(2)}, u32[]{:S(2)}) collective-permute-start(bf16[2,1040,128]{2,1,0:T(8,128)(2,1)} %pad_maximum_fusion), channel_id=1, source_target_pairs={{0,16},{16,0},{32,48},{48,32},{64,80},{80,64},{96,112},{112,96},{1... | collective-permute-start | bytes 1597448 | tf_op jit(solution)/shard_map/right_core/ppermute | solution.py:180
  60.4 3.6 %collective-permute-done.5.refs_1_ = bf16[1040,128]{1,0:T(8,128)(2,1)S(1)} collective-permute-done((bf16[1040,128]{1,0:T(8,128)(2,1)S(1)}, bf16[1040,128]{1,0:T(8,128)(2,1)S(1)}, u32[]{:S(2)}, u32[]{:S(2)}) %collective-permute-start.5) | collective-permute-done | bytes 266272 | tf_op jit(solution)/shard_map/left_x/ppermute | solution.py:178
  64.3 2.3 %shard_map.85 = (f32[512,512]{1,0:T(8,128)S(1)}, f32[8,128]{1,0:T(8,128)S(1)}) custom-call(s32[32]{0:T(128)S(1)} %reshape.156.slot_ref, s32[256]{0:T(256)S(1)} %bitcast.53, s32[16]{0:T(128)S(1)} %reshape.154.mask_ref, bf16[1040,128]{1,0:T(8,128)(2,1)S(1)} %add.46.refs_0_, ...), custom_call_target="tpu_custom_call", output_to_operand_aliasing={{0}: (10, {})} | custom-call | tf_op jit(solution)/shard_map/pallas_call | solution.py:250
  66.7 6.2 %all_to_all.10 = f32[4,8,128]{2,1,0:T(8,128)S(1)} all-to-all(f32[4,8,128]{2,1,0:T(8,128)S(1)} %broadcast_in_dim.46), channel_id=1, replica_groups={{0,16,256,272},{32,48,288,304},{64,80,320,336},{96,112,352,368},{128,14..., dimensions={0} | all-to-all | bytes 32768 | tf_op jit(solution)/shard_map/all_to_all | solution.py:47
  72.9 19.7 %all_to_all.11 = f32[8,8,128]{2,1,0:T(8,128)S(1)} all-to-all(f32[8,8,128]{2,1,0:T(8,128)S(1)} %broadcast_in_dim.47), channel_id=1, replica_groups={{0,32,64,96,128,160,192,224},{16,48,80,112,144,176,208,240},{256,288,32..., dimensions={0} | all-to-all | bytes 65536 | tf_op jit(solution)/shard_map/all_to_all | solution.py:47
  92.6 1.1 %broadcast_multiply_fusion = f32[512,512]{1,0:T(8,128)} fusion(f32[512,512]{1,0:T(8,128)S(1)} %get-tuple-element.29, f32[512]{0:T(512)S(1)} %divide_bitcast_fusion), kind=kLoop, calls=%fused_computation.1 | loop fusion | flops 262144 | bytes 2099200 | tf_op jit(solution)/shard_map/mul | solution.py:273
  (54 shorter events, 1.2 us)
Async XLA Ops:
  0.0 3.9 %copy-start = (bf16[1,1,2,16,128,128]{5,4,3,2,1,0:T(8,128)(2,1)S(1)}, bf16[1,1,2,16,128,128]{5,4,3,2,1,0:T(8,128)(2,1)}, u32[]{:S(2)}) copy-start(bf16[1,1,2,16,128,128]{5,4,3,2,1,0:T(8,128)(2,1)} %param.8) | copy-start | bytes 3145732
  0.7 1.0 %copy-start.2 = (bf16[1,1,16,128,128]{4,3,2,1,0:T(8,128)(2,1)S(1)}, bf16[1,1,16,128,128]{4,3,2,1,0:T(8,128)(2,1)}, u32[]{:S(2)}) copy-start(bf16[1,1,16,128,128]{4,3,2,1,0:T(8,128)(2,1)} %param.11) | copy-start | bytes 1572868
  1.8 0.7 copy-start.3
  2.4 1.4 %copy-start.6 = (s32[1,1,2,16]{3,2,1,0:T(2,128)S(1)}, s32[1,1,2,16]{3,2,1,0:T(2,128)}, u32[]{:S(2)}) copy-start(s32[1,1,2,16]{3,2,1,0:T(2,128)} %param.9) | copy-start | bytes 388
  3.1 6.4 %collective-permute-start.8 = (bf16[2,1040,128]{2,1,0:T(8,128)(2,1)S(1)}, bf16[2,1040,128]{2,1,0:T(8,128)(2,1)S(1)}, u32[]{:S(2)}, u32[]{:S(2)}) collective-permute-start(bf16[2,1040,128]{2,1,0:T(8,128)(2,1)S(1)} %shard_map.83), channel_id=1, source_target_pairs={{480,224},{496,240},{481,225},{497,241},{482,226},{498,242},{483,2... | collective-permute-start | bytes 1597448 | tf_op jit(solution)/shard_map/right_step/ppermute | solution.py:156
  3.9 0.7 copy-start.4
  5.2 2.8 %collective-permute-start = (bf16[1040,128]{1,0:T(8,128)(2,1)S(1)}, bf16[1040,128]{1,0:T(8,128)(2,1)S(1)}, u32[]{:S(2)}, u32[]{:S(2)}) collective-permute-start(bf16[1040,128]{1,0:T(8,128)(2,1)S(1)} %get-tuple-element.19), channel_id=1, source_target_pairs={{15,13},{31,29},{47,45},{63,61},{79,77},{95,93},{111,109},{127,125... | collective-permute-start | bytes 798728 | tf_op jit(solution)/shard_map/left_scatter/ppermute | solution.py:152
  5.9 2.8 %collective-permute-start.1 = (bf16[1040,128]{1,0:T(8,128)(2,1)S(1)}, bf16[1040,128]{1,0:T(8,128)(2,1)S(1)}, u32[]{:S(2)}, u32[]{:S(2)}) collective-permute-start(bf16[1040,128]{1,0:T(8,128)(2,1)S(1)} %get-tuple-element.20), channel_id=1, source_target_pairs={{15,12},{31,28},{47,44},{63,60},{79,76},{95,92},{111,108},{127,124... | collective-permute-start | bytes 798728 | tf_op jit(solution)/shard_map/left_scatter/ppermute | solution.py:152
  6.5 2.1 %collective-permute-start.2 = (bf16[1040,128]{1,0:T(8,128)(2,1)S(1)}, bf16[1040,128]{1,0:T(8,128)(2,1)S(1)}, u32[]{:S(2)}, u32[]{:S(2)}) collective-permute-start(bf16[1040,128]{1,0:T(8,128)(2,1)S(1)} %get-tuple-element.21), channel_id=1, source_target_pairs={{15,14},{31,30},{47,46},{63,62},{79,78},{95,94},{111,110},{127,126... | collective-permute-start | bytes 798728 | tf_op jit(solution)/shard_map/left_scatter/ppermute | solution.py:152
  7.3 2.3 %collective-permute-start.9 = (bf16[1040,128]{1,0:T(8,128)(2,1)S(1)}, bf16[1040,128]{1,0:T(8,128)(2,1)S(1)}, u32[]{:S(2)}, u32[]{:S(2)}) collective-permute-start(bf16[1040,128]{1,0:T(8,128)(2,1)S(1)} %get-tuple-element.35), channel_id=1, source_target_pairs={{480,320},{496,336},{481,321},{497,337},{482,322},{498,338},{483,3... | collective-permute-start | bytes 798728 | tf_op jit(solution)/shard_map/right_step/ppermute | solution.py:156
  8.0 1.7 %collective-permute-start.13 = (bf16[1040,128]{1,0:T(8,128)(2,1)S(1)}, bf16[1040,128]{1,0:T(8,128)(2,1)S(1)}, u32[]{:S(2)}, u32[]{:S(2)}) collective-permute-start(bf16[1040,128]{1,0:T(8,128)(2,1)S(1)} %get-tuple-element.36), channel_id=1, source_target_pairs={{480,384},{496,400},{481,385},{497,401},{482,386},{498,402},{483,3... | collective-permute-start | bytes 798728 | tf_op jit(solution)/shard_map/right_step/ppermute | solution.py:156
  8.8 3.9 %collective-permute-start.3 = (bf16[1040,128]{1,0:T(8,128)(2,1)S(1)}, bf16[1040,128]{1,0:T(8,128)(2,1)S(1)}, u32[]{:S(2)}, u32[]{:S(2)}) collective-permute-start(bf16[1040,128]{1,0:T(8,128)(2,1)S(1)} %add_add_fusion.2), channel_id=1, source_target_pairs={{12,0},{268,264},{13,1},{269,265},{14,2},{270,266},{15,3},{271,267... | collective-permute-start | bytes 798728 | tf_op jit(solution)/shard_map/left_y/ppermute | solution.py:166
  9.6 1.6 %copy-start.1 = (f32[512,512]{1,0:T(8,128)S(1)}, f32[512,512]{1,0:T(8,128)}, u32[]{:S(2)}) copy-start(f32[512,512]{1,0:T(8,128)} %c_ref) | copy-start | bytes 3145732
  9.7 4.4 %collective-permute-start.11 = (bf16[1040,128]{1,0:T(8,128)(2,1)S(1)}, bf16[1040,128]{1,0:T(8,128)(2,1)S(1)}, u32[]{:S(2)}, u32[]{:S(2)}) collective-permute-start(bf16[1040,128]{1,0:T(8,128)(2,1)S(1)} %get-tuple-element.22), channel_id=1, source_target_pairs={{320,64},{336,80},{224,128},{240,144},{321,65},{337,81},{225,129},... | collective-permute-start | bytes 798728 | tf_op jit(solution)/shard_map/right_step/ppermute | solution.py:156
  10.5 3.5 %collective-permute-start.10 = (bf16[1040,128]{1,0:T(8,128)(2,1)S(1)}, bf16[1040,128]{1,0:T(8,128)(2,1)S(1)}, u32[]{:S(2)}, u32[]{:S(2)}) collective-permute-start(bf16[1040,128]{1,0:T(8,128)(2,1)S(1)} %get-tuple-element.22), channel_id=1, source_target_pairs={{480,288},{496,304},{320,384},{336,400},{224,32},{240,48},{481,289... | collective-permute-start | bytes 798728 | tf_op jit(solution)/shard_map/right_step/ppermute | solution.py:156
  11.3 4.2 %collective-permute-start.15 = (bf16[1040,128]{1,0:T(8,128)(2,1)S(1)}, bf16[1040,128]{1,0:T(8,128)(2,1)S(1)}, u32[]{:S(2)}, u32[]{:S(2)}) collective-permute-start(bf16[1040,128]{1,0:T(8,128)(2,1)S(1)} %get-tuple-element.26), channel_id=1, source_target_pairs={{384,128},{400,144},{224,64},{240,80},{385,129},{401,145},{225,65}... | collective-permute-start | bytes 798728 | tf_op jit(solution)/shard_map/right_step/ppermute | solution.py:156
  12.0 3.5 %collective-permute-start.14 = (bf16[1040,128]{1,0:T(8,128)(2,1)S(1)}, bf16[1040,128]{1,0:T(8,128)(2,1)S(1)}, u32[]{:S(2)}, u32[]{:S(2)}) collective-permute-start(bf16[1040,128]{1,0:T(8,128)(2,1)S(1)} %get-tuple-element.26), channel_id=1, source_target_pairs={{480,416},{496,432},{384,320},{400,336},{224,160},{240,176},{481,4... | collective-permute-start | bytes 798728 | tf_op jit(solution)/shard_map/right_step/ppermute | solution.py:156
  12.8 28.2 %collective-permute-start.4 = (bf16[1040,128]{1,0:T(8,128)(2,1)S(1)}, bf16[1040,128]{1,0:T(8,128)(2,1)S(1)}, u32[]{:S(2)}, u32[]{:S(2)}) collective-permute-start(bf16[1040,128]{1,0:T(8,128)(2,1)S(1)} %add.45), channel_id=1, source_target_pairs={{12,8},{0,4},{268,256},{264,260},{13,9},{1,5},{269,257},{265,261},... | collective-permute-start | bytes 798728 | tf_op jit(solution)/shard_map/left_y/ppermute | solution.py:171
  14.2 2.7 %copy-start.5 = (s32[4,4]{1,0:T(4,128)S(1)}, s32[4,4]{1,0:T(4,128)}, u32[]{:S(2)}) copy-start(s32[4,4]{1,0:T(4,128)} %param.15) | copy-start | bytes 196
  14.2 39.9 %collective-permute-start.12 = (bf16[1040,128]{1,0:T(8,128)(2,1)S(1)}, bf16[1040,128]{1,0:T(8,128)(2,1)S(1)}, u32[]{:S(2)}, u32[]{:S(2)}) collective-permute-start(bf16[1040,128]{1,0:T(8,128)(2,1)S(1)} %add_add_fusion.1), channel_id=1, source_target_pairs={{32,0},{48,16},{288,256},{304,272},{224,192},{240,208},{480,448},{... | collective-permute-start | bytes 798728 | tf_op jit(solution)/shard_map/right_step/ppermute | solution.py:156
  15.5 38.6 %collective-permute-start.16 = (bf16[1040,128]{1,0:T(8,128)(2,1)S(1)}, bf16[1040,128]{1,0:T(8,128)(2,1)S(1)}, u32[]{:S(2)}, u32[]{:S(2)}) collective-permute-start(bf16[1040,128]{1,0:T(8,128)(2,1)S(1)} %add_add_fusion), channel_id=1, source_target_pairs={{160,192},{176,208},{416,448},{432,464},{224,0},{240,16},{480,256}... | collective-permute-start | bytes 798728 | tf_op jit(solution)/shard_map/right_step/ppermute | solution.py:156
  41.0 17.4 %collective-permute-start.7 = (bf16[1040,128]{1,0:T(8,128)(2,1)S(1)}, bf16[1040,128]{1,0:T(8,128)(2,1)S(1)}, u32[]{:S(2)}, u32[]{:S(2)}) collective-permute-start(bf16[1040,128]{1,0:T(8,128)(2,1)S(1)} %add.46.refs_0_), channel_id=1, source_target_pairs={{0,3},{1,0},{2,1},{3,2},{4,7},{5,4},{6,5},{7,6},{8,11},{9,8},{10,9... | collective-permute-start | bytes 798728 | tf_op jit(solution)/shard_map/left_x/ppermute | solution.py:178
  46.9 13.5 %collective-permute-start.6 = (bf16[1040,128]{1,0:T(8,128)(2,1)S(1)}, bf16[1040,128]{1,0:T(8,128)(2,1)S(1)}, u32[]{:S(2)}, u32[]{:S(2)}) collective-permute-start(bf16[1040,128]{1,0:T(8,128)(2,1)S(1)} %add.46.refs_0_), channel_id=1, source_target_pairs={{0,2},{1,3},{2,0},{3,1},{4,6},{5,7},{6,4},{7,5},{8,10},{9,11},{10,... | collective-permute-start | bytes 798728 | tf_op jit(solution)/shard_map/left_x/ppermute | solution.py:178
  50.7 13.3 %collective-permute-start.5 = (bf16[1040,128]{1,0:T(8,128)(2,1)S(1)}, bf16[1040,128]{1,0:T(8,128)(2,1)S(1)}, u32[]{:S(2)}, u32[]{:S(2)}) collective-permute-start(bf16[1040,128]{1,0:T(8,128)(2,1)S(1)} %add.46.refs_0_), channel_id=1, source_target_pairs={{0,1},{1,2},{2,3},{3,0},{4,5},{5,6},{6,7},{7,4},{8,9},{9,10},{10,1... | collective-permute-start | bytes 798728 | tf_op jit(solution)/shard_map/left_x/ppermute | solution.py:178
  58.4 5.7 %collective-permute-start.17 = (bf16[2,1040,128]{2,1,0:T(8,128)(2,1)}, bf16[2,1040,128]{2,1,0:T(8,128)(2,1)S(1)}, u32[]{:S(2)}, u32[]{:S(2)}) collective-permute-start(bf16[2,1040,128]{2,1,0:T(8,128)(2,1)} %pad_maximum_fusion), channel_id=1, source_target_pairs={{0,16},{16,0},{32,48},{48,32},{64,80},{80,64},{96,112},{112,96},{1... | collective-permute-start | bytes 1597448 | tf_op jit(solution)/shard_map/right_core/ppermute | solution.py:180

commit v5 on v4

--- a/solution.py
+++ b/solution.py
@@ -132,10 +132,10 @@
 
         return [(at(y, a), at(to, b)) for y, a, to, b in moves]
 
-    both = [(y, a, y, b) for a, b in ((2, 1), (0, 7), (3, 4), (5, 6)) for y in range(Y_LO)]
+    both = [(y, a, y, b) for a, b in ((0, 1), (6, 7), (4, 5), (3, 2)) for y in range(Y_LO)]
     return [
         [pairs((1, 0, 1, 3))],
-        [pairs((1, 0, 1, 2), (1, 3, 1, 5), (0, 0, 0, 2)), pairs((1, 3, 0, 3), (0, 0, 0, 5))],
+        [pairs((1, 0, 1, 6), (0, 0, 0, 6), (1, 3, 1, 4)), pairs((1, 3, 0, 3), (0, 0, 0, 4))],
         [pairs(*both)],
     ]
 

time: 94.3 us -> 94.6 us (level)
  the two profiles are of different devices: /device:TPU:16 before, /device:TPU:48 now
where the time goes in v5:
time: 94.6 us; the launch traced here: 94.1 us
  blocking collectives  35.5 us (38%)
  starting transfers between devices  27.6 us (29%)
  waiting for transfers between devices  20.4 us (22%)
  Pallas kernels  3.87 us (4%)
  other arithmetic  2.79 us (3%)
  local copies, waits for them, and re-layouts  2.76 us (3%)
  between operations  1.14 us (1%)
    all_to_all x2, blocking collectives, gather(): lax.all_to_all(jnp.broadcast_to(array, (n,) + array.shape), axis, 0, 0, a...  35.5 us
    ppermute x3, starting transfers between devices, panels_everywhere(): lefts.append(lax.ppermute(left, 'col', pairs))  13 us
    ppermute x3, waiting for transfers between devices, panels_everywhere(): lax.ppermute(quarters[q], 'col', [(col_of(Y_HI - 1, X - 1), col_of(Y_HI -...  9.39 us
    ppermute x9, starting transfers between devices, right_send(): lax.ppermute(array, 'row', [(row_of(*a, c), row_of(*b, c)) for a, b in pa...  7.48 us
    ppermute x9, waiting for transfers between devices, right_send(): lax.ppermute(array, 'row', [(row_of(*a, c), row_of(*b, c)) for a, b in pa...  5.65 us
    ppermute x3, starting transfers between devices, panels_everywhere(): lax.ppermute(quarters[q], 'col', [(col_of(Y_HI - 1, X - 1), col_of(Y_HI -...  2.65 us
    pallas_call x1, Pallas kernels, product(): pl.pallas_call(product_kernel, out_shape=(jax.ShapeDtypeStruct((MB * TILE...  2.53 us
    unnamed x14, local copies, waits for them, and re-layouts  2.36 us
  transfers between devices with their start and end apart: 18, of which 5 were waited for; matrix products, arithmetic and copies ran while one was open for 2% of the time, Pallas kernels for 1%

profile of v5, /device:TPU:48, one launch (start us, length us, event | category | flops | bytes accessed | tf_op | source)
XLA Modules:
  0.0 94.1 jit_solution(9961801762400055747)
XLA Ops:
  0.8 1.0 %copy-done.2 = bf16[1,1,16,128,128]{4,3,2,1,0:T(8,128)(2,1)S(1)} copy-done((bf16[1,1,16,128,128]{4,3,2,1,0:T(8,128)(2,1)S(1)}, bf16[1,1,16,128,128]{4,3,2,1,0:T(8,128)(2,1)}, u32[]{:S(2)}) %copy-start.2) | copy-done | bytes 524312
  1.8 0.7 copy-done.3
  2.4 0.6 shard_map.83
  3.1 0.7 collective-permute-start.8
  3.9 0.7 copy-done.4
  5.2 0.7 collective-permute-start
  5.9 1.3 %collective-permute-start.1 = (bf16[1040,128]{1,0:T(8,128)(2,1)S(1)}, bf16[1040,128]{1,0:T(8,128)(2,1)S(1)}, u32[]{:S(2)}, u32[]{:S(2)}) collective-permute-start(bf16[1040,128]{1,0:T(8,128)(2,1)S(1)} %get-tuple-element.20), channel_id=1, source_target_pairs={{15,12},{31,28},{47,44},{63,60},{79,76},{95,92},{111,108},{127,124... | collective-permute-start | bytes 798728 | tf_op jit(solution)/shard_map/left_scatter/ppermute | solution.py:152
  7.2 0.7 collective-permute-start.2
  7.9 0.7 collective-permute-start.9
  8.6 0.7 collective-permute-start.13
  9.3 9.4 %collective-permute-done.1 = bf16[1040,128]{1,0:T(8,128)(2,1)S(1)} collective-permute-done((bf16[1040,128]{1,0:T(8,128)(2,1)S(1)}, bf16[1040,128]{1,0:T(8,128)(2,1)S(1)}, u32[]{:S(2)}, u32[]{:S(2)}) %collective-permute-start.1) | collective-permute-done | bytes 266272 | tf_op jit(solution)/shard_map/left_scatter/ppermute | solution.py:152
  18.7 1.3 %collective-permute-start.3 = (bf16[1040,128]{1,0:T(8,128)(2,1)S(1)}, bf16[1040,128]{1,0:T(8,128)(2,1)S(1)}, u32[]{:S(2)}, u32[]{:S(2)}) collective-permute-start(bf16[1040,128]{1,0:T(8,128)(2,1)S(1)} %add_add_fusion.2), channel_id=1, source_target_pairs={{12,0},{268,264},{13,1},{269,265},{14,2},{270,266},{15,3},{271,267... | collective-permute-start | bytes 798728 | tf_op jit(solution)/shard_map/left_y/ppermute | solution.py:166
  20.3 0.8 collective-permute-start.11
  21.1 0.7 collective-permute-start.10
  21.9 0.7 collective-permute-start.15
  22.6 0.7 collective-permute-start.14
  23.3 1.8 %collective-permute-done.3 = bf16[1040,128]{1,0:T(8,128)(2,1)S(1)} collective-permute-done((bf16[1040,128]{1,0:T(8,128)(2,1)S(1)}, bf16[1040,128]{1,0:T(8,128)(2,1)S(1)}, u32[]{:S(2)}, u32[]{:S(2)}) %collective-permute-start.3) | collective-permute-done | bytes 266272 | tf_op jit(solution)/shard_map/left_y/ppermute | solution.py:166
  25.2 1.3 %collective-permute-start.4 = (bf16[1040,128]{1,0:T(8,128)(2,1)S(1)}, bf16[1040,128]{1,0:T(8,128)(2,1)S(1)}, u32[]{:S(2)}, u32[]{:S(2)}) collective-permute-start(bf16[1040,128]{1,0:T(8,128)(2,1)S(1)} %add.45), channel_id=1, source_target_pairs={{12,8},{0,4},{268,256},{264,260},{13,9},{1,5},{269,257},{265,261},... | collective-permute-start | bytes 798728 | tf_op jit(solution)/shard_map/left_y/ppermute | solution.py:171
  26.6 1.3 %collective-permute-start.12 = (bf16[1040,128]{1,0:T(8,128)(2,1)S(1)}, bf16[1040,128]{1,0:T(8,128)(2,1)S(1)}, u32[]{:S(2)}, u32[]{:S(2)}) collective-permute-start(bf16[1040,128]{1,0:T(8,128)(2,1)S(1)} %add_add_fusion.1), channel_id=1, source_target_pairs={{224,0},{240,16},{480,256},{496,272},{160,192},{176,208},{416,448}... | collective-permute-start | bytes 798728 | tf_op jit(solution)/shard_map/right_step/ppermute | solution.py:156
  27.9 1.3 %collective-permute-start.16 = (bf16[1040,128]{1,0:T(8,128)(2,1)S(1)}, bf16[1040,128]{1,0:T(8,128)(2,1)S(1)}, u32[]{:S(2)}, u32[]{:S(2)}) collective-permute-start(bf16[1040,128]{1,0:T(8,128)(2,1)S(1)} %add_add_fusion), channel_id=1, source_target_pairs={{224,192},{240,208},{480,448},{496,464},{32,0},{48,16},{288,256},{... | collective-permute-start | bytes 798728 | tf_op jit(solution)/shard_map/right_step/ppermute | solution.py:156
  29.3 1.6 %collective-permute-done.4 = bf16[1040,128]{1,0:T(8,128)(2,1)S(1)} collective-permute-done((bf16[1040,128]{1,0:T(8,128)(2,1)S(1)}, bf16[1040,128]{1,0:T(8,128)(2,1)S(1)}, u32[]{:S(2)}, u32[]{:S(2)}) %collective-permute-start.4) | collective-permute-done | bytes 266272 | tf_op jit(solution)/shard_map/left_y/ppermute | solution.py:171
  31.0 5.8 %collective-permute-start.7 = (bf16[1040,128]{1,0:T(8,128)(2,1)S(1)}, bf16[1040,128]{1,0:T(8,128)(2,1)S(1)}, u32[]{:S(2)}, u32[]{:S(2)}) collective-permute-start(bf16[1040,128]{1,0:T(8,128)(2,1)S(1)} %add.46.refs_0_), channel_id=1, source_target_pairs={{0,3},{1,0},{2,1},{3,2},{4,7},{5,4},{6,5},{7,6},{8,11},{9,8},{10,9... | collective-permute-start | bytes 798728 | tf_op jit(solution)/shard_map/left_x/ppermute | solution.py:178
  36.9 3.8 %collective-permute-start.6 = (bf16[1040,128]{1,0:T(8,128)(2,1)S(1)}, bf16[1040,128]{1,0:T(8,128)(2,1)S(1)}, u32[]{:S(2)}, u32[]{:S(2)}) collective-permute-start(bf16[1040,128]{1,0:T(8,128)(2,1)S(1)} %add.46.refs_0_), channel_id=1, source_target_pairs={{0,2},{1,3},{2,0},{3,1},{4,6},{5,7},{6,4},{7,5},{8,10},{9,11},{10,... | collective-permute-start | bytes 798728 | tf_op jit(solution)/shard_map/left_x/ppermute | solution.py:178
  40.7 3.3 %collective-permute-start.5 = (bf16[1040,128]{1,0:T(8,128)(2,1)S(1)}, bf16[1040,128]{1,0:T(8,128)(2,1)S(1)}, u32[]{:S(2)}, u32[]{:S(2)}) collective-permute-start(bf16[1040,128]{1,0:T(8,128)(2,1)S(1)} %add.46.refs_0_), channel_id=1, source_target_pairs={{0,1},{1,2},{2,3},{3,0},{4,5},{5,6},{6,7},{7,4},{8,9},{9,10},{10,1... | collective-permute-start | bytes 798728 | tf_op jit(solution)/shard_map/left_x/ppermute | solution.py:178
  44.0 5.6 %collective-permute-done.12 = bf16[1040,128]{1,0:T(8,128)(2,1)S(1)} collective-permute-done((bf16[1040,128]{1,0:T(8,128)(2,1)S(1)}, bf16[1040,128]{1,0:T(8,128)(2,1)S(1)}, u32[]{:S(2)}, u32[]{:S(2)}) %collective-permute-start.12) | collective-permute-done | bytes 266272 | tf_op jit(solution)/shard_map/right_step/ppermute | solution.py:156
  49.8 0.8 pad_maximum_fusion
  50.7 1.9 %collective-permute-start.17 = (bf16[2,1040,128]{2,1,0:T(8,128)(2,1)}, bf16[2,1040,128]{2,1,0:T(8,128)(2,1)S(1)}, u32[]{:S(2)}, u32[]{:S(2)}) collective-permute-start(bf16[2,1040,128]{2,1,0:T(8,128)(2,1)} %pad_maximum_fusion), channel_id=1, source_target_pairs={{0,16},{16,0},{32,48},{48,32},{64,80},{80,64},{96,112},{112,96},{1... | collective-permute-start | bytes 1597448 | tf_op jit(solution)/shard_map/right_core/ppermute | solution.py:180
  52.8 1.9 %collective-permute-done.17.refs_6_ = bf16[2,1040,128]{2,1,0:T(8,128)(2,1)S(1)} collective-permute-done((bf16[2,1040,128]{2,1,0:T(8,128)(2,1)}, bf16[2,1040,128]{2,1,0:T(8,128)(2,1)S(1)}, u32[]{:S(2)}, u32[]{:S(2)}) %collective-permute-start.17) | collective-permute-done | bytes 532512 | tf_op jit(solution)/shard_map/right_core/ppermute | solution.py:180
  54.9 2.5 %shard_map.85 = (f32[512,512]{1,0:T(8,128)S(1)}, f32[8,128]{1,0:T(8,128)S(1)}) custom-call(s32[32]{0:T(128)S(1)} %reshape.156.slot_ref, s32[256]{0:T(256)S(1)} %bitcast.53, s32[16]{0:T(128)S(1)} %reshape.154.mask_ref, bf16[1040,128]{1,0:T(8,128)(2,1)S(1)} %add.46.refs_0_, ...), custom_call_target="tpu_custom_call", output_to_operand_aliasing={{0}: (10, {})} | custom-call | tf_op jit(solution)/shard_map/pallas_call | solution.py:250
  57.4 6.8 %all_to_all.10 = f32[4,8,128]{2,1,0:T(8,128)S(1)} all-to-all(f32[4,8,128]{2,1,0:T(8,128)S(1)} %broadcast_in_dim.46), channel_id=1, replica_groups={{0,16,256,272},{32,48,288,304},{64,80,320,336},{96,112,352,368},{128,14..., dimensions={0} | all-to-all | bytes 32768 | tf_op jit(solution)/shard_map/all_to_all | solution.py:47
  64.3 28.7 %all_to_all.11 = f32[8,8,128]{2,1,0:T(8,128)S(1)} all-to-all(f32[8,8,128]{2,1,0:T(8,128)S(1)} %broadcast_in_dim.47), channel_id=1, replica_groups={{0,32,64,96,128,160,192,224},{16,48,80,112,144,176,208,240},{256,288,32..., dimensions={0} | all-to-all | bytes 65536 | tf_op jit(solution)/shard_map/all_to_all | solution.py:47
  93.0 1.1 %broadcast_multiply_fusion = f32[512,512]{1,0:T(8,128)} fusion(f32[512,512]{1,0:T(8,128)S(1)} %get-tuple-element.29, f32[512]{0:T(512)S(1)} %divide_bitcast_fusion), kind=kLoop, calls=%fused_computation.1 | loop fusion | flops 262144 | bytes 2099200 | tf_op jit(solution)/shard_map/mul | solution.py:273
  (54 shorter events, 2.0 us)
Async XLA Ops:
  0.0 3.9 %copy-start = (bf16[1,1,2,16,128,128]{5,4,3,2,1,0:T(8,128)(2,1)S(1)}, bf16[1,1,2,16,128,128]{5,4,3,2,1,0:T(8,128)(2,1)}, u32[]{:S(2)}) copy-start(bf16[1,1,2,16,128,128]{5,4,3,2,1,0:T(8,128)(2,1)} %param.8) | copy-start | bytes 3145732
  0.7 1.0 %copy-start.2 = (bf16[1,1,16,128,128]{4,3,2,1,0:T(8,128)(2,1)S(1)}, bf16[1,1,16,128,128]{4,3,2,1,0:T(8,128)(2,1)}, u32[]{:S(2)}) copy-start(bf16[1,1,16,128,128]{4,3,2,1,0:T(8,128)(2,1)} %param.11) | copy-start | bytes 1572868
  1.8 0.7 copy-start.3
  2.4 1.4 %copy-start.6 = (s32[1,1,2,16]{3,2,1,0:T(2,128)S(1)}, s32[1,1,2,16]{3,2,1,0:T(2,128)}, u32[]{:S(2)}) copy-start(s32[1,1,2,16]{3,2,1,0:T(2,128)} %param.9) | copy-start | bytes 388
  3.1 17.0 %collective-permute-start.8 = (bf16[2,1040,128]{2,1,0:T(8,128)(2,1)S(1)}, bf16[2,1040,128]{2,1,0:T(8,128)(2,1)S(1)}, u32[]{:S(2)}, u32[]{:S(2)}) collective-permute-start(bf16[2,1040,128]{2,1,0:T(8,128)(2,1)S(1)} %shard_map.83), channel_id=1, source_target_pairs={{480,224},{496,240},{481,225},{497,241},{482,226},{498,242},{483,2... | collective-permute-start | bytes 1597448 | tf_op jit(solution)/shard_map/right_step/ppermute | solution.py:156
  3.9 0.7 copy-start.4
  5.2 3.4 %collective-permute-start = (bf16[1040,128]{1,0:T(8,128)(2,1)S(1)}, bf16[1040,128]{1,0:T(8,128)(2,1)S(1)}, u32[]{:S(2)}, u32[]{:S(2)}) collective-permute-start(bf16[1040,128]{1,0:T(8,128)(2,1)S(1)} %get-tuple-element.19), channel_id=1, source_target_pairs={{15,13},{31,29},{47,45},{63,61},{79,77},{95,93},{111,109},{127,125... | collective-permute-start | bytes 798728 | tf_op jit(solution)/shard_map/left_scatter/ppermute | solution.py:152
  5.9 12.8 %collective-permute-start.1 = (bf16[1040,128]{1,0:T(8,128)(2,1)S(1)}, bf16[1040,128]{1,0:T(8,128)(2,1)S(1)}, u32[]{:S(2)}, u32[]{:S(2)}) collective-permute-start(bf16[1040,128]{1,0:T(8,128)(2,1)S(1)} %get-tuple-element.20), channel_id=1, source_target_pairs={{15,12},{31,28},{47,44},{63,60},{79,76},{95,92},{111,108},{127,124... | collective-permute-start | bytes 798728 | tf_op jit(solution)/shard_map/left_scatter/ppermute | solution.py:152
  7.2 11.5 %collective-permute-start.2 = (bf16[1040,128]{1,0:T(8,128)(2,1)S(1)}, bf16[1040,128]{1,0:T(8,128)(2,1)S(1)}, u32[]{:S(2)}, u32[]{:S(2)}) collective-permute-start(bf16[1040,128]{1,0:T(8,128)(2,1)S(1)} %get-tuple-element.21), channel_id=1, source_target_pairs={{15,14},{31,30},{47,46},{63,62},{79,78},{95,94},{111,110},{127,126... | collective-permute-start | bytes 798728 | tf_op jit(solution)/shard_map/left_scatter/ppermute | solution.py:152
  7.9 12.3 %collective-permute-start.9 = (bf16[1040,128]{1,0:T(8,128)(2,1)S(1)}, bf16[1040,128]{1,0:T(8,128)(2,1)S(1)}, u32[]{:S(2)}, u32[]{:S(2)}) collective-permute-start(bf16[1040,128]{1,0:T(8,128)(2,1)S(1)} %get-tuple-element.35), channel_id=1, source_target_pairs={{480,320},{496,336},{481,321},{497,337},{482,322},{498,338},{483,3... | collective-permute-start | bytes 798728 | tf_op jit(solution)/shard_map/right_step/ppermute | solution.py:156
  8.6 11.6 %collective-permute-start.13 = (bf16[1040,128]{1,0:T(8,128)(2,1)S(1)}, bf16[1040,128]{1,0:T(8,128)(2,1)S(1)}, u32[]{:S(2)}, u32[]{:S(2)}) collective-permute-start(bf16[1040,128]{1,0:T(8,128)(2,1)S(1)} %get-tuple-element.36), channel_id=1, source_target_pairs={{480,384},{496,400},{481,385},{497,401},{482,386},{498,402},{483,3... | collective-permute-start | bytes 798728 | tf_op jit(solution)/shard_map/right_step/ppermute | solution.py:156
  18.7 6.3 %collective-permute-start.3 = (bf16[1040,128]{1,0:T(8,128)(2,1)S(1)}, bf16[1040,128]{1,0:T(8,128)(2,1)S(1)}, u32[]{:S(2)}, u32[]{:S(2)}) collective-permute-start(bf16[1040,128]{1,0:T(8,128)(2,1)S(1)} %add_add_fusion.2), channel_id=1, source_target_pairs={{12,0},{268,264},{13,1},{269,265},{14,2},{270,266},{15,3},{271,267... | collective-permute-start | bytes 798728 | tf_op jit(solution)/shard_map/left_y/ppermute | solution.py:166
  20.2 1.6 %copy-start.1 = (f32[512,512]{1,0:T(8,128)S(1)}, f32[512,512]{1,0:T(8,128)}, u32[]{:S(2)}) copy-start(f32[512,512]{1,0:T(8,128)} %c_ref) | copy-start | bytes 3145732
  20.3 6.1 %collective-permute-start.11 = (bf16[1040,128]{1,0:T(8,128)(2,1)S(1)}, bf16[1040,128]{1,0:T(8,128)(2,1)S(1)}, u32[]{:S(2)}, u32[]{:S(2)}) collective-permute-start(bf16[1040,128]{1,0:T(8,128)(2,1)S(1)} %get-tuple-element.22), channel_id=1, source_target_pairs={{320,64},{336,80},{224,96},{240,112},{321,65},{337,81},{225,97},{2... | collective-permute-start | bytes 798728 | tf_op jit(solution)/shard_map/right_step/ppermute | solution.py:156
  21.1 5.3 %collective-permute-start.10 = (bf16[1040,128]{1,0:T(8,128)(2,1)S(1)}, bf16[1040,128]{1,0:T(8,128)(2,1)S(1)}, u32[]{:S(2)}, u32[]{:S(2)}) collective-permute-start(bf16[1040,128]{1,0:T(8,128)(2,1)S(1)} %get-tuple-element.22), channel_id=1, source_target_pairs={{480,416},{496,432},{224,160},{240,176},{320,352},{336,368},{481,4... | collective-permute-start | bytes 798728 | tf_op jit(solution)/shard_map/right_step/ppermute | solution.py:156
  21.9 5.9 %collective-permute-start.15 = (bf16[1040,128]{1,0:T(8,128)(2,1)S(1)}, bf16[1040,128]{1,0:T(8,128)(2,1)S(1)}, u32[]{:S(2)}, u32[]{:S(2)}) collective-permute-start(bf16[1040,128]{1,0:T(8,128)(2,1)S(1)} %get-tuple-element.26), channel_id=1, source_target_pairs={{384,128},{400,144},{224,96},{240,112},{385,129},{401,145},{225,97... | collective-permute-start | bytes 798728 | tf_op jit(solution)/shard_map/right_step/ppermute | solution.py:156
  22.6 5.3 %collective-permute-start.14 = (bf16[1040,128]{1,0:T(8,128)(2,1)S(1)}, bf16[1040,128]{1,0:T(8,128)(2,1)S(1)}, u32[]{:S(2)}, u32[]{:S(2)}) collective-permute-start(bf16[1040,128]{1,0:T(8,128)(2,1)S(1)} %get-tuple-element.26), channel_id=1, source_target_pairs={{480,288},{496,304},{224,32},{240,48},{384,352},{400,368},{481,289... | collective-permute-start | bytes 798728 | tf_op jit(solution)/shard_map/right_step/ppermute | solution.py:156
  25.2 5.8 %collective-permute-start.4 = (bf16[1040,128]{1,0:T(8,128)(2,1)S(1)}, bf16[1040,128]{1,0:T(8,128)(2,1)S(1)}, u32[]{:S(2)}, u32[]{:S(2)}) collective-permute-start(bf16[1040,128]{1,0:T(8,128)(2,1)S(1)} %add.45), channel_id=1, source_target_pairs={{12,8},{0,4},{268,256},{264,260},{13,9},{1,5},{269,257},{265,261},... | collective-permute-start | bytes 798728 | tf_op jit(solution)/shard_map/left_y/ppermute | solution.py:171
  26.5 2.7 %copy-start.5 = (s32[4,4]{1,0:T(4,128)S(1)}, s32[4,4]{1,0:T(4,128)}, u32[]{:S(2)}) copy-start(s32[4,4]{1,0:T(4,128)} %param.15) | copy-start | bytes 196
  26.6 23.1 %collective-permute-start.12 = (bf16[1040,128]{1,0:T(8,128)(2,1)S(1)}, bf16[1040,128]{1,0:T(8,128)(2,1)S(1)}, u32[]{:S(2)}, u32[]{:S(2)}) collective-permute-start(bf16[1040,128]{1,0:T(8,128)(2,1)S(1)} %add_add_fusion.1), channel_id=1, source_target_pairs={{224,0},{240,16},{480,256},{496,272},{160,192},{176,208},{416,448}... | collective-permute-start | bytes 798728 | tf_op jit(solution)/shard_map/right_step/ppermute | solution.py:156
  27.9 21.8 %collective-permute-start.16 = (bf16[1040,128]{1,0:T(8,128)(2,1)S(1)}, bf16[1040,128]{1,0:T(8,128)(2,1)S(1)}, u32[]{:S(2)}, u32[]{:S(2)}) collective-permute-start(bf16[1040,128]{1,0:T(8,128)(2,1)S(1)} %add_add_fusion), channel_id=1, source_target_pairs={{224,192},{240,208},{480,448},{496,464},{32,0},{48,16},{288,256},{... | collective-permute-start | bytes 798728 | tf_op jit(solution)/shard_map/right_step/ppermute | solution.py:156
  31.0 19.7 %collective-permute-start.7 = (bf16[1040,128]{1,0:T(8,128)(2,1)S(1)}, bf16[1040,128]{1,0:T(8,128)(2,1)S(1)}, u32[]{:S(2)}, u32[]{:S(2)}) collective-permute-start(bf16[1040,128]{1,0:T(8,128)(2,1)S(1)} %add.46.refs_0_), channel_id=1, source_target_pairs={{0,3},{1,0},{2,1},{3,2},{4,7},{5,4},{6,5},{7,6},{8,11},{9,8},{10,9... | collective-permute-start | bytes 798728 | tf_op jit(solution)/shard_map/left_x/ppermute | solution.py:178
  36.9 15.7 %collective-permute-start.6 = (bf16[1040,128]{1,0:T(8,128)(2,1)S(1)}, bf16[1040,128]{1,0:T(8,128)(2,1)S(1)}, u32[]{:S(2)}, u32[]{:S(2)}) collective-permute-start(bf16[1040,128]{1,0:T(8,128)(2,1)S(1)} %add.46.refs_0_), channel_id=1, source_target_pairs={{0,2},{1,3},{2,0},{3,1},{4,6},{5,7},{6,4},{7,5},{8,10},{9,11},{10,... | collective-permute-start | bytes 798728 | tf_op jit(solution)/shard_map/left_x/ppermute | solution.py:178
  40.7 11.9 %collective-permute-start.5 = (bf16[1040,128]{1,0:T(8,128)(2,1)S(1)}, bf16[1040,128]{1,0:T(8,128)(2,1)S(1)}, u32[]{:S(2)}, u32[]{:S(2)}) collective-permute-start(bf16[1040,128]{1,0:T(8,128)(2,1)S(1)} %add.46.refs_0_), channel_id=1, source_target_pairs={{0,1},{1,2},{2,3},{3,0},{4,5},{5,6},{6,7},{7,4},{8,9},{9,10},{10,1... | collective-permute-start | bytes 798728 | tf_op jit(solution)/shard_map/left_x/ppermute | solution.py:178
  50.7 4.0 %collective-permute-start.17 = (bf16[2,1040,128]{2,1,0:T(8,128)(2,1)}, bf16[2,1040,128]{2,1,0:T(8,128)(2,1)S(1)}, u32[]{:S(2)}, u32[]{:S(2)}) collective-permute-start(bf16[2,1040,128]{2,1,0:T(8,128)(2,1)} %pad_maximum_fusion), channel_id=1, source_target_pairs={{0,16},{16,0},{32,48},{48,32},{64,80},{80,64},{96,112},{112,96},{1... | collective-permute-start | bytes 1597448 | tf_op jit(solution)/shard_map/right_core/ppermute | solution.py:180

commit v6 on v5

--- a/solution.py
+++ b/solution.py
@@ -61,6 +61,9 @@
 
 def after(array, *others):
     return lax.optimization_barrier((array, *others))[0]
+
+
+SHIFTS = (0, 1, 3, 2)
 
 
 def fill(tiles_ref, message_refs, slot_of, sems):
@@ -172,7 +175,7 @@
     mine = [right_step(mine[h], right_steps(h)[2]) for h in range(HALVES)]
     mine = [after(half, left) for half in mine]
     lefts = [left]
-    for d in range(1, X):
+    for d in SHIFTS[1:]:
         with jax.named_scope("left_x"):
             pairs = [(col_of(y, x_), col_of(y, (x_ + d) % X)) for y in range(Y_HI) for x_ in range(X)]
             lefts.append(lax.ppermute(left, "col", pairs))
@@ -201,12 +204,12 @@
     rights = [*mine, *(other_ref.at[h] for h in range(HALVES))]
     kept_ref[...] = held_ref[...]
     core, x = lax.axis_index("row") % CORE, lax.axis_index("col") % X
-    for d, left_ref in enumerate(lefts):
+    for i, (d, left_ref) in enumerate(zip(SHIFTS, lefts)):
         section = ((x + X - d) % X) // (X // SECTIONS)
         which = jnp.where(section == core, 0, 1)
 
         def step(t, carry):
-            slot = slot_ref[d * LQ + t]
+            slot = slot_ref[i * LQ + t]
 
             @pl.when(slot >= 0)
             def _():

time: 94.6 us -> 92.4 us (0.977)
  the two profiles are of different devices: /device:TPU:48 before, /device:TPU:16 now
where the time goes in v6:
time: 92.4 us; the launch traced here: 91.9 us
  waiting for transfers between devices  28.3 us (31%)
  starting transfers between devices  27 us (29%)
  blocking collectives  26.1 us (28%)
  Pallas kernels  3.8 us (4%)
  other arithmetic  2.8 us (3%)
  local copies, waits for them, and re-layouts  2.76 us (3%)
  between operations  1.15 us (1%)
    all_to_all x2, blocking collectives, gather(): lax.all_to_all(jnp.broadcast_to(array, (n,) + array.shape), axis, 0, 0, a...  26.1 us
    ppermute x1, waiting for transfers between devices, panels_everywhere(): left = left + lax.ppermute(left, both, second)  24 us
    ppermute x3, starting transfers between devices, panels_everywhere(): lefts.append(lax.ppermute(left, 'col', pairs))  13.6 us
    ppermute x9, starting transfers between devices, right_send(): lax.ppermute(array, 'row', [(row_of(*a, c), row_of(*b, c)) for a, b in pa...  7.48 us
    ppermute x3, waiting for transfers between devices, panels_everywhere(): lefts.append(lax.ppermute(left, 'col', pairs))  4.25 us
    pallas_call x1, Pallas kernels, product(): pl.pallas_call(product_kernel, out_shape=(jax.ShapeDtypeStruct((MB * TILE...  2.47 us
    unnamed x14, local copies, waits for them, and re-layouts  2.36 us
    ppermute x3, starting transfers between devices, panels_everywhere(): lax.ppermute(quarters[q], 'col', [(col_of(Y_HI - 1, X - 1), col_of(Y_HI -...  2.03 us
  transfers between devices with their start and end apart: 18, of which 3 were waited for; matrix products, arithmetic and copies ran while one was open for 2% of the time, Pallas kernels for 1%

profile of v6, /device:TPU:16, one launch (start us, length us, event | category | flops | bytes accessed | tf_op | source)
XLA Modules:
  0.0 91.9 jit_solution(16739809274957868466)
XLA Ops:
  0.8 1.0 %copy-done.2 = bf16[1,1,16,128,128]{4,3,2,1,0:T(8,128)(2,1)S(1)} copy-done((bf16[1,1,16,128,128]{4,3,2,1,0:T(8,128)(2,1)S(1)}, bf16[1,1,16,128,128]{4,3,2,1,0:T(8,128)(2,1)}, u32[]{:S(2)}) %copy-start.2) | copy-done | bytes 524312
  1.8 0.7 copy-done.3
  2.4 0.6 shard_map.83
  3.1 0.7 collective-permute-start.8
  3.9 0.7 copy-done.4
  4.5 0.6 shard_map.82
  5.2 0.7 collective-permute-start
  5.9 0.7 collective-permute-start.1
  6.5 0.7 collective-permute-start.2
  7.3 0.7 collective-permute-start.9
  8.0 0.7 collective-permute-start.13
  8.8 0.7 collective-permute-start.3
  9.5 0.1 add.47
  9.7 0.8 collective-permute-start.11
  10.5 0.7 collective-permute-start.10
  11.3 0.7 collective-permute-start.15
  12.0 0.7 collective-permute-start.14
  12.8 1.3 %collective-permute-start.4 = (bf16[1040,128]{1,0:T(8,128)(2,1)S(1)}, bf16[1040,128]{1,0:T(8,128)(2,1)S(1)}, u32[]{:S(2)}, u32[]{:S(2)}) collective-permute-start(bf16[1040,128]{1,0:T(8,128)(2,1)S(1)} %add.45), channel_id=1, source_target_pairs={{12,8},{0,4},{268,256},{264,260},{13,9},{1,5},{269,257},{265,261},... | collective-permute-start | bytes 798728 | tf_op jit(solution)/shard_map/left_y/ppermute | solution.py:174
  14.2 1.3 %collective-permute-start.12 = (bf16[1040,128]{1,0:T(8,128)(2,1)S(1)}, bf16[1040,128]{1,0:T(8,128)(2,1)S(1)}, u32[]{:S(2)}, u32[]{:S(2)}) collective-permute-start(bf16[1040,128]{1,0:T(8,128)(2,1)S(1)} %add_add_fusion.1), channel_id=1, source_target_pairs={{224,0},{240,16},{480,256},{496,272},{160,192},{176,208},{416,448}... | collective-permute-start | bytes 798728 | tf_op jit(solution)/shard_map/right_step/ppermute | solution.py:159
  15.5 1.3 %collective-permute-start.16 = (bf16[1040,128]{1,0:T(8,128)(2,1)S(1)}, bf16[1040,128]{1,0:T(8,128)(2,1)S(1)}, u32[]{:S(2)}, u32[]{:S(2)}) collective-permute-start(bf16[1040,128]{1,0:T(8,128)(2,1)S(1)} %add_add_fusion), channel_id=1, source_target_pairs={{224,192},{240,208},{480,448},{496,464},{32,0},{48,16},{288,256},{... | collective-permute-start | bytes 798728 | tf_op jit(solution)/shard_map/right_step/ppermute | solution.py:159
  16.9 24.0 %collective-permute-done.4 = bf16[1040,128]{1,0:T(8,128)(2,1)S(1)} collective-permute-done((bf16[1040,128]{1,0:T(8,128)(2,1)S(1)}, bf16[1040,128]{1,0:T(8,128)(2,1)S(1)}, u32[]{:S(2)}, u32[]{:S(2)}) %collective-permute-start.4) | collective-permute-done | bytes 266272 | tf_op jit(solution)/shard_map/left_y/ppermute | solution.py:174
  41.0 7.8 %collective-permute-start.7 = (bf16[1040,128]{1,0:T(8,128)(2,1)S(1)}, bf16[1040,128]{1,0:T(8,128)(2,1)S(1)}, u32[]{:S(2)}, u32[]{:S(2)}) collective-permute-start(bf16[1040,128]{1,0:T(8,128)(2,1)S(1)} %add.46.refs_0_), channel_id=1, source_target_pairs={{0,2},{1,3},{2,0},{3,1},{4,6},{5,7},{6,4},{7,5},{8,10},{9,11},{10,... | collective-permute-start | bytes 798728 | tf_op jit(solution)/shard_map/left_x/ppermute | solution.py:181
  48.8 1.9 %collective-permute-start.6 = (bf16[1040,128]{1,0:T(8,128)(2,1)S(1)}, bf16[1040,128]{1,0:T(8,128)(2,1)S(1)}, u32[]{:S(2)}, u32[]{:S(2)}) collective-permute-start(bf16[1040,128]{1,0:T(8,128)(2,1)S(1)} %add.46.refs_0_), channel_id=1, source_target_pairs={{0,3},{1,0},{2,1},{3,2},{4,7},{5,4},{6,5},{7,6},{8,11},{9,8},{10,9... | collective-permute-start | bytes 798728 | tf_op jit(solution)/shard_map/left_x/ppermute | solution.py:181
  50.7 3.9 %collective-permute-start.5 = (bf16[1040,128]{1,0:T(8,128)(2,1)S(1)}, bf16[1040,128]{1,0:T(8,128)(2,1)S(1)}, u32[]{:S(2)}, u32[]{:S(2)}) collective-permute-start(bf16[1040,128]{1,0:T(8,128)(2,1)S(1)} %add.46.refs_0_), channel_id=1, source_target_pairs={{0,1},{1,2},{2,3},{3,0},{4,5},{5,6},{6,7},{7,4},{8,9},{9,10},{10,1... | collective-permute-start | bytes 798728 | tf_op jit(solution)/shard_map/left_x/ppermute | solution.py:181
  54.9 0.8 pad_maximum_fusion
  55.7 1.9 %collective-permute-start.17 = (bf16[2,1040,128]{2,1,0:T(8,128)(2,1)}, bf16[2,1040,128]{2,1,0:T(8,128)(2,1)S(1)}, u32[]{:S(2)}, u32[]{:S(2)}) collective-permute-start(bf16[2,1040,128]{2,1,0:T(8,128)(2,1)} %pad_maximum_fusion), channel_id=1, source_target_pairs={{0,16},{16,0},{32,48},{48,32},{64,80},{80,64},{96,112},{112,96},{1... | collective-permute-start | bytes 1597448 | tf_op jit(solution)/shard_map/right_core/ppermute | solution.py:183
  57.6 2.1 %collective-permute-done.6.refs_2_ = bf16[1040,128]{1,0:T(8,128)(2,1)S(1)} collective-permute-done((bf16[1040,128]{1,0:T(8,128)(2,1)S(1)}, bf16[1040,128]{1,0:T(8,128)(2,1)S(1)}, u32[]{:S(2)}, u32[]{:S(2)}) %collective-permute-start.6) | collective-permute-done | bytes 266272 | tf_op jit(solution)/shard_map/left_x/ppermute | solution.py:181
  59.7 2.2 %collective-permute-done.5.refs_1_ = bf16[1040,128]{1,0:T(8,128)(2,1)S(1)} collective-permute-done((bf16[1040,128]{1,0:T(8,128)(2,1)S(1)}, bf16[1040,128]{1,0:T(8,128)(2,1)S(1)}, u32[]{:S(2)}, u32[]{:S(2)}) %collective-permute-start.5) | collective-permute-done | bytes 266272 | tf_op jit(solution)/shard_map/left_x/ppermute | solution.py:181
  62.2 2.5 %shard_map.85 = (f32[512,512]{1,0:T(8,128)S(1)}, f32[8,128]{1,0:T(8,128)S(1)}) custom-call(s32[32]{0:T(128)S(1)} %reshape.156.slot_ref, s32[256]{0:T(256)S(1)} %bitcast.53, s32[16]{0:T(128)S(1)} %reshape.154.mask_ref, bf16[1040,128]{1,0:T(8,128)(2,1)S(1)} %add.46.refs_0_, ...), custom_call_target="tpu_custom_call", output_to_operand_aliasing={{0}: (10, {})} | custom-call | tf_op jit(solution)/shard_map/pallas_call | solution.py:253
  64.7 6.3 %all_to_all.10 = f32[4,8,128]{2,1,0:T(8,128)S(1)} all-to-all(f32[4,8,128]{2,1,0:T(8,128)S(1)} %broadcast_in_dim.46), channel_id=1, replica_groups={{0,16,256,272},{32,48,288,304},{64,80,320,336},{96,112,352,368},{128,14..., dimensions={0} | all-to-all | bytes 32768 | tf_op jit(solution)/shard_map/all_to_all | solution.py:47
  71.0 19.8 %all_to_all.11 = f32[8,8,128]{2,1,0:T(8,128)S(1)} all-to-all(f32[8,8,128]{2,1,0:T(8,128)S(1)} %broadcast_in_dim.47), channel_id=1, replica_groups={{0,32,64,96,128,160,192,224},{16,48,80,112,144,176,208,240},{256,288,32..., dimensions={0} | all-to-all | bytes 65536 | tf_op jit(solution)/shard_map/all_to_all | solution.py:47
  90.8 1.1 %broadcast_multiply_fusion = f32[512,512]{1,0:T(8,128)} fusion(f32[512,512]{1,0:T(8,128)S(1)} %get-tuple-element.29, f32[512]{0:T(512)S(1)} %divide_bitcast_fusion), kind=kLoop, calls=%fused_computation.1 | loop fusion | flops 262144 | bytes 2099200 | tf_op jit(solution)/shard_map/mul | solution.py:276
  (54 shorter events, 1.2 us)
Async XLA Ops:
  0.0 3.9 %copy-start = (bf16[1,1,2,16,128,128]{5,4,3,2,1,0:T(8,128)(2,1)S(1)}, bf16[1,1,2,16,128,128]{5,4,3,2,1,0:T(8,128)(2,1)}, u32[]{:S(2)}) copy-start(bf16[1,1,2,16,128,128]{5,4,3,2,1,0:T(8,128)(2,1)} %param.8) | copy-start | bytes 3145732
  0.7 1.0 %copy-start.2 = (bf16[1,1,16,128,128]{4,3,2,1,0:T(8,128)(2,1)S(1)}, bf16[1,1,16,128,128]{4,3,2,1,0:T(8,128)(2,1)}, u32[]{:S(2)}) copy-start(bf16[1,1,16,128,128]{4,3,2,1,0:T(8,128)(2,1)} %param.11) | copy-start | bytes 1572868
  1.8 0.7 copy-start.3
  2.4 1.4 %copy-start.6 = (s32[1,1,2,16]{3,2,1,0:T(2,128)S(1)}, s32[1,1,2,16]{3,2,1,0:T(2,128)}, u32[]{:S(2)}) copy-start(s32[1,1,2,16]{3,2,1,0:T(2,128)} %param.9) | copy-start | bytes 388
  3.1 6.4 %collective-permute-start.8 = (bf16[2,1040,128]{2,1,0:T(8,128)(2,1)S(1)}, bf16[2,1040,128]{2,1,0:T(8,128)(2,1)S(1)}, u32[]{:S(2)}, u32[]{:S(2)}) collective-permute-start(bf16[2,1040,128]{2,1,0:T(8,128)(2,1)S(1)} %shard_map.83), channel_id=1, source_target_pairs={{480,224},{496,240},{481,225},{497,241},{482,226},{498,242},{483,2... | collective-permute-start | bytes 1597448 | tf_op jit(solution)/shard_map/right_step/ppermute | solution.py:159
  3.9 0.7 copy-start.4
  5.2 2.8 %collective-permute-start = (bf16[1040,128]{1,0:T(8,128)(2,1)S(1)}, bf16[1040,128]{1,0:T(8,128)(2,1)S(1)}, u32[]{:S(2)}, u32[]{:S(2)}) collective-permute-start(bf16[1040,128]{1,0:T(8,128)(2,1)S(1)} %get-tuple-element.19), channel_id=1, source_target_pairs={{15,13},{31,29},{47,45},{63,61},{79,77},{95,93},{111,109},{127,125... | collective-permute-start | bytes 798728 | tf_op jit(solution)/shard_map/left_scatter/ppermute | solution.py:155
  5.9 2.8 %collective-permute-start.1 = (bf16[1040,128]{1,0:T(8,128)(2,1)S(1)}, bf16[1040,128]{1,0:T(8,128)(2,1)S(1)}, u32[]{:S(2)}, u32[]{:S(2)}) collective-permute-start(bf16[1040,128]{1,0:T(8,128)(2,1)S(1)} %get-tuple-element.20), channel_id=1, source_target_pairs={{15,12},{31,28},{47,44},{63,60},{79,76},{95,92},{111,108},{127,124... | collective-permute-start | bytes 798728 | tf_op jit(solution)/shard_map/left_scatter/ppermute | solution.py:155
  6.5 2.1 %collective-permute-start.2 = (bf16[1040,128]{1,0:T(8,128)(2,1)S(1)}, bf16[1040,128]{1,0:T(8,128)(2,1)S(1)}, u32[]{:S(2)}, u32[]{:S(2)}) collective-permute-start(bf16[1040,128]{1,0:T(8,128)(2,1)S(1)} %get-tuple-element.21), channel_id=1, source_target_pairs={{15,14},{31,30},{47,46},{63,62},{79,78},{95,94},{111,110},{127,126... | collective-permute-start | bytes 798728 | tf_op jit(solution)/shard_map/left_scatter/ppermute | solution.py:155
  7.3 2.3 %collective-permute-start.9 = (bf16[1040,128]{1,0:T(8,128)(2,1)S(1)}, bf16[1040,128]{1,0:T(8,128)(2,1)S(1)}, u32[]{:S(2)}, u32[]{:S(2)}) collective-permute-start(bf16[1040,128]{1,0:T(8,128)(2,1)S(1)} %get-tuple-element.35), channel_id=1, source_target_pairs={{480,320},{496,336},{481,321},{497,337},{482,322},{498,338},{483,3... | collective-permute-start | bytes 798728 | tf_op jit(solution)/shard_map/right_step/ppermute | solution.py:159
  8.0 1.7 %collective-permute-start.13 = (bf16[1040,128]{1,0:T(8,128)(2,1)S(1)}, bf16[1040,128]{1,0:T(8,128)(2,1)S(1)}, u32[]{:S(2)}, u32[]{:S(2)}) collective-permute-start(bf16[1040,128]{1,0:T(8,128)(2,1)S(1)} %get-tuple-element.36), channel_id=1, source_target_pairs={{480,384},{496,400},{481,385},{497,401},{482,386},{498,402},{483,3... | collective-permute-start | bytes 798728 | tf_op jit(solution)/shard_map/right_step/ppermute | solution.py:159
  8.8 3.9 %collective-permute-start.3 = (bf16[1040,128]{1,0:T(8,128)(2,1)S(1)}, bf16[1040,128]{1,0:T(8,128)(2,1)S(1)}, u32[]{:S(2)}, u32[]{:S(2)}) collective-permute-start(bf16[1040,128]{1,0:T(8,128)(2,1)S(1)} %add_add_fusion.2), channel_id=1, source_target_pairs={{12,0},{268,264},{13,1},{269,265},{14,2},{270,266},{15,3},{271,267... | collective-permute-start | bytes 798728 | tf_op jit(solution)/shard_map/left_y/ppermute | solution.py:169
  9.6 1.6 %copy-start.1 = (f32[512,512]{1,0:T(8,128)S(1)}, f32[512,512]{1,0:T(8,128)}, u32[]{:S(2)}) copy-start(f32[512,512]{1,0:T(8,128)} %c_ref) | copy-start | bytes 3145732
  9.7 4.4 %collective-permute-start.11 = (bf16[1040,128]{1,0:T(8,128)(2,1)S(1)}, bf16[1040,128]{1,0:T(8,128)(2,1)S(1)}, u32[]{:S(2)}, u32[]{:S(2)}) collective-permute-start(bf16[1040,128]{1,0:T(8,128)(2,1)S(1)} %get-tuple-element.22), channel_id=1, source_target_pairs={{320,64},{336,80},{224,96},{240,112},{321,65},{337,81},{225,97},{2... | collective-permute-start | bytes 798728 | tf_op jit(solution)/shard_map/right_step/ppermute | solution.py:159
  10.5 3.5 %collective-permute-start.10 = (bf16[1040,128]{1,0:T(8,128)(2,1)S(1)}, bf16[1040,128]{1,0:T(8,128)(2,1)S(1)}, u32[]{:S(2)}, u32[]{:S(2)}) collective-permute-start(bf16[1040,128]{1,0:T(8,128)(2,1)S(1)} %get-tuple-element.22), channel_id=1, source_target_pairs={{480,416},{496,432},{224,160},{240,176},{320,352},{336,368},{481,4... | collective-permute-start | bytes 798728 | tf_op jit(solution)/shard_map/right_step/ppermute | solution.py:159
  11.3 4.2 %collective-permute-start.15 = (bf16[1040,128]{1,0:T(8,128)(2,1)S(1)}, bf16[1040,128]{1,0:T(8,128)(2,1)S(1)}, u32[]{:S(2)}, u32[]{:S(2)}) collective-permute-start(bf16[1040,128]{1,0:T(8,128)(2,1)S(1)} %get-tuple-element.26), channel_id=1, source_target_pairs={{384,128},{400,144},{224,96},{240,112},{385,129},{401,145},{225,97... | collective-permute-start | bytes 798728 | tf_op jit(solution)/shard_map/right_step/ppermute | solution.py:159
  12.0 3.5 %collective-permute-start.14 = (bf16[1040,128]{1,0:T(8,128)(2,1)S(1)}, bf16[1040,128]{1,0:T(8,128)(2,1)S(1)}, u32[]{:S(2)}, u32[]{:S(2)}) collective-permute-start(bf16[1040,128]{1,0:T(8,128)(2,1)S(1)} %get-tuple-element.26), channel_id=1, source_target_pairs={{480,288},{496,304},{224,32},{240,48},{384,352},{400,368},{481,289... | collective-permute-start | bytes 798728 | tf_op jit(solution)/shard_map/right_step/ppermute | solution.py:159
  12.8 28.2 %collective-permute-start.4 = (bf16[1040,128]{1,0:T(8,128)(2,1)S(1)}, bf16[1040,128]{1,0:T(8,128)(2,1)S(1)}, u32[]{:S(2)}, u32[]{:S(2)}) collective-permute-start(bf16[1040,128]{1,0:T(8,128)(2,1)S(1)} %add.45), channel_id=1, source_target_pairs={{12,8},{0,4},{268,256},{264,260},{13,9},{1,5},{269,257},{265,261},... | collective-permute-start | bytes 798728 | tf_op jit(solution)/shard_map/left_y/ppermute | solution.py:174
  14.2 2.7 %copy-start.5 = (s32[4,4]{1,0:T(4,128)S(1)}, s32[4,4]{1,0:T(4,128)}, u32[]{:S(2)}) copy-start(s32[4,4]{1,0:T(4,128)} %param.15) | copy-start | bytes 196
  14.2 40.5 %collective-permute-start.12 = (bf16[1040,128]{1,0:T(8,128)(2,1)S(1)}, bf16[1040,128]{1,0:T(8,128)(2,1)S(1)}, u32[]{:S(2)}, u32[]{:S(2)}) collective-permute-start(bf16[1040,128]{1,0:T(8,128)(2,1)S(1)} %add_add_fusion.1), channel_id=1, source_target_pairs={{224,0},{240,16},{480,256},{496,272},{160,192},{176,208},{416,448}... | collective-permute-start | bytes 798728 | tf_op jit(solution)/shard_map/right_step/ppermute | solution.py:159
  15.5 39.2 %collective-permute-start.16 = (bf16[1040,128]{1,0:T(8,128)(2,1)S(1)}, bf16[1040,128]{1,0:T(8,128)(2,1)S(1)}, u32[]{:S(2)}, u32[]{:S(2)}) collective-permute-start(bf16[1040,128]{1,0:T(8,128)(2,1)S(1)} %add_add_fusion), channel_id=1, source_target_pairs={{224,192},{240,208},{480,448},{496,464},{32,0},{48,16},{288,256},{... | collective-permute-start | bytes 798728 | tf_op jit(solution)/shard_map/right_step/ppermute | solution.py:159
  41.0 14.7 %collective-permute-start.7 = (bf16[1040,128]{1,0:T(8,128)(2,1)S(1)}, bf16[1040,128]{1,0:T(8,128)(2,1)S(1)}, u32[]{:S(2)}, u32[]{:S(2)}) collective-permute-start(bf16[1040,128]{1,0:T(8,128)(2,1)S(1)} %add.46.refs_0_), channel_id=1, source_target_pairs={{0,2},{1,3},{2,0},{3,1},{4,6},{5,7},{6,4},{7,5},{8,10},{9,11},{10,... | collective-permute-start | bytes 798728 | tf_op jit(solution)/shard_map/left_x/ppermute | solution.py:181
  48.8 10.9 %collective-permute-start.6 = (bf16[1040,128]{1,0:T(8,128)(2,1)S(1)}, bf16[1040,128]{1,0:T(8,128)(2,1)S(1)}, u32[]{:S(2)}, u32[]{:S(2)}) collective-permute-start(bf16[1040,128]{1,0:T(8,128)(2,1)S(1)} %add.46.refs_0_), channel_id=1, source_target_pairs={{0,3},{1,0},{2,1},{3,2},{4,7},{5,4},{6,5},{7,6},{8,11},{9,8},{10,9... | collective-permute-start | bytes 798728 | tf_op jit(solution)/shard_map/left_x/ppermute | solution.py:181
  50.7 11.1 %collective-permute-start.5 = (bf16[1040,128]{1,0:T(8,128)(2,1)S(1)}, bf16[1040,128]{1,0:T(8,128)(2,1)S(1)}, u32[]{:S(2)}, u32[]{:S(2)}) collective-permute-start(bf16[1040,128]{1,0:T(8,128)(2,1)S(1)} %add.46.refs_0_), channel_id=1, source_target_pairs={{0,1},{1,2},{2,3},{3,0},{4,5},{5,6},{6,7},{7,4},{8,9},{9,10},{10,1... | collective-permute-start | bytes 798728 | tf_op jit(solution)/shard_map/left_x/ppermute | solution.py:181
  55.7 6.3 %collective-permute-start.17 = (bf16[2,1040,128]{2,1,0:T(8,128)(2,1)}, bf16[2,1040,128]{2,1,0:T(8,128)(2,1)S(1)}, u32[]{:S(2)}, u32[]{:S(2)}) collective-permute-start(bf16[2,1040,128]{2,1,0:T(8,128)(2,1)} %pad_maximum_fusion), channel_id=1, source_target_pairs={{0,16},{16,0},{32,48},{48,32},{64,80},{80,64},{96,112},{112,96},{1... | collective-permute-start | bytes 1597448 | tf_op jit(solution)/shard_map/right_core/ppermute | solution.py:183

commit v7 on v6

--- a/solution.py
+++ b/solution.py
@@ -148,6 +148,9 @@
     first, second = y_pairs()
     message = (RH * TILE + PAD, TILE)
     a_tiles, b_tiles = a_tiles.reshape(SECTIONS * KA * TILE, TILE), b_tiles.reshape(KB * TILE, TILE)
+    a_index, a_count, b_index, b_count = lax.optimization_barrier(
+        (a_index.reshape(-1), a_count.reshape(-1), b_index.reshape(-1), b_count.reshape(-1))
+    )
     *quarters, left = messages(left_kernel, [message] * X, X, a_index, a_count, a_tiles)
     (right,) = messages(right_kernel, [(HALVES, *message)], HALVES, b_index, b_count, b_tiles)
     for q in (1, 0, 2):

time: 92.4 us -> 92.7 us (level)
    unnamed x14 -> x12, local copies, waits for them, and re-layouts: 2.36 us -> 1.72 us
where the time goes in v7:
time: 92.7 us; the launch traced here: 92.3 us
  waiting for transfers between devices  28.3 us (31%)
  starting transfers between devices  27 us (29%)
  blocking collectives  25.8 us (28%)
  Pallas kernels  4.43 us (5%)
  other arithmetic  2.82 us (3%)
  local copies, waits for them, and re-layouts  2.79 us (3%)
  between operations  1.16 us (1%)
    all_to_all x2, blocking collectives, gather(): lax.all_to_all(jnp.broadcast_to(array, (n,) + array.shape), axis, 0, 0, a...  25.8 us
    ppermute x1, waiting for transfers between devices, panels_everywhere(): left = left + lax.ppermute(left, both, second)  24 us
    ppermute x3, starting transfers between devices, panels_everywhere(): lefts.append(lax.ppermute(left, 'col', pairs))  13.6 us
    ppermute x9, starting transfers between devices, right_send(): lax.ppermute(array, 'row', [(row_of(*a, c), row_of(*b, c)) for a, b in pa...  7.47 us
    ppermute x3, waiting for transfers between devices, panels_everywhere(): lefts.append(lax.ppermute(left, 'col', pairs))  4.25 us
    pallas_call x1, Pallas kernels, product(): pl.pallas_call(product_kernel, out_shape=(jax.ShapeDtypeStruct((MB * TILE...  3.09 us
    ppermute x3, starting transfers between devices, panels_everywhere(): lax.ppermute(quarters[q], 'col', [(col_of(Y_HI - 1, X - 1), col_of(Y_HI -...  2.03 us
    ppermute x1, starting transfers between devices, panels_everywhere(): lax.ppermute(jnp.stack(mine), 'row', [(r, r ^ 1) for r in range(N_ROW)])  1.91 us
  transfers between devices with their start and end apart: 18, of which 3 were waited for; matrix products, arithmetic and copies ran while one was open for 2% of the time, Pallas kernels for 1%

profile of v7, /device:TPU:16, one launch (start us, length us, event | category | flops | bytes accessed | tf_op | source)
XLA Modules:
  0.0 92.3 jit_solution(4641634003137702152)
XLA Ops:
  0.7 0.8 reshape.145.index_ref
  1.5 1.0 %copy-done.2 = bf16[1,1,16,128,128]{4,3,2,1,0:T(8,128)(2,1)S(1)} copy-done((bf16[1,1,16,128,128]{4,3,2,1,0:T(8,128)(2,1)S(1)}, bf16[1,1,16,128,128]{4,3,2,1,0:T(8,128)(2,1)}, u32[]{:S(2)}) %copy-start.2) | copy-done | bytes 524312
  2.5 0.7 copy-done.3
  3.2 0.6 shard_map.83
  3.9 0.7 collective-permute-start.8
  4.6 0.6 shard_map.82
  5.2 0.7 collective-permute-start
  5.9 0.7 collective-permute-start.1
  6.6 0.7 collective-permute-start.2
  7.3 0.7 collective-permute-start.9
  8.0 0.7 collective-permute-start.13
  8.8 0.7 collective-permute-start.3
  9.5 0.1 add.47
  9.8 0.8 collective-permute-start.11
  10.6 0.7 collective-permute-start.10
  11.4 0.7 collective-permute-start.15
  12.1 0.7 collective-permute-start.14
  12.8 1.3 %collective-permute-start.4 = (bf16[1040,128]{1,0:T(8,128)(2,1)S(1)}, bf16[1040,128]{1,0:T(8,128)(2,1)S(1)}, u32[]{:S(2)}, u32[]{:S(2)}) collective-permute-start(bf16[1040,128]{1,0:T(8,128)(2,1)S(1)} %add.45), channel_id=1, source_target_pairs={{12,8},{0,4},{268,256},{264,260},{13,9},{1,5},{269,257},{265,261},... | collective-permute-start | bytes 798728 | tf_op jit(solution)/shard_map/left_y/ppermute | solution.py:177
  14.2 1.3 %collective-permute-start.12 = (bf16[1040,128]{1,0:T(8,128)(2,1)S(1)}, bf16[1040,128]{1,0:T(8,128)(2,1)S(1)}, u32[]{:S(2)}, u32[]{:S(2)}) collective-permute-start(bf16[1040,128]{1,0:T(8,128)(2,1)S(1)} %add_add_fusion.1), channel_id=1, source_target_pairs={{224,0},{240,16},{480,256},{496,272},{160,192},{176,208},{416,448}... | collective-permute-start | bytes 798728 | tf_op jit(solution)/shard_map/right_step/ppermute | solution.py:162
  15.6 1.3 %collective-permute-start.16 = (bf16[1040,128]{1,0:T(8,128)(2,1)S(1)}, bf16[1040,128]{1,0:T(8,128)(2,1)S(1)}, u32[]{:S(2)}, u32[]{:S(2)}) collective-permute-start(bf16[1040,128]{1,0:T(8,128)(2,1)S(1)} %add_add_fusion), channel_id=1, source_target_pairs={{224,192},{240,208},{480,448},{496,464},{32,0},{48,16},{288,256},{... | collective-permute-start | bytes 798728 | tf_op jit(solution)/shard_map/right_step/ppermute | solution.py:162
  17.0 24.0 %collective-permute-done.4 = bf16[1040,128]{1,0:T(8,128)(2,1)S(1)} collective-permute-done((bf16[1040,128]{1,0:T(8,128)(2,1)S(1)}, bf16[1040,128]{1,0:T(8,128)(2,1)S(1)}, u32[]{:S(2)}, u32[]{:S(2)}) %collective-permute-start.4) | collective-permute-done | bytes 266272 | tf_op jit(solution)/shard_map/left_y/ppermute | solution.py:177
  41.1 7.8 %collective-permute-start.7 = (bf16[1040,128]{1,0:T(8,128)(2,1)S(1)}, bf16[1040,128]{1,0:T(8,128)(2,1)S(1)}, u32[]{:S(2)}, u32[]{:S(2)}) collective-permute-start(bf16[1040,128]{1,0:T(8,128)(2,1)S(1)} %add.46.refs_0_), channel_id=1, source_target_pairs={{0,2},{1,3},{2,0},{3,1},{4,6},{5,7},{6,4},{7,5},{8,10},{9,11},{10,... | collective-permute-start | bytes 798728 | tf_op jit(solution)/shard_map/left_x/ppermute | solution.py:184
  48.9 1.9 %collective-permute-start.6 = (bf16[1040,128]{1,0:T(8,128)(2,1)S(1)}, bf16[1040,128]{1,0:T(8,128)(2,1)S(1)}, u32[]{:S(2)}, u32[]{:S(2)}) collective-permute-start(bf16[1040,128]{1,0:T(8,128)(2,1)S(1)} %add.46.refs_0_), channel_id=1, source_target_pairs={{0,3},{1,0},{2,1},{3,2},{4,7},{5,4},{6,5},{7,6},{8,11},{9,8},{10,9... | collective-permute-start | bytes 798728 | tf_op jit(solution)/shard_map/left_x/ppermute | solution.py:184
  50.8 3.9 %collective-permute-start.5 = (bf16[1040,128]{1,0:T(8,128)(2,1)S(1)}, bf16[1040,128]{1,0:T(8,128)(2,1)S(1)}, u32[]{:S(2)}, u32[]{:S(2)}) collective-permute-start(bf16[1040,128]{1,0:T(8,128)(2,1)S(1)} %add.46.refs_0_), channel_id=1, source_target_pairs={{0,1},{1,2},{2,3},{3,0},{4,5},{5,6},{6,7},{7,4},{8,9},{9,10},{10,1... | collective-permute-start | bytes 798728 | tf_op jit(solution)/shard_map/left_x/ppermute | solution.py:184
  54.9 0.8 pad_maximum_fusion
  55.8 1.9 %collective-permute-start.17 = (bf16[2,1040,128]{2,1,0:T(8,128)(2,1)}, bf16[2,1040,128]{2,1,0:T(8,128)(2,1)S(1)}, u32[]{:S(2)}, u32[]{:S(2)}) collective-permute-start(bf16[2,1040,128]{2,1,0:T(8,128)(2,1)} %pad_maximum_fusion), channel_id=1, source_target_pairs={{0,16},{16,0},{32,48},{48,32},{64,80},{80,64},{96,112},{112,96},{1... | collective-permute-start | bytes 1597448 | tf_op jit(solution)/shard_map/right_core/ppermute | solution.py:186
  57.7 2.1 %collective-permute-done.6.refs_2_ = bf16[1040,128]{1,0:T(8,128)(2,1)S(1)} collective-permute-done((bf16[1040,128]{1,0:T(8,128)(2,1)S(1)}, bf16[1040,128]{1,0:T(8,128)(2,1)S(1)}, u32[]{:S(2)}, u32[]{:S(2)}) %collective-permute-start.6) | collective-permute-done | bytes 266272 | tf_op jit(solution)/shard_map/left_x/ppermute | solution.py:184
  59.8 2.2 %collective-permute-done.5.refs_1_ = bf16[1040,128]{1,0:T(8,128)(2,1)S(1)} collective-permute-done((bf16[1040,128]{1,0:T(8,128)(2,1)S(1)}, bf16[1040,128]{1,0:T(8,128)(2,1)S(1)}, u32[]{:S(2)}, u32[]{:S(2)}) %collective-permute-start.5) | collective-permute-done | bytes 266272 | tf_op jit(solution)/shard_map/left_x/ppermute | solution.py:184
  62.2 3.1 %shard_map.85 = (f32[512,512]{1,0:T(8,128)S(1)}, f32[8,128]{1,0:T(8,128)S(1)}) custom-call(s32[32]{0:T(128)S(1)} %reshape.156.slot_ref, s32[256]{0:T(256)S(1)} %bitcast.53, s32[16]{0:T(128)S(1)} %reshape.154.mask_ref, bf16[1040,128]{1,0:T(8,128)(2,1)S(1)} %add.46.refs_0_, ...), custom_call_target="tpu_custom_call", output_to_operand_aliasing={{0}: (10, {})} | custom-call | tf_op jit(solution)/shard_map/pallas_call | solution.py:256
  65.3 6.2 %all_to_all.10 = f32[4,8,128]{2,1,0:T(8,128)S(1)} all-to-all(f32[4,8,128]{2,1,0:T(8,128)S(1)} %broadcast_in_dim.46), channel_id=1, replica_groups={{0,16,256,272},{32,48,288,304},{64,80,320,336},{96,112,352,368},{128,14..., dimensions={0} | all-to-all | bytes 32768 | tf_op jit(solution)/shard_map/all_to_all | solution.py:47
  71.6 19.6 %all_to_all.11 = f32[8,8,128]{2,1,0:T(8,128)S(1)} all-to-all(f32[8,8,128]{2,1,0:T(8,128)S(1)} %broadcast_in_dim.47), channel_id=1, replica_groups={{0,32,64,96,128,160,192,224},{16,48,80,112,144,176,208,240},{256,288,32..., dimensions={0} | all-to-all | bytes 65536 | tf_op jit(solution)/shard_map/all_to_all | solution.py:47
  91.2 1.1 %broadcast_multiply_fusion = f32[512,512]{1,0:T(8,128)} fusion(f32[512,512]{1,0:T(8,128)S(1)} %get-tuple-element.37, f32[512]{0:T(512)S(1)} %divide_bitcast_fusion), kind=kLoop, calls=%fused_computation.1 | loop fusion | flops 262144 | bytes 2099200 | tf_op jit(solution)/shard_map/mul | solution.py:279
  (52 shorter events, 1.2 us)
Async XLA Ops:
  0.0 4.6 %copy-start = (bf16[1,1,2,16,128,128]{5,4,3,2,1,0:T(8,128)(2,1)S(1)}, bf16[1,1,2,16,128,128]{5,4,3,2,1,0:T(8,128)(2,1)}, u32[]{:S(2)}) copy-start(bf16[1,1,2,16,128,128]{5,4,3,2,1,0:T(8,128)(2,1)} %param.8) | copy-start | bytes 3145732
  1.5 1.0 %copy-start.2 = (bf16[1,1,16,128,128]{4,3,2,1,0:T(8,128)(2,1)S(1)}, bf16[1,1,16,128,128]{4,3,2,1,0:T(8,128)(2,1)}, u32[]{:S(2)}) copy-start(bf16[1,1,16,128,128]{4,3,2,1,0:T(8,128)(2,1)} %param.11) | copy-start | bytes 1572868
  2.5 0.7 copy-start.3
  3.9 0.7 copy-start.4
  3.9 5.6 %collective-permute-start.8 = (bf16[2,1040,128]{2,1,0:T(8,128)(2,1)S(1)}, bf16[2,1040,128]{2,1,0:T(8,128)(2,1)S(1)}, u32[]{:S(2)}, u32[]{:S(2)}) collective-permute-start(bf16[2,1040,128]{2,1,0:T(8,128)(2,1)S(1)} %shard_map.83), channel_id=1, source_target_pairs={{480,224},{496,240},{481,225},{497,241},{482,226},{498,242},{483,2... | collective-permute-start | bytes 1597448 | tf_op jit(solution)/shard_map/right_step/ppermute | solution.py:162
  5.2 2.8 %collective-permute-start = (bf16[1040,128]{1,0:T(8,128)(2,1)S(1)}, bf16[1040,128]{1,0:T(8,128)(2,1)S(1)}, u32[]{:S(2)}, u32[]{:S(2)}) collective-permute-start(bf16[1040,128]{1,0:T(8,128)(2,1)S(1)} %get-tuple-element.25), channel_id=1, source_target_pairs={{15,13},{31,29},{47,45},{63,61},{79,77},{95,93},{111,109},{127,125... | collective-permute-start | bytes 798728 | tf_op jit(solution)/shard_map/left_scatter/ppermute | solution.py:158
  5.9 2.8 %collective-permute-start.1 = (bf16[1040,128]{1,0:T(8,128)(2,1)S(1)}, bf16[1040,128]{1,0:T(8,128)(2,1)S(1)}, u32[]{:S(2)}, u32[]{:S(2)}) collective-permute-start(bf16[1040,128]{1,0:T(8,128)(2,1)S(1)} %get-tuple-element.26), channel_id=1, source_target_pairs={{15,12},{31,28},{47,44},{63,60},{79,76},{95,92},{111,108},{127,124... | collective-permute-start | bytes 798728 | tf_op jit(solution)/shard_map/left_scatter/ppermute | solution.py:158
  6.6 2.1 %collective-permute-start.2 = (bf16[1040,128]{1,0:T(8,128)(2,1)S(1)}, bf16[1040,128]{1,0:T(8,128)(2,1)S(1)}, u32[]{:S(2)}, u32[]{:S(2)}) collective-permute-start(bf16[1040,128]{1,0:T(8,128)(2,1)S(1)} %get-tuple-element.27), channel_id=1, source_target_pairs={{15,14},{31,30},{47,46},{63,62},{79,78},{95,94},{111,110},{127,126... | collective-permute-start | bytes 798728 | tf_op jit(solution)/shard_map/left_scatter/ppermute | solution.py:158
  7.3 2.3 %collective-permute-start.9 = (bf16[1040,128]{1,0:T(8,128)(2,1)S(1)}, bf16[1040,128]{1,0:T(8,128)(2,1)S(1)}, u32[]{:S(2)}, u32[]{:S(2)}) collective-permute-start(bf16[1040,128]{1,0:T(8,128)(2,1)S(1)} %get-tuple-element.43), channel_id=1, source_target_pairs={{480,320},{496,336},{481,321},{497,337},{482,322},{498,338},{483,3... | collective-permute-start | bytes 798728 | tf_op jit(solution)/shard_map/right_step/ppermute | solution.py:162
  8.0 1.7 %collective-permute-start.13 = (bf16[1040,128]{1,0:T(8,128)(2,1)S(1)}, bf16[1040,128]{1,0:T(8,128)(2,1)S(1)}, u32[]{:S(2)}, u32[]{:S(2)}) collective-permute-start(bf16[1040,128]{1,0:T(8,128)(2,1)S(1)} %get-tuple-element.44), channel_id=1, source_target_pairs={{480,384},{496,400},{481,385},{497,401},{482,386},{498,402},{483,3... | collective-permute-start | bytes 798728 | tf_op jit(solution)/shard_map/right_step/ppermute | solution.py:162
  8.8 3.9 %collective-permute-start.3 = (bf16[1040,128]{1,0:T(8,128)(2,1)S(1)}, bf16[1040,128]{1,0:T(8,128)(2,1)S(1)}, u32[]{:S(2)}, u32[]{:S(2)}) collective-permute-start(bf16[1040,128]{1,0:T(8,128)(2,1)S(1)} %add_add_fusion.2), channel_id=1, source_target_pairs={{12,0},{268,264},{13,1},{269,265},{14,2},{270,266},{15,3},{271,267... | collective-permute-start | bytes 798728 | tf_op jit(solution)/shard_map/left_y/ppermute | solution.py:172
  9.6 1.6 %copy-start.1 = (f32[512,512]{1,0:T(8,128)S(1)}, f32[512,512]{1,0:T(8,128)}, u32[]{:S(2)}) copy-start(f32[512,512]{1,0:T(8,128)} %c_ref) | copy-start | bytes 3145732
  9.8 4.4 %collective-permute-start.11 = (bf16[1040,128]{1,0:T(8,128)(2,1)S(1)}, bf16[1040,128]{1,0:T(8,128)(2,1)S(1)}, u32[]{:S(2)}, u32[]{:S(2)}) collective-permute-start(bf16[1040,128]{1,0:T(8,128)(2,1)S(1)} %get-tuple-element.30), channel_id=1, source_target_pairs={{320,64},{336,80},{224,96},{240,112},{321,65},{337,81},{225,97},{2... | collective-permute-start | bytes 798728 | tf_op jit(solution)/shard_map/right_step/ppermute | solution.py:162
  10.6 3.5 %collective-permute-start.10 = (bf16[1040,128]{1,0:T(8,128)(2,1)S(1)}, bf16[1040,128]{1,0:T(8,128)(2,1)S(1)}, u32[]{:S(2)}, u32[]{:S(2)}) collective-permute-start(bf16[1040,128]{1,0:T(8,128)(2,1)S(1)} %get-tuple-element.30), channel_id=1, source_target_pairs={{480,416},{496,432},{224,160},{240,176},{320,352},{336,368},{481,4... | collective-permute-start | bytes 798728 | tf_op jit(solution)/shard_map/right_step/ppermute | solution.py:162
  11.4 4.2 %collective-permute-start.15 = (bf16[1040,128]{1,0:T(8,128)(2,1)S(1)}, bf16[1040,128]{1,0:T(8,128)(2,1)S(1)}, u32[]{:S(2)}, u32[]{:S(2)}) collective-permute-start(bf16[1040,128]{1,0:T(8,128)(2,1)S(1)} %get-tuple-element.34), channel_id=1, source_target_pairs={{384,128},{400,144},{224,96},{240,112},{385,129},{401,145},{225,97... | collective-permute-start | bytes 798728 | tf_op jit(solution)/shard_map/right_step/ppermute | solution.py:162
  12.1 3.5 %collective-permute-start.14 = (bf16[1040,128]{1,0:T(8,128)(2,1)S(1)}, bf16[1040,128]{1,0:T(8,128)(2,1)S(1)}, u32[]{:S(2)}, u32[]{:S(2)}) collective-permute-start(bf16[1040,128]{1,0:T(8,128)(2,1)S(1)} %get-tuple-element.34), channel_id=1, source_target_pairs={{480,288},{496,304},{224,32},{240,48},{384,352},{400,368},{481,289... | collective-permute-start | bytes 798728 | tf_op jit(solution)/shard_map/right_step/ppermute | solution.py:162
  12.8 28.2 %collective-permute-start.4 = (bf16[1040,128]{1,0:T(8,128)(2,1)S(1)}, bf16[1040,128]{1,0:T(8,128)(2,1)S(1)}, u32[]{:S(2)}, u32[]{:S(2)}) collective-permute-start(bf16[1040,128]{1,0:T(8,128)(2,1)S(1)} %add.45), channel_id=1, source_target_pairs={{12,8},{0,4},{268,256},{264,260},{13,9},{1,5},{269,257},{265,261},... | collective-permute-start | bytes 798728 | tf_op jit(solution)/shard_map/left_y/ppermute | solution.py:177
  14.2 2.7 %copy-start.5 = (s32[4,4]{1,0:T(4,128)S(1)}, s32[4,4]{1,0:T(4,128)}, u32[]{:S(2)}) copy-start(s32[4,4]{1,0:T(4,128)} %param.15) | copy-start | bytes 196
  14.2 40.5 %collective-permute-start.12 = (bf16[1040,128]{1,0:T(8,128)(2,1)S(1)}, bf16[1040,128]{1,0:T(8,128)(2,1)S(1)}, u32[]{:S(2)}, u32[]{:S(2)}) collective-permute-start(bf16[1040,128]{1,0:T(8,128)(2,1)S(1)} %add_add_fusion.1), channel_id=1, source_target_pairs={{224,0},{240,16},{480,256},{496,272},{160,192},{176,208},{416,448}... | collective-permute-start | bytes 798728 | tf_op jit(solution)/shard_map/right_step/ppermute | solution.py:162
  15.6 39.2 %collective-permute-start.16 = (bf16[1040,128]{1,0:T(8,128)(2,1)S(1)}, bf16[1040,128]{1,0:T(8,128)(2,1)S(1)}, u32[]{:S(2)}, u32[]{:S(2)}) collective-permute-start(bf16[1040,128]{1,0:T(8,128)(2,1)S(1)} %add_add_fusion), channel_id=1, source_target_pairs={{224,192},{240,208},{480,448},{496,464},{32,0},{48,16},{288,256},{... | collective-permute-start | bytes 798728 | tf_op jit(solution)/shard_map/right_step/ppermute | solution.py:162
  41.1 14.7 %collective-permute-start.7 = (bf16[1040,128]{1,0:T(8,128)(2,1)S(1)}, bf16[1040,128]{1,0:T(8,128)(2,1)S(1)}, u32[]{:S(2)}, u32[]{:S(2)}) collective-permute-start(bf16[1040,128]{1,0:T(8,128)(2,1)S(1)} %add.46.refs_0_), channel_id=1, source_target_pairs={{0,2},{1,3},{2,0},{3,1},{4,6},{5,7},{6,4},{7,5},{8,10},{9,11},{10,... | collective-permute-start | bytes 798728 | tf_op jit(solution)/shard_map/left_x/ppermute | solution.py:184
  48.9 10.9 %collective-permute-start.6 = (bf16[1040,128]{1,0:T(8,128)(2,1)S(1)}, bf16[1040,128]{1,0:T(8,128)(2,1)S(1)}, u32[]{:S(2)}, u32[]{:S(2)}) collective-permute-start(bf16[1040,128]{1,0:T(8,128)(2,1)S(1)} %add.46.refs_0_), channel_id=1, source_target_pairs={{0,3},{1,0},{2,1},{3,2},{4,7},{5,4},{6,5},{7,6},{8,11},{9,8},{10,9... | collective-permute-start | bytes 798728 | tf_op jit(solution)/shard_map/left_x/ppermute | solution.py:184
  50.8 11.1 %collective-permute-start.5 = (bf16[1040,128]{1,0:T(8,128)(2,1)S(1)}, bf16[1040,128]{1,0:T(8,128)(2,1)S(1)}, u32[]{:S(2)}, u32[]{:S(2)}) collective-permute-start(bf16[1040,128]{1,0:T(8,128)(2,1)S(1)} %add.46.refs_0_), channel_id=1, source_target_pairs={{0,1},{1,2},{2,3},{3,0},{4,5},{5,6},{6,7},{7,4},{8,9},{9,10},{10,1... | collective-permute-start | bytes 798728 | tf_op jit(solution)/shard_map/left_x/ppermute | solution.py:184
  55.8 6.3 %collective-permute-start.17 = (bf16[2,1040,128]{2,1,0:T(8,128)(2,1)}, bf16[2,1040,128]{2,1,0:T(8,128)(2,1)S(1)}, u32[]{:S(2)}, u32[]{:S(2)}) collective-permute-start(bf16[2,1040,128]{2,1,0:T(8,128)(2,1)} %pad_maximum_fusion), channel_id=1, source_target_pairs={{0,16},{16,0},{32,48},{48,32},{64,80},{80,64},{96,112},{112,96},{1... | collective-permute-start | bytes 1597448 | tf_op jit(solution)/shard_map/right_core/ppermute | solution.py:186
